TPU v7x, 128 devices: a whole 4x4x4 slice. The times are simulated.
128 devices in a mesh: src: 2 (over z_lo), pen: 64 (over y, z_hi, x, core).
Axes of the slice: x: 4, y: 4, z: 4 (z_hi: 2, z_lo: 2; z = z_hi * 2 + z_lo), core: 2. Of those that a mesh axis runs over, the one named last changes fastest.
Arguments:
- permeability: float32 [128, 128, 128], P('pen'), may hold values from -6 to 6
- direction: float32 [128, 128, 128], P('pen'), may hold values from -6 to 6
- injection: float32 [2, 128, 128, 128], P('src', 'pen'), may hold values from -6 to 6
- lift_rock: float32 [32], replicated, may hold values from -6 to 6
- lift_well: float32 [32], replicated, may hold values from -6 to 6
- spectral: float32 [6912, 2, 32, 32], P('pen'), may hold values from -6 to 6
- pointwise: float32 [32, 32], replicated, may hold values from -1 to 1
- offsets: float32 [32], replicated, may hold values from -3 to 3
Outputs:
- gauss_newton: float32 [128, 128, 128], P('pen')
All inputs are finite; a program needn't handle non-finite values.
Results may differ from a plain program's by a relative error of at most 0.0001.
Values sent between devices are 32-bit elements; how exact they have to be, the bound alone decides.
No kernel may reach another device: no remote copies, remote signals or barrier semaphores. Data moves between devices by JAX's collectives and lax.ppermute only.
A program may use at most 128 MiB of HBM per device.

v0:
```python
import math

import jax
import jax.numpy as jnp
from jax import lax
from jax.sharding import PartitionSpec as P

MODES = 12


highest = lax.Precision.HIGHEST


def contract(pattern, lefthand, righthand):
    return jnp.einsum(pattern, lefthand, righthand, precision=highest)


def phase_table(frequencies, length, offset, extent):
    positions = offset + jnp.arange(extent, dtype=jnp.int32)
    windings = jnp.mod(frequencies[:, None] * positions[None, :], length)
    angles = windings.astype(jnp.float32) * (2.0 * math.pi / length)
    return (jnp.cos(angles), jnp.sin(angles))


def make_tables(extent_x, extent_y, extent_z, kept_modes, offset, planes):
    ladder = jnp.arange(kept_modes, dtype=jnp.int32)
    signed = jnp.concatenate([ladder, ladder - 2 * kept_modes])
    cosine_outer, sine_outer = phase_table(signed, extent_x, offset, planes)
    cosine_middle, sine_middle = phase_table(signed, extent_y, 0, extent_y)
    cosine_inner, sine_inner = phase_table(ladder, extent_z, 0, extent_z)
    return (cosine_outer, sine_outer, cosine_middle, sine_middle, cosine_inner, sine_inner)


def depth_weights(kept_modes):
    ladder = jnp.arange(kept_modes, dtype=jnp.int32)
    return jnp.where(ladder == 0, 1.0, 2.0).astype(jnp.float32)


def forward(fields, tables, scaling):
    cosine_outer, sine_outer, cosine_middle, sine_middle, cosine_inner, sine_inner = tables
    members = fields.shape[0]
    inner_real = contract("bxyz,kz->bxyk", fields, cosine_inner)
    inner_imag = -contract("bxyz,kz->bxyk", fields, sine_inner)
    middle_real = contract("bxyk,jy->bxjk", inner_real, cosine_middle) + contract(
        "bxyk,jy->bxjk", inner_imag, sine_middle
    )
    middle_imag = contract("bxyk,jy->bxjk", inner_imag, cosine_middle) - contract(
        "bxyk,jy->bxjk", inner_real, sine_middle
    )
    outer_real = contract("bxjk,ix->ijkb", middle_real, cosine_outer) + contract(
        "bxjk,ix->ijkb", middle_imag, sine_outer
    )
    outer_imag = contract("bxjk,ix->ijkb", middle_imag, cosine_outer) - contract(
        "bxjk,ix->ijkb", middle_real, sine_outer
    )
    stacked = jnp.stack([outer_real, outer_imag], axis=3)
    return stacked.reshape(-1, 2, members) * scaling


def backward(spectra, tables, depth_scale, scaling):
    cosine_outer, sine_outer, cosine_middle, sine_middle, cosine_inner, sine_inner = tables
    members = spectra.shape[2]
    shaped = spectra.reshape(
        cosine_outer.shape[0], cosine_middle.shape[0], cosine_inner.shape[0], 2, members
    )
    shaped = shaped * depth_scale[None, None, :, None, None]
    real_part = shaped[:, :, :, 0]
    imag_part = shaped[:, :, :, 1]
    outer_real = contract("ijkb,ix->bxjk", real_part, cosine_outer) - contract(
        "ijkb,ix->bxjk", imag_part, sine_outer
    )
    outer_imag = contract("ijkb,ix->bxjk", real_part, sine_outer) + contract(
        "ijkb,ix->bxjk", imag_part, cosine_outer
    )
    middle_real = contract("bxjk,jy->bxyk", outer_real, cosine_middle) - contract(
        "bxjk,jy->bxyk", outer_imag, sine_middle
    )
    middle_imag = contract("bxjk,jy->bxyk", outer_real, sine_middle) + contract(
        "bxjk,jy->bxyk", outer_imag, cosine_middle
    )
    field = contract("bxyk,kz->bxyz", middle_real, cosine_inner) - contract(
        "bxyk,kz->bxyz", middle_imag, sine_inner
    )
    return field * scaling


def mix(weights, spectra):
    weight_real = weights[:, 0]
    weight_imag = weights[:, 1]
    spec_real = spectra[:, 0]
    spec_imag = spectra[:, 1]
    out_real = contract("mio,msi->mso", weight_real, spec_real) - contract(
        "mio,msi->mso", weight_imag, spec_imag
    )
    out_imag = contract("mio,msi->mso", weight_real, spec_imag) + contract(
        "mio,msi->mso", weight_imag, spec_real
    )
    return jnp.stack([out_real, out_imag], axis=1)


def mix_adjoint(weights, spectra):
    weight_real = weights[:, 0]
    weight_imag = weights[:, 1]
    spec_real = spectra[:, 0]
    spec_imag = spectra[:, 1]
    in_real = contract("mio,mso->msi", weight_real, spec_real) + contract(
        "mio,mso->msi", weight_imag, spec_imag
    )
    in_imag = contract("mio,mso->msi", weight_real, spec_imag) - contract(
        "mio,mso->msi", weight_imag, spec_real
    )
    return jnp.stack([in_real, in_imag], axis=1)


def slope(values):
    return jax.grad(lambda inputs: jnp.sum(jax.nn.gelu(inputs)))(values)


def shards(permeability, direction, injection, lift_rock, lift_well, spectral, pointwise, offsets):
    planes, height, depth = permeability.shape
    devices = lax.axis_size("pen")
    tables = make_tables(
        planes * devices, height, depth, MODES, lax.axis_index("pen") * planes, planes
    )
    scaling = 1.0 / math.sqrt(planes * devices * height * depth)
    depth_scale = depth_weights(MODES)
    mode_scale = jnp.tile(depth_scale, 4 * MODES * MODES)
    sources_here = injection.shape[0]
    channels = lift_rock.shape[0]
    members = sources_here * channels
    unit_scale = jnp.ones_like(depth_scale)
    lifted = (
        lift_rock[None, :, None, None, None] * permeability[None, None]
        + lift_well[None, :, None, None, None] * injection[:, None]
    )
    fields = jnp.concatenate(
        [lifted.reshape(members, planes, height, depth), direction[None]], axis=0
    )
    spectra = lax.psum_scatter(
        forward(fields, tables, scaling), "pen", scatter_dimension=0, tiled=True
    )
    lifted_spec = spectra[:, :, :members].reshape(-1, 2, sources_here, channels)
    direction_spec = spectra[:, :, members]
    coeffs = mix(spectral, lifted_spec)
    tangent_spec = mix(spectral, direction_spec[:, :, None, None] * lift_rock)[:, :, 0]
    all_coeffs, all_tangent = (
        lax.all_gather(coeffs, "pen", axis=0, tiled=True),
        lax.all_gather(tangent_spec, "pen", axis=0, tiled=True),
    )
    rock_weight = contract("io,i->o", pointwise, lift_rock)
    tangent = (
        backward(all_tangent, tables, depth_scale, scaling)
        + rock_weight[:, None, None, None] * direction[None]
    )
    through = backward(
        all_coeffs.reshape(all_coeffs.shape[0], 2, members), tables, depth_scale, scaling
    )
    through = through.reshape(sources_here, channels, planes, height, depth)
    mixed_field = (
        through
        + contract("io,sixyz->soxyz", pointwise, lifted)
        + offsets[None, :, None, None, None]
    )
    slopes = slope(mixed_field)
    adjoint = slopes * slopes * tangent[None]
    local_term = contract("o,soxyz->xyz", rock_weight, adjoint)
    adjoint_term = (
        forward(adjoint.reshape(members, planes, height, depth), tables, scaling)
        * mode_scale[:, None, None]
    )
    adjoint_spec = lax.psum_scatter(adjoint_term, "pen", scatter_dimension=0, tiled=True).reshape(
        -1, 2, sources_here, channels
    )
    pulled = mix_adjoint(spectral, adjoint_spec)
    gathered = lax.all_gather(pulled, "pen", axis=0, tiled=True)
    pulled_fields = backward(
        gathered.reshape(gathered.shape[0], 2, members), tables, unit_scale, scaling
    )
    pulled_fields = pulled_fields.reshape(sources_here, channels, planes, height, depth)
    through_adjoint = contract("c,scxyz->xyz", lift_rock, pulled_fields)
    return lax.psum(through_adjoint + local_term, "src")


def solution(mesh):
    placed = (
        P("pen", None, None),
        P("pen", None, None),
        P("src", "pen", None, None),
        P(),
        P(),
        P("pen", None, None, None),
        P(),
        P(),
    )
    return jax.shard_map(
        shards, mesh=mesh, in_specs=placed, out_specs=P("pen", None, None), check_vma=False
    )
```

profile of v0, /device:TPU:1, one launch (start us, length us, event | category | flops | bytes accessed | tf_op | source)
XLA Modules:
  0.0 1855.0 jit_solution(10995625835561437970)
XLA Ops:
  27.0 4.9 fusion.109
  41.4 5.3 subtract_bitcast_fusion.1
  49.5 4.7 stack.46
  57.0 26.6 %copy.235 = f32[6912,2,33]{2,1,0:T(2,128)} copy(f32[6912,2,33]{2,0,1:T(8,128)S(1)} %maximum_multiply_fusion) | data formatting | bytes 3649536 | tf_op jit(solution)/shard_map/mul | solution.py:57
  85.4 652.8 %all-reduce.8.cloned.1.call-done = f32[6912,2,33]{2,1,0:T(2,128)} async-done(((f32[6912,2,33]{2,1,0:T(2,128)}), f32[6912,2,33]{2,1,0:T(2,128)}) %all-reduce.8.cloned.1.call-update) | async-done | bytes 1824784
  743.8 10.4 fusion.14
  754.3 68.4 %all-gather.9.cloned.1.call-done = f32[6912,2,1,32]{3,1,2,0:T(2,128)} async-done(((f32[108,2,1,32]{3,1,2,0:T(2,128)}), f32[6912,2,1,32]{3,1,2,0:T(2,128)}) %all-gather.9.cloned.1.call-update) | async-done | bytes 1769488 | tf_op jit(solution)/shard_map/all_gather | solution.py:148
  822.7 80.8 %all-gather.5.cloned.1.call-done = f32[6912,2,1,32]{3,1,2,0:T(2,128)} async-done(((f32[108,2,1,32]{3,1,2,0:T(2,128)}), f32[6912,2,1,32]{3,1,2,0:T(2,128)}) %all-gather.5.cloned.1.call-update) | async-done | bytes 1769488 | tf_op jit(solution)/shard_map/all_gather | solution.py:147
  903.4 18.7 %copy_multiply_fusion.1 = (f32[24,24,12,2,32]{4,0,2,1,3:T(8,128)}, f32[24,24,12,2,32]{4,0,2,1,3:T(8,128)}) fusion(f32[24,24,12,2,32]{4,3,2,1,0:T(2,128)} %bitcast.330, f32[12]{0:T(128)S(1)} %compare_select_fusion.2, f32[24,24,12,2,32]{4,3,2,1,0:T(2,128)} %bitcast.329), kind=kLoop, calls=%fused_computation.2 | loop fusion | flops 884736 | bytes 7077936 | tf_op jit(solution)/shard_map/mul | solution.py:66
  947.2 6.9 fusion.71
  955.0 7.1 fusion.73
  963.8 6.7 fusion.69
  970.6 13.7 fusion.8
  1011.7 4.8 stack.54
  1033.6 6.7 copy.268
  1040.4 648.5 %all-reduce.10.cloned.1.call-done = f32[6912,2,32]{2,1,0:T(2,128)} async-done(((f32[6912,2,32]{2,1,0:T(2,128)}), f32[6912,2,32]{2,1,0:T(2,128)}) %all-reduce.10.cloned.1.call-update) | async-done | bytes 1769488
  1691.2 6.4 fusion.10
  1697.7 75.1 %all-gather.7.cloned.1.call-done = f32[6912,2,1,32]{3,1,2,0:T(2,128)} async-done(((f32[108,2,1,32]{3,1,2,0:T(2,128)}), f32[6912,2,1,32]{3,1,2,0:T(2,128)}) %all-gather.7.cloned.1.call-update) | async-done | bytes 1769488 | tf_op jit(solution)/shard_map/all_gather | solution.py:175
  1772.7 10.9 fusion.365
  1791.5 4.4 fusion.50
  1803.3 6.9 fusion.66
  1810.2 6.7 subtract_multiply_fusion
  1816.9 4.6 fusion.12
  1822.2 24.2 %all-reduce.6.cloned.1.call-done = f32[2,128,128]{2,1,0:T(8,128)} async-done(((f32[2,128,128]{2,1,0:T(8,128)}), f32[2,128,128]{2,1,0:T(8,128)}) %all-reduce.6.cloned.1.call-update) | async-done | bytes 131088 | tf_op jit(solution)/shard_map/psum | solution.py:181
  (147 shorter events, 133.7 us)
Async XLA Ops:
  6.5 737.2 %copy-start = (f32[32,32]{1,0:T(8,128)S(1)}, f32[32,32]{1,0:T(8,128)}, u32[]{:S(2)}) copy-start(f32[32,32]{1,0:T(8,128)} %param.14) | copy-start | bytes 12292
  6.5 731.7 %all-reduce.8.cloned.1.call-start = ((), (), s32[]{:S(2)}) async-start(), calls=%async_computation.4 | async-start | bytes 14155776
  8.2 7.6 copy-start.2
  15.9 16.0 copy-start.10
  21.4 10.5 copy-start.9
  21.4 10.5 copy-start.14
  83.5 655.8 %copy-start.16 = (f32[32]{0:T(128)S(1)}, f32[32]{0:T(128)}, u32[]{:S(2)}) copy-start(f32[32]{0:T(128)} %param.11) | copy-start | bytes 388
  83.5 656.9 %copy-start.6 = (f32[108,2,32,32]{0,3,2,1:T(8,128)S(1)}, f32[108,2,32,32]{0,3,2,1:T(8,128)}, u32[]{:S(2)}) copy-start(f32[108,2,32,32]{0,3,2,1:T(8,128)} %param.13) | copy-start | bytes 2654212
  83.6 739.1 %all-gather.9.cloned.1.call-start = ((), (), s32[]{:S(2)}) async-start(), calls=%async_computation.3 | async-start | bytes 7188480 | tf_op jit(solution)/shard_map/all_gather | solution.py:148
  741.7 161.7 %all-gather.5.cloned.1.call-start = ((), (), s32[]{:S(2)}) async-start(), calls=%async_computation | async-start | bytes 7188480 | tf_op jit(solution)/shard_map/all_gather | solution.py:147
  742.6 946.4 %all-reduce.10.cloned.1.call-start = ((), (), s32[]{:S(2)}) async-start(), calls=%async_computation.5 | async-start | bytes 14155776
  743.8 226.8 %copy-start.18 = (f32[1,32]{1,0:T(1,128)}, f32[1,32]{1,0:T(1,128)S(1)}, u32[]{:S(2)}) copy-start(f32[1,32]{1,0:T(1,128)S(1)} %fusion.219) | copy-start | bytes 388
  903.4 18.8 %copy-start.11 = (s32[24]{0:T(128)S(1)}, s32[24]{0:T(128)}, u32[]{:S(2)}) copy-start(s32[24]{0:T(128)} %copy-done.10) | copy-start | bytes 292
  903.4 18.8 %copy-start.15 = (s32[2]{0:T(128)S(1)}, s32[2]{0:T(128)}, u32[]{:S(2)}) copy-start(s32[2]{0:T(128)} %copy-done.14) | copy-start | bytes 28
  922.2 8.0 copy-start.3
  930.2 8.1 slice-start
  962.1 8.5 copy-start.5
  962.1 8.5 copy-start.13
  962.1 8.5 copy-start.20
  1040.3 649.6 %copy-start.7 = (f32[108,2,32,32]{0,3,2,1:T(8,128)S(1)}, f32[108,2,32,32]{0,3,2,1:T(8,128)}, u32[]{:S(2)}) copy-start(f32[108,2,32,32]{0,3,2,1:T(8,128)} %param.13) | copy-start | bytes 2654212
  1040.3 650.9 %copy-start.19 = (f32[1,32]{1,0:T(1,128)S(1)}, f32[1,32]{1,0:T(1,128)}, u32[]{:S(2)}) copy-start(f32[1,32]{1,0:T(1,128)} %copy-done.18) | copy-start | bytes 388
  1040.3 732.4 %all-gather.7.cloned.1.call-start = ((), (), s32[]{:S(2)}) async-start(), calls=%async_computation.1 | async-start | bytes 7188480 | tf_op jit(solution)/shard_map/all_gather | solution.py:175
  1691.2 155.2 %all-reduce.6.cloned.1.call-start = ((), (), s32[]{:S(2)}) async-start(), calls=%async_computation.2 | async-start | bytes 262144 | tf_op jit(solution)/shard_map/psum | solution.py:181
  1810.2 37.8 %copy-start.1 = (f32[32,32]{1,0:T(8,128)S(1)}, f32[32,32]{1,0:T(8,128)}, u32[]{:S(2)}) copy-start(f32[32,32]{1,0:T(8,128)} %param.14) | copy-start | bytes 12292
  (6 other events, 27.9 us)
Sparse Core Ops, SparseCore 0:
  83.7 654.4 all-reduce.7
  741.8 80.7 all-gather.8
  826.2 77.1 all-gather.4
  1040.5 648.4 all-reduce.9
  1691.9 80.7 all-gather.6
  1822.4 23.9 all-reduce.5
where the time goes:
time: 1860 us
  waiting for transfers between devices  1550 us (83%)
  matrix products  177 us (10%)
  local copies, waits for them, and re-layouts  86.1 us (5%)
  other arithmetic  26.4 us (1%)
    unnamed x8, waiting for transfers between devices  1300 us
    dot_general x54, matrix products, contract(): return jnp.einsum(pattern, lefthand, righthand, precision=highest)  177 us
    all_gather x1, waiting for transfers between devices, shards(): lax.all_gather(coeffs, 'pen', axis=0, tiled=True)  80.8 us
    all_gather x1, waiting for transfers between devices, shards(): gathered = lax.all_gather(pulled, 'pen', axis=0, tiled=True)  75.1 us
    all_gather x1, waiting for transfers between devices, shards(): lax.all_gather(tangent_spec, 'pen', axis=0, tiled=True)  68.4 us
  transfers between devices with their start and end apart: 6, of which 6 were waited for; matrix products, arithmetic and copies ran while one was open for 1% of the time, Pallas kernels for 0%

commit v1 on v0

v1 whole, which is shorter than its diff:
```python
import math

import jax
import jax.numpy as jnp
import ml_dtypes
import numpy as np
from jax import lax
from jax.experimental import pallas as pl
from jax.experimental.pallas import tpu as pltpu
from jax.sharding import PartitionSpec as P

MODES = 12
GRID = 128
LANES = 128
BETAS = 8
KAPPAS = 8
OWNERS = BETAS * KAPPAS
CHANNELS = 32
CH = CHANNELS // KAPPAS
HALF = 24
F32 = jnp.float32
BF16 = jnp.bfloat16


def halves(table):
    top = np.asarray(table, np.float32).astype(ml_dtypes.bfloat16)
    rest = (np.asarray(table, np.float64) - top.astype(np.float64)).astype(np.float32)
    return top, rest.astype(ml_dtypes.bfloat16)


def signed(j):
    return np.where(j < MODES, j, j - 3 * MODES)


def build_tables():
    point = np.arange(GRID)
    angle = 2 * np.pi / GRID
    scale = 1.0 / math.sqrt(GRID**3)
    c = np.arange(MODES)
    weight = np.where(c == 0, 1.0, 2.0)
    cos_z = np.cos(angle * ((c[:, None] * point[None]) % GRID))
    sin_z = np.sin(angle * ((c[:, None] * point[None]) % GRID))
    b = np.arange(2 * MODES)
    turn = (signed(b)[:, None] * point[None]) % GRID
    cos_y, sin_y = np.cos(angle * turn), np.sin(angle * turn)
    re, im = slice(0, MODES), slice(MODES, HALF)

    za = np.zeros((GRID, 2 * LANES))
    za[:, 0:12], za[:, 12:24] = cos_z.T, -sin_z.T
    za[:, 128:140], za[:, 140:152] = -sin_z.T, -cos_z.T
    za *= scale

    order = (3 * np.arange(BETAS)[None, :] + np.arange(3)[:, None]).reshape(-1)
    ya = np.concatenate([cos_y[order], sin_y[order]], axis=1)

    x_of = (2 * np.arange(64)[None, :] + np.arange(2)[:, None]).reshape(-1)
    xb = np.zeros((BETAS, 2 * OWNERS, GRID))
    for beta in range(BETAS):
        for slot in range(64):
            j = (beta - 3 * slot) % 8
            if j < 3:
                a = (3 * slot + j) // 8
                ang = angle * ((signed(np.array(a)) * x_of) % GRID)
                xb[beta, slot], xb[beta, 64 + slot] = np.cos(ang), np.sin(ang)
    xi = xb.transpose(0, 2, 1).copy()

    eb = np.zeros((2 * LANES, 3, 2, LANES))
    for bi in range(3):
        for ch in range(CH):
            for k in range(MODES):
                lr, li = bi * HALF + k, bi * HALF + MODES + k
                hr, hi = ch * HALF + k, ch * HALF + MODES + k
                for lane in (hr, hi):
                    eb[lr, bi, 0, lane] = 1
                    eb[LANES + li, bi, 0, lane] = 1
                sign = {hr: -1, hi: 1}
                for lane in (hr, hi):
                    eb[li, bi, 1, lane] = sign[lane]
                    eb[LANES + lr, bi, 1, lane] = -sign[lane]
    eb = eb.reshape(2 * LANES, 6 * LANES)

    yc = np.zeros((2, 2, 2, GRID, BETAS, 2, 3, 2))
    for beta in range(BETAS):
        for bi in range(3):
            for plane in range(2):
                for field in range(2):
                    yc[plane, field, 0, :, beta, plane, bi, field] = cos_y[3 * beta + bi]
                    yc[plane, field, 1, :, beta, plane, bi, field] = sin_y[3 * beta + bi]
    yc = yc.reshape(8 * GRID, 12 * BETAS)

    zc = np.zeros((2, LANES, CH, GRID))
    zf = np.zeros((CH, GRID, 2, LANES))
    for ch in range(CH):
        at = ch * HALF
        r, i = slice(at, at + MODES), slice(at + MODES, at + HALF)
        zc[0, r, ch], zc[0, i, ch] = weight[:, None] * cos_z, -weight[:, None] * sin_z
        zc[1, r, ch], zc[1, i, ch] = -weight[:, None] * sin_z, -weight[:, None] * cos_z
        wc, ws = (weight[:, None] * cos_z).T, (weight[:, None] * sin_z).T
        zf[ch, :, 0, r], zf[ch, :, 0, i] = wc, -ws
        zf[ch, :, 1, r], zf[ch, :, 1, i] = -ws, -wc
    zc = zc.reshape(2 * LANES, CH * GRID) * scale
    zf = zf.reshape(CH * GRID, 2 * LANES) * scale

    ed = np.zeros((3, 2, LANES, 2, LANES))
    for bi in range(3):
        for ch in range(CH):
            for k in range(MODES):
                lr, li = bi * HALF + k, bi * HALF + MODES + k
                hr, hi = ch * HALF + k, ch * HALF + MODES + k
                ed[bi, 0, hr, 0, lr] = ed[bi, 0, hi, 0, lr] = 1
                ed[bi, 1, hr, 0, li], ed[bi, 1, hi, 0, li] = 1, -1
                ed[bi, 1, hr, 1, lr], ed[bi, 1, hi, 1, lr] = -1, 1
                ed[bi, 0, hr, 1, li] = ed[bi, 0, hi, 1, li] = 1
    ed = ed.reshape(6 * LANES, 2 * LANES)

    ye = np.zeros((3, 2, GRID, 2, BETAS, KAPPAS))
    ze = np.zeros((3, 2, LANES, GRID))
    for bi in range(3):
        for beta in range(BETAS):
            ye[bi, 0, :, :, beta, :] = cos_y[3 * beta + bi][:, None, None]
            ye[bi, 1, :, :, beta, :] = sin_y[3 * beta + bi][:, None, None]
        r, i = slice(bi * HALF, bi * HALF + MODES), slice(bi * HALF + MODES, (bi + 1) * HALF)
        ze[bi, 0, r], ze[bi, 0, i] = cos_z, -sin_z
        ze[bi, 1, r], ze[bi, 1, i] = -sin_z, -cos_z
    ye = ye.reshape(6 * GRID, 2 * OWNERS)
    ze = ze.reshape(6 * LANES, GRID) * scale

    return dict(
        za=halves(za), ya=halves(ya), xb=halves(xb), xi=halves(xi), yc=halves(yc),
        zc=halves(zc), zf=halves(zf), ye=halves(ye), ze=halves(ze),
        eb=eb.astype(ml_dtypes.bfloat16), ed=ed.astype(ml_dtypes.bfloat16),
    )


def split(x):
    top = x.astype(BF16)
    return top, (x - top.astype(F32)).astype(BF16)


def dot(a, b):
    return lax.dot_general(a, b, (((1,), (0,)), ((), ())), preferred_element_type=F32)


def left(table_hi, table_lo, x):
    hi, lo = split(x)
    return dot(table_hi, hi) + dot(table_hi, lo) + dot(table_lo, hi)


def right(x, table_hi, table_lo):
    hi, lo = split(x)
    return dot(hi, table_hi) + dot(lo, table_hi) + dot(hi, table_lo)


def right_exact(x, table):
    hi, lo = split(x)
    return dot(hi, table) + dot(lo, table)


def part_mask(shape):
    lane = lax.broadcasted_iota(jnp.int32, shape, 1)
    return lax.rem(lane, HALF) < MODES


def swap(x, real):
    return jnp.where(real, pltpu.roll(x, LANES - MODES, 1), pltpu.roll(x, MODES, 1))


def planes_kernel(p_ref, d_ref, i_ref, zh, zl, yh, yl, out_ref):
    x = jnp.concatenate([r[k] for r in (p_ref, d_ref, i_ref) for k in range(2)], axis=0)
    z = right(x, zh[...], zl[...])
    cols = [
        jnp.concatenate([z[k * GRID : (k + 1) * GRID, :LANES], z[k * GRID : (k + 1) * GRID, LANES:]], axis=0)
        for k in range(6)
    ]
    v = left(yh[...], yl[...], jnp.concatenate(cols, axis=1))
    for k in range(6):
        block = v[:, k * LANES : (k + 1) * LANES]
        total = block[0:8]
        for bi in (1, 2):
            total = total + pltpu.roll(block[8 * bi : 8 * bi + 8], HALF * bi, 1)
        out_ref[:, k, :] = total


def owners_kernel(beta_ref, r_ref, xbh, xbl, xih, xil, eb, out_ref):
    fields = [
        jnp.concatenate([r_ref[:, 2 * f, :], r_ref[:, 2 * f + 1, :]], axis=0) for f in range(3)
    ]
    g = left(xbh[0], xbl[0], jnp.concatenate(fields, axis=1))
    pre = [
        right_exact(
            jnp.concatenate(
                [g[:64, f * LANES : (f + 1) * LANES], g[64:, f * LANES : (f + 1) * LANES]], axis=1
            ),
            eb[...],
        )
        for f in range(3)
    ]
    real = part_mask((OWNERS, LANES))
    stack = []
    for bi in range(3):
        t, w = r_ref[:, 6 + bi, :], r_ref[:, 9 + bi, :]
        ts, ws = swap(t, real), swap(w, real)
        lo, mid, hi = 2 * bi * LANES, (2 * bi + 1) * LANES, (2 * bi + 2) * LANES
        coeff = (
            t * pre[0][:, lo:mid] + ts * pre[0][:, mid:hi]
            + w * pre[2][:, lo:mid] + ws * pre[2][:, mid:hi]
        )
        tangent = t * pre[1][:, lo:mid] + ts * pre[1][:, mid:hi]
        for q in (coeff, tangent):
            s = swap(q, real)
            stack.append(jnp.concatenate([q, jnp.where(real, -s, s)], axis=0))
    o = left(xih[0], xil[0], jnp.concatenate(stack, axis=1))
    for plane in range(2):
        for k in range(6):
            out_ref[:, plane * 6 + k, :] = o[plane * 64 : plane * 64 + 64, k * LANES : (k + 1) * LANES]


ROOT = math.sqrt(2.0 / math.pi)
CUBIC = 0.044715


def slope(x):
    square = x * x
    t = jnp.tanh(ROOT * x * (1.0 + CUBIC * square))
    return 0.5 * (1.0 + t) + 0.5 * ROOT * x * (1.0 - t * t) * (1.0 + 3.0 * CUBIC * square)


def field_kernel(
    scal, r_ref, p_ref, d_ref, i_ref, ych, ycl, zch, zcl, zfh, zfl, yfh, yfl,
    out_ref, local_ref, y_ref, z_ref,
):
    local_ref[...] = jnp.zeros_like(local_ref)

    def pair(kp, carry):
        rhs = jnp.concatenate(
            [
                jnp.concatenate([r_ref[beta * KAPPAS + 2 * kp + k] for beta in range(BETAS)], axis=0)
                for k in range(2)
            ],
            axis=1,
        )
        y_ref[...] = left(ych[...], ycl[...], rhs)
        for k in range(2):
            lanes = slice(k * LANES, (k + 1) * LANES)
            for plane in range(2):
                got = []
                for field in range(2):
                    base = (plane * 2 + field) * 2 * GRID
                    ab = jnp.concatenate(
                        [y_ref[base : base + GRID, lanes], y_ref[base + GRID : base + 2 * GRID, lanes]],
                        axis=1,
                    )
                    got.append(right(ab, zch[...], zcl[...]))
                perm, direc, inj = p_ref[plane], d_ref[plane], i_ref[plane]
                adj, local = [], local_ref[plane]
                for ch in range(CH):
                    o = (2 * kp + k) * CH + ch
                    rock = scal[0, o]
                    cells = slice(ch * GRID, (ch + 1) * GRID)
                    mixed = got[0][:, cells] + rock * perm + scal[1, o] * inj + scal[2, o]
                    s = slope(mixed)
                    a = s * s * (got[1][:, cells] + rock * direc)
                    local = local + rock * a
                    adj.append(a)
                local_ref[plane] = local
                z = right(jnp.concatenate(adj, axis=1), zfh[...], zfl[...])
                z_ref[2 * (2 * kp + k) + plane, :GRID] = z[:, :LANES]
                z_ref[2 * (2 * kp + k) + plane, GRID:] = z[:, LANES:]
        return carry

    lax.fori_loop(0, KAPPAS // 2, pair, 0)
    v = left(yfh[...], yfl[...], jnp.concatenate([z_ref[k] for k in range(2 * KAPPAS)], axis=1))
    for kappa in range(KAPPAS):
        for plane in range(2):
            at = (2 * kappa + plane) * LANES
            for bi in range(3):
                out_ref[:, kappa, plane * 3 + bi, :] = v[8 * bi : 8 * bi + 8, at : at + LANES]


def pull_kernel(beta_ref, r_ref, t_ref, xbh, xbl, xih, xil, ed, out_ref):
    fields = [
        jnp.concatenate([r_ref[:, bi, :], r_ref[:, 3 + bi, :]], axis=0) for bi in range(3)
    ]
    g = left(xbh[0], xbl[0], jnp.concatenate(fields, axis=1))
    real = part_mask((OWNERS, LANES))
    parts = []
    for bi in range(3):
        t = t_ref[:, 6 + bi, :]
        fr, fi = g[:64, bi * LANES : (bi + 1) * LANES], g[64:, bi * LANES : (bi + 1) * LANES]
        s = swap(fi, real)
        v = fr + jnp.where(real, s, -s)
        parts += [t * v, t * swap(v, real)]
    q = right_exact(jnp.concatenate(parts, axis=1), ed[...])
    h = left(xih[0], xil[0], jnp.concatenate([q[:, :LANES], q[:, LANES:]], axis=0))
    for plane in range(2):
        out_ref[:, plane, :] = h[plane * 64 : plane * 64 + 64]


def final_kernel(r_ref, mine_ref, theirs_ref, yh, yl, zh, zl, out_ref):
    g = left(yh[...], yl[...], jnp.concatenate([r_ref[:, 0, :], r_ref[:, 1, :]], axis=1))
    for plane in range(2):
        rows = jnp.concatenate(
            [g[k * GRID : (k + 1) * GRID, plane * LANES : (plane + 1) * LANES] for k in range(6)], axis=1
        )
        out_ref[plane] = right(rows, zh[...], zl[...]) + (mine_ref[plane] + theirs_ref[plane])


VMEM = pl.BlockSpec(memory_space=pltpu.VMEM)
SMEM = pl.BlockSpec(memory_space=pltpu.SMEM)
PARAMS = dict(compiler_params=pltpu.CompilerParams(vmem_limit_bytes=40 * 1024 * 1024))


def whole(shape):
    return pl.BlockSpec(shape, lambda i, beta: (0,) * len(shape))


def by_beta(shape):
    return pl.BlockSpec((1,) + shape, lambda i, beta: (beta[0], 0, 0))


def shards(permeability, direction, injection, lift_rock, lift_well, spectral, pointwise, offsets):
    tab = {
        k: tuple(jnp.asarray(x) for x in v) if isinstance(v, tuple) else jnp.asarray(v)
        for k, v in TABLES.items()
    }
    pen = lax.axis_index("pen")
    beta = (pen // KAPPAS).astype(jnp.int32).reshape(1)
    inj = injection[0]

    folded = jnp.stack(
        [
            jnp.sum(spectral * lift_rock[None, None, :, None], axis=2),
            jnp.sum(spectral * lift_well[None, None, :, None], axis=2),
        ]
    )
    folded = folded.reshape(2, 3, 3, MODES, 2, KAPPAS, CH).transpose(1, 5, 0, 2, 6, 4, 3)
    folded = folded.reshape(3, KAPPAS, 6, CH * HALF)
    folded = jnp.pad(folded, ((0, 5), (0, 0), (0, 0), (0, LANES - CH * HALF)))
    folded = jnp.roll(folded, lax.rem(3 * pen, BETAS), axis=0)

    spec_planes = pl.pallas_call(
        planes_kernel,
        out_shape=jax.ShapeDtypeStruct((BETAS, 6, LANES), F32),
        in_specs=[VMEM] * 7,
        out_specs=VMEM,
        name="planes",
        **PARAMS,
    )(permeability, direction, inj, *tab["za"], *tab["ya"])
    send = jnp.concatenate(
        [jnp.broadcast_to(spec_planes[:, None], (BETAS, KAPPAS, 6, LANES)), folded], axis=2
    ).reshape(OWNERS, 12, LANES)
    owned = lax.all_to_all(send, "pen", 0, 0, tiled=True)

    square = (2 * OWNERS, GRID)
    send = pl.pallas_call(
        owners_kernel,
        out_shape=jax.ShapeDtypeStruct((OWNERS, 12, LANES), F32),
        grid_spec=pltpu.PrefetchScalarGridSpec(
            num_scalar_prefetch=1,
            grid=(1,),
            in_specs=[whole((OWNERS, 12, LANES))] + [by_beta(square)] * 4 + [whole((2 * LANES, 6 * LANES))],
            out_specs=whole((OWNERS, 12, LANES)),
        ),
        name="owners",
        **PARAMS,
    )(beta, owned, *tab["xb"], *tab["xi"], tab["eb"])
    got = lax.all_to_all(send, "pen", 0, 0, tiled=True)

    rock = jnp.sum(pointwise * lift_rock[:, None], axis=0)
    well = jnp.sum(pointwise * lift_well[:, None], axis=0)
    scal = jnp.stack([rock, well, offsets])
    send, local = pl.pallas_call(
        field_kernel,
        out_shape=[
            jax.ShapeDtypeStruct((BETAS, KAPPAS, 6, LANES), F32),
            jax.ShapeDtypeStruct((2, GRID, GRID), F32),
        ],
        in_specs=[SMEM] + [VMEM] * 12,
        out_specs=[VMEM] * 2,
        scratch_shapes=[
            pltpu.VMEM((8 * GRID, 2 * LANES), F32),
            pltpu.VMEM((2 * KAPPAS, 2 * GRID, LANES), F32),
        ],
        name="field",
        **PARAMS,
    )(scal, got, permeability, direction, inj, *tab["yc"], *tab["zc"], *tab["zf"], *tab["ya"])
    theirs = lax.ppermute(local, "src", [(0, 1), (1, 0)])
    back = lax.all_to_all(send.reshape(OWNERS, 6, LANES), "pen", 0, 0, tiled=True)

    send = pl.pallas_call(
        pull_kernel,
        out_shape=jax.ShapeDtypeStruct((OWNERS, 2, LANES), F32),
        grid_spec=pltpu.PrefetchScalarGridSpec(
            num_scalar_prefetch=1,
            grid=(1,),
            in_specs=[whole((OWNERS, 6, LANES)), whole((OWNERS, 12, LANES))]
            + [by_beta(square)] * 4
            + [whole((6 * LANES, 2 * LANES))],
            out_specs=whole((OWNERS, 2, LANES)),
        ),
        name="pull",
        **PARAMS,
    )(beta, back, owned, *tab["xb"], *tab["xi"], tab["ed"])
    send = jnp.concatenate([send, send], axis=0)
    last = lax.all_to_all(send, ("src", "pen"), 0, 0, tiled=True)

    return pl.pallas_call(
        final_kernel,
        out_shape=jax.ShapeDtypeStruct((2, GRID, GRID), F32),
        in_specs=[VMEM] * 7,
        out_specs=VMEM,
        name="final",
        **PARAMS,
    )(last, local, theirs, *tab["ye"], *tab["ze"])


TABLES = build_tables()


def solution(mesh):
    placed = (
        P("pen", None, None),
        P("pen", None, None),
        P("src", "pen", None, None),
        P(),
        P(),
        P("pen", None, None, None),
        P(),
        P(),
    )
    return jax.shard_map(
        shards, mesh=mesh, in_specs=placed, out_specs=P("pen", None, None), check_vma=False
    )
```

time: 1860 us -> 106 us (0.06)
  waiting for transfers between devices: 1550 us -> 46.9 us
  matrix products: 177 us -> 0 us
  local copies, waits for them, and re-layouts: 86.1 us -> 8.17 us
  starting transfers between devices: 0.42 us -> 26.9 us
  other arithmetic: 26.4 us -> 3.3 us
  Pallas kernels: 0 us -> 19.9 us
    unnamed x8 -> x0, waiting for transfers between devices: 1300 us -> none
    all_gather x3 -> x0, waiting for transfers between devices: 224 us -> none  [the longest x1 80.8 us: shards(): lax.all_gather(coeffs, 'pen', axis=0, tiled=True)]
    dot_general x54 -> x0, matrix products: 177 us -> none  [contract(): return jnp.einsum(pattern, lefthand, righthand, precision=highest)]
    all_to_all x0 -> x4, waiting for transfers between devices: none -> 46.9 us  [the longest x1 14 us: shards(): owned = lax.all_to_all(send, 'pen', 0, 0, tiled=True)]
    mul x3 -> x0, local copies, waits for them, and re-layouts: 34.1 us -> none  [the longest x1 26.6 us: forward(): return stacked.reshape(-1, 2, members) * scaling]
    all_to_all x0 -> x4, starting transfers between devices: none -> 26.1 us  [the longest x1 12.4 us: shards(): owned = lax.all_to_all(send, 'pen', 0, 0, tiled=True)]
    psum x1 -> x0, waiting for transfers between devices: 24.2 us -> none  [shards(): return lax.psum(through_adjoint + local_term, 'src')]
    another operation x13 -> x2, local copies, waits for them, and re-layouts: 23.6 us -> 0.41 us  [shards(): jnp.stack([jnp.sum(spectral * lift_rock[None, None, :, None], axis=2), jn...]
  transfers between devices with their start and end apart: 6 -> 5, of which waited for: 6 -> 4; matrix products, arithmetic and copies ran while one was open for 1% -> 1% of each run, Pallas kernels for 0% -> 1%
where the time goes in v1:
time: 106 us; the launch traced here: 105 us
  waiting for transfers between devices  46.9 us (44%)
  starting transfers between devices  26.9 us (25%)
  Pallas kernels  19.9 us (19%)
  local copies, waits for them, and re-layouts  8.17 us (8%)
  other arithmetic  3.3 us (3%)
    all_to_all x1, waiting for transfers between devices, shards(): owned = lax.all_to_all(send, 'pen', 0, 0, tiled=True)  14 us
    pallas_call x1, Pallas kernels, shards(): pl.pallas_call(field_kernel, out_shape=[jax.ShapeDtypeStruct((BETAS, KAPP...  13.6 us
    all_to_all x1, waiting for transfers between devices, shards(): got = lax.all_to_all(send, 'pen', 0, 0, tiled=True)  12.6 us
    all_to_all x1, starting transfers between devices, shards(): owned = lax.all_to_all(send, 'pen', 0, 0, tiled=True)  12.4 us
    all_to_all x1, waiting for transfers between devices, shards(): lax.all_to_all(send.reshape(OWNERS, 6, LANES), 'pen', 0, 0, tiled=True)  10.5 us
    all_to_all x1, waiting for transfers between devices, shards(): last = lax.all_to_all(send, ('src', 'pen'), 0, 0, tiled=True)  9.78 us
    unnamed x58, local copies, waits for them, and re-layouts  5.65 us
    all_to_all x1, starting transfers between devices, shards(): got = lax.all_to_all(send, 'pen', 0, 0, tiled=True)  4.78 us
  transfers between devices with their start and end apart: 5, of which 4 were waited for; matrix products, arithmetic and copies ran while one was open for 1% of the time, Pallas kernels for 1%

profile of v1, /device:TPU:1, one launch (start us, length us, event | category | flops | bytes accessed | tf_op | source)
XLA Modules:
  0.0 105.4 jit_solution(4585733640330762977)
XLA Ops:
  0.7 1.5 %multiply_reduce_fusion.1 = (f32[108,2,32]{0,2,1:T(8,128)S(1)}, f32[108,2,32]{0,2,1:T(8,128)S(1)}) fusion(f32[108,2,32,32]{0,3,2,1:T(8,128)} %param.33, f32[32]{0:T(128)S(1)} %copy-done.26, f32[32]{0:T(128)S(1)} %copy-done.27), kind=kLoop, calls=%fused_computation.1 | loop fusion | flops 870912 | bytes 940288 | tf_op jit(solution)/shard_map/reduce_sum | solution.py:332
  3.3 0.7 reshape.23
  4.2 0.7 copy-done.21
  5.2 1.0 planes.1
  6.2 0.9 copy.30
  7.1 12.4 %all-to-all-start = ((f32[64,12,128]{2,1,0:T(8,128)}), f32[64,12,128]{2,1,0:T(8,128)S(1)}, u32[]{:S(2)}, u32[]{:S(2)}) async-start(f32[64,12,128]{2,1,0:T(8,128)} %bitcast.6), calls=%async_computation | async-start | bytes 1048576 | tf_op jit(solution)/shard_map/all_to_all | solution.py:352
  19.6 14.0 %all-to-all-done.r_ref.t_ref = f32[64,12,128]{2,1,0:T(8,128)S(1)} async-done(((f32[64,12,128]{2,1,0:T(8,128)}), f32[64,12,128]{2,1,0:T(8,128)S(1)}, u32[]{:S(2)}, u32[]{:S(2)}) %all-to-all-start) | async-done | bytes 393248 | tf_op jit(solution)/shard_map/all_to_all | solution.py:352
  33.6 2.1 %owners.1 = f32[64,12,128]{2,1,0:T(8,128)} custom-call(s32[1]{0:T(128)} %bitcast.beta_ref, f32[64,12,128]{2,1,0:T(8,128)S(1)} %all-to-all-done.r_ref.t_ref, bf16[8,128,128]{2,1,0:T(8,128)(2,1)S(1)} %copy-done, bf16[8,128,128]{2,1,0:T(8,128)(2,1)S(1)} %copy-done.1, bf16[8,128,128]{2,1,0:T(8,128)(2,1)S(1)} %copy-done.2, bf16[8,128,128]{2,1,0:T(8,128)(2,1)S(1)} %copy-done.3, ...), custom_call_target="tpu_custom_call" | custom-call | tf_op jit(solution)/shard_map/owners/pallas_call | solution.py:355
  35.8 4.8 %all-to-all-start.1 = ((f32[64,12,128]{2,1,0:T(8,128)}), f32[64,12,128]{2,1,0:T(8,128)S(1)}, u32[]{:S(2)}, u32[]{:S(2)}) async-start(f32[64,12,128]{2,1,0:T(8,128)} %owners.1), calls=%async_computation.1 | async-start | bytes 1048576 | tf_op jit(solution)/shard_map/all_to_all | solution.py:367
  40.6 0.8 multiply_reduce_fusion.3
  42.1 12.6 %all-to-all-done.1.r_ref = f32[64,12,128]{2,1,0:T(8,128)S(1)} async-done(((f32[64,12,128]{2,1,0:T(8,128)}), f32[64,12,128]{2,1,0:T(8,128)S(1)}, u32[]{:S(2)}, u32[]{:S(2)}) %all-to-all-start.1) | async-done | bytes 393248 | tf_op jit(solution)/shard_map/all_to_all | solution.py:367
  54.7 0.9 copy-done.13
  55.6 0.9 copy-done.14
  56.6 0.7 copy-done.25
  57.3 13.6 %field.1 = (f32[8,8,6,128]{3,2,1,0:T(8,128)}, f32[2,128,128]{2,1,0:T(8,128)S(1)}) custom-call(f32[3,32]{1,0:T(4,128)S(1)} %pad_maximum_fusion.2.scal, f32[64,12,128]{2,1,0:T(8,128)S(1)} %all-to-all-done.1.r_ref, f32[2,128,128]{2,1,0:T(8,128)S(1)} %copy-done.4, f32[2,128,128]{2,1,0:T(8,128)S(1)} %copy-done.5, f32[2,128,128]{2,1,0:T(8,128)S(1)} %bitcast.16, ...), custom_call_target="tpu_custom_call" | custom-call | tf_op jit(solution)/shard_map/field/pallas_call | solution.py:372
  70.9 0.7 copy-done.19
  71.6 4.8 %all-to-all-start.2 = ((f32[64,6,128]{2,1,0:T(8,128)}), f32[64,6,128]{2,1,0:T(8,128)S(1)}, u32[]{:S(2)}, u32[]{:S(2)}) async-start(f32[64,6,128]{2,1,0:T(8,128)} %bitcast.7), calls=%async_computation.2 | async-start | bytes 524288 | tf_op jit(solution)/shard_map/all_to_all | solution.py:388
  76.3 0.8 collective-permute-start
  77.2 10.5 %all-to-all-done.2.r_ref = f32[64,6,128]{2,1,0:T(8,128)S(1)} async-done(((f32[64,6,128]{2,1,0:T(8,128)}), f32[64,6,128]{2,1,0:T(8,128)S(1)}, u32[]{:S(2)}, u32[]{:S(2)}) %all-to-all-start.2) | async-done | bytes 196640 | tf_op jit(solution)/shard_map/all_to_all | solution.py:388
  87.7 1.0 pull.1
  88.7 0.7 pad_maximum_fusion.1
  89.4 4.1 %all-to-all-start.3 = ((f32[128,2,128]{2,1,0:T(2,128)}), f32[128,2,128]{2,1,0:T(2,128)S(1)}, u32[]{:S(2)}, u32[]{:S(2)}) async-start(f32[128,2,128]{2,1,0:T(2,128)} %pad_maximum_fusion.1), calls=%async_computation.3 | async-start | bytes 262144 | tf_op jit(solution)/shard_map/all_to_all | solution.py:405
  93.5 9.8 %all-to-all-done.3.r_ref = f32[128,2,128]{2,1,0:T(2,128)S(1)} async-done(((f32[128,2,128]{2,1,0:T(2,128)}), f32[128,2,128]{2,1,0:T(2,128)S(1)}, u32[]{:S(2)}, u32[]{:S(2)}) %all-to-all-start.3) | async-done | bytes 131104 | tf_op jit(solution)/shard_map/all_to_all | solution.py:405
  103.3 2.1 %final.1 = f32[2,128,128]{2,1,0:T(8,128)} custom-call(f32[128,2,128]{2,1,0:T(2,128)S(1)} %all-to-all-done.3.r_ref, f32[2,128,128]{2,1,0:T(8,128)S(1)} %copy-done.20, f32[2,128,128]{2,1,0:T(8,128)S(1)} %collective-permute-done.theirs_ref, bf16[768,128]{1,0:T(8,128)(2,1)S(1)} %copy-done.15, bf16[768,128]{1,0:T(8,128)(2,1)S(1)} %copy-done.16, ...), custom_call_target="tpu_custom_call" | custom-call | tf_op jit(solution)/shard_map/final/pallas_call | solution.py:407
  (63 shorter events, 2.9 us)
Async XLA Ops:
  4.1 1.0 copy-start.4
  4.1 1.0 copy-start.5
  4.1 1.1 %copy-start.6 = (f32[1,2,128,128]{3,2,1,0:T(8,128)S(1)}, f32[1,2,128,128]{3,2,1,0:T(8,128)}, u32[]{:S(2)}) copy-start(f32[1,2,128,128]{3,2,1,0:T(8,128)} %param.30) | copy-start | bytes 393220
  6.2 27.4 %copy-start.8 = (bf16[256,768]{1,0:T(8,128)(2,1)S(1)}, bf16[256,768]{1,0:T(8,128)(2,1)}, u32[]{:S(2)}) copy-start(bf16[256,768]{1,0:T(8,128)(2,1)} %constant.105.clone.eb) | copy-start | bytes 1179652
  7.1 26.5 %copy-start = (bf16[8,128,128]{2,1,0:T(8,128)(2,1)S(1)}, bf16[8,128,128]{2,1,0:T(8,128)(2,1)}, u32[]{:S(2)}) copy-start(bf16[8,128,128]{2,1,0:T(8,128)(2,1)} %constant.91.clone.xbh) | copy-start | bytes 786436
  7.1 26.5 %copy-start.1 = (bf16[8,128,128]{2,1,0:T(8,128)(2,1)S(1)}, bf16[8,128,128]{2,1,0:T(8,128)(2,1)}, u32[]{:S(2)}) copy-start(bf16[8,128,128]{2,1,0:T(8,128)(2,1)} %constant.92.clone.xbl) | copy-start | bytes 786436
  7.1 26.5 %copy-start.2 = (bf16[8,128,128]{2,1,0:T(8,128)(2,1)S(1)}, bf16[8,128,128]{2,1,0:T(8,128)(2,1)}, u32[]{:S(2)}) copy-start(bf16[8,128,128]{2,1,0:T(8,128)(2,1)} %constant.93.clone.xih) | copy-start | bytes 786436
  7.1 26.5 %copy-start.3 = (bf16[8,128,128]{2,1,0:T(8,128)(2,1)S(1)}, bf16[8,128,128]{2,1,0:T(8,128)(2,1)}, u32[]{:S(2)}) copy-start(bf16[8,128,128]{2,1,0:T(8,128)(2,1)} %constant.94.clone.xil) | copy-start | bytes 786436
  7.1 26.5 %all-to-all-start = ((f32[64,12,128]{2,1,0:T(8,128)}), f32[64,12,128]{2,1,0:T(8,128)S(1)}, u32[]{:S(2)}, u32[]{:S(2)}) async-start(f32[64,12,128]{2,1,0:T(8,128)} %bitcast.6), calls=%async_computation | async-start | bytes 1048576 | tf_op jit(solution)/shard_map/all_to_all | solution.py:352
  35.8 18.8 %copy-start.9 = (bf16[512,256]{1,0:T(8,128)(2,1)S(1)}, bf16[512,256]{1,0:T(8,128)(2,1)}, u32[]{:S(2)}) copy-start(bf16[512,256]{1,0:T(8,128)(2,1)} %constant.100.clone.zfl) | copy-start | bytes 786436
  35.8 18.8 %copy-start.10 = (bf16[1024,96]{1,0:T(8,128)(2,1)S(1)}, bf16[1024,96]{1,0:T(8,128)(2,1)}, u32[]{:S(2)}) copy-start(bf16[1024,96]{1,0:T(8,128)(2,1)} %constant.95.clone.ych) | copy-start | bytes 589828
  35.8 18.8 %copy-start.11 = (bf16[1024,96]{1,0:T(8,128)(2,1)S(1)}, bf16[1024,96]{1,0:T(8,128)(2,1)}, u32[]{:S(2)}) copy-start(bf16[1024,96]{1,0:T(8,128)(2,1)} %constant.96.clone.ycl) | copy-start | bytes 589828
  35.8 18.8 %copy-start.12 = (bf16[256,512]{1,0:T(8,128)(2,1)S(1)}, bf16[256,512]{1,0:T(8,128)(2,1)}, u32[]{:S(2)}) copy-start(bf16[256,512]{1,0:T(8,128)(2,1)} %constant.97.clone.zch) | copy-start | bytes 786436
  35.8 18.8 %all-to-all-start.1 = ((f32[64,12,128]{2,1,0:T(8,128)}), f32[64,12,128]{2,1,0:T(8,128)S(1)}, u32[]{:S(2)}, u32[]{:S(2)}) async-start(f32[64,12,128]{2,1,0:T(8,128)} %owners.1), calls=%async_computation.1 | async-start | bytes 1048576 | tf_op jit(solution)/shard_map/all_to_all | solution.py:367
  54.6 1.0 copy-start.13
  71.6 16.1 %copy-start.7 = (bf16[768,256]{1,0:T(8,128)(2,1)S(1)}, bf16[768,256]{1,0:T(8,128)(2,1)}, u32[]{:S(2)}) copy-start(bf16[768,256]{1,0:T(8,128)(2,1)} %constant.106.clone.ed) | copy-start | bytes 1179652
  71.6 4.8 %copy-start.20 = (f32[2,128,128]{2,1,0:T(8,128)S(1)}, f32[2,128,128]{2,1,0:T(8,128)}, u32[]{:S(2)}) copy-start(f32[2,128,128]{2,1,0:T(8,128)} %copy-done.19) | copy-start | bytes 393220
  71.6 16.1 %all-to-all-start.2 = ((f32[64,6,128]{2,1,0:T(8,128)}), f32[64,6,128]{2,1,0:T(8,128)S(1)}, u32[]{:S(2)}, u32[]{:S(2)}) async-start(f32[64,6,128]{2,1,0:T(8,128)} %bitcast.7), calls=%async_computation.2 | async-start | bytes 524288 | tf_op jit(solution)/shard_map/all_to_all | solution.py:388
  76.3 17.2 %collective-permute-start = (f32[2,128,128]{2,1,0:T(8,128)S(1)}, f32[2,128,128]{2,1,0:T(8,128)S(1)}, u32[]{:S(2)}, u32[]{:S(2)}) collective-permute-start(f32[2,128,128]{2,1,0:T(8,128)S(1)} %copy-done.20), channel_id=1, source_target_pairs={{0,64},{64,0},{1,65},{65,1},{2,66},{66,2},{3,67},{67,3},{4,68},{68... | collective-permute-start | bytes 393224 | tf_op jit(solution)/shard_map/ppermute | solution.py:387
  87.7 15.7 %copy-start.17 = (bf16[768,128]{1,0:T(8,128)(2,1)S(1)}, bf16[768,128]{1,0:T(8,128)(2,1)}, u32[]{:S(2)}) copy-start(bf16[768,128]{1,0:T(8,128)(2,1)} %constant.103.clone.zh) | copy-start | bytes 589828
  87.7 15.7 %copy-start.18 = (bf16[768,128]{1,0:T(8,128)(2,1)S(1)}, bf16[768,128]{1,0:T(8,128)(2,1)}, u32[]{:S(2)}) copy-start(bf16[768,128]{1,0:T(8,128)(2,1)} %constant.104.clone.zl) | copy-start | bytes 589828
  88.7 14.7 %copy-start.15 = (bf16[768,128]{1,0:T(8,128)(2,1)S(1)}, bf16[768,128]{1,0:T(8,128)(2,1)}, u32[]{:S(2)}) copy-start(bf16[768,128]{1,0:T(8,128)(2,1)} %constant.101.clone.yh) | copy-start | bytes 589828
  88.7 14.6 %copy-start.16 = (bf16[768,128]{1,0:T(8,128)(2,1)S(1)}, bf16[768,128]{1,0:T(8,128)(2,1)}, u32[]{:S(2)}) copy-start(bf16[768,128]{1,0:T(8,128)(2,1)} %constant.102.clone.yl) | copy-start | bytes 589828
  89.4 13.9 %all-to-all-start.3 = ((f32[128,2,128]{2,1,0:T(2,128)}), f32[128,2,128]{2,1,0:T(2,128)S(1)}, u32[]{:S(2)}, u32[]{:S(2)}) async-start(f32[128,2,128]{2,1,0:T(2,128)} %pad_maximum_fusion.1), calls=%async_computation.3 | async-start | bytes 262144 | tf_op jit(solution)/shard_map/all_to_all | solution.py:405
  (10 other events, 7.7 us)

commit v2 on v1

v2 whole, which is shorter than its diff:
```python
import math

import jax
import jax.numpy as jnp
import ml_dtypes
import numpy as np
from jax import lax
from jax.experimental import pallas as pl
from jax.experimental.pallas import tpu as pltpu
from jax.sharding import PartitionSpec as P

MODES = 12
GRID = 128
LANES = 128
BETAS = 8
KAPPAS = 8
OWNERS = BETAS * KAPPAS
CHANNELS = 32
CH = CHANNELS // KAPPAS
HALF = 24
PAIR = 48
FIELD_ROWS = 864
F32 = jnp.float32
BF16 = jnp.bfloat16


def halves(table):
    top = np.asarray(table, np.float32).astype(ml_dtypes.bfloat16)
    rest = (np.asarray(table, np.float64) - top.astype(np.float64)).astype(np.float32)
    return top, rest.astype(ml_dtypes.bfloat16)


def signed(j):
    return np.where(j < MODES, j, j - 3 * MODES)


def build_tables():
    point = np.arange(GRID)
    angle = 2 * np.pi / GRID
    scale = 1.0 / math.sqrt(GRID**3)
    c = np.arange(MODES)
    weight = np.where(c == 0, 1.0, 2.0)
    cos_z = np.cos(angle * ((c[:, None] * point[None]) % GRID))
    sin_z = np.sin(angle * ((c[:, None] * point[None]) % GRID))
    b = np.arange(2 * MODES)
    turn = (signed(b)[:, None] * point[None]) % GRID
    cos_y, sin_y = np.cos(angle * turn), np.sin(angle * turn)
    re, im = slice(0, MODES), slice(MODES, HALF)

    za = np.zeros((GRID, 2 * LANES))
    za[:, 0:12], za[:, 12:24] = cos_z.T, -sin_z.T
    za[:, 128:140], za[:, 140:152] = -sin_z.T, -cos_z.T
    za *= scale

    order = (3 * np.arange(BETAS)[None, :] + np.arange(3)[:, None]).reshape(-1)
    ya = np.concatenate([cos_y[order], sin_y[order]], axis=1)

    first = np.zeros((320, 2 * LANES), ml_dtypes.bfloat16)
    first[0:128], first[128:256] = halves(za)
    first[256:280], first[288:312] = halves(ya)

    x_of = (2 * np.arange(64)[None, :] + np.arange(2)[:, None]).reshape(-1)
    xb = np.zeros((BETAS, 2 * OWNERS, GRID))
    for beta in range(BETAS):
        for slot in range(64):
            j = (beta - 3 * slot) % 8
            if j < 3:
                a = (3 * slot + j) // 8
                ang = angle * ((signed(np.array(a)) * x_of) % GRID)
                xb[beta, slot], xb[beta, 64 + slot] = np.cos(ang), np.sin(ang)
    xi = xb.transpose(0, 2, 1).copy()

    eb = np.zeros((2 * LANES, 3, 2, LANES))
    for bi in range(3):
        for ch in range(CH):
            for k in range(MODES):
                lr, li = bi * HALF + k, bi * HALF + MODES + k
                hr, hi = ch * HALF + k, ch * HALF + MODES + k
                for lane in (hr, hi):
                    eb[lr, bi, 0, lane] = 1
                    eb[LANES + li, bi, 0, lane] = 1
                sign = {hr: -1, hi: 1}
                for lane in (hr, hi):
                    eb[li, bi, 1, lane] = sign[lane]
                    eb[LANES + lr, bi, 1, lane] = -sign[lane]
    eb = eb.reshape(2 * LANES, 6 * LANES)

    zc = np.zeros((LANES, 2, GRID))
    for q in range(2):
        r, i = slice(q * HALF, q * HALF + MODES), slice(q * HALF + MODES, (q + 1) * HALF)
        rs, js = slice(PAIR + r.start, PAIR + r.stop), slice(PAIR + i.start, PAIR + i.stop)
        zc[r, q], zc[i, q] = weight[:, None] * cos_z, -weight[:, None] * sin_z
        zc[rs, q], zc[js, q] = -weight[:, None] * sin_z, -weight[:, None] * cos_z
    zh, zl = halves(zc.reshape(LANES, 2 * GRID) * scale)
    yh, yl = halves(np.concatenate([cos_y[order], sin_y[order]], axis=0))
    field = np.zeros((FIELD_ROWS, 2 * GRID), ml_dtypes.bfloat16)
    field[0:128], field[128:256], field[256:384] = zh, zh, zl
    field[384:640, :LANES], field[384:640, LANES:] = zh.T, zl.T
    field[640:688, :GRID], field[640:688, GRID:] = yh, yh
    field[688:736, :GRID] = yl
    field[736:864, 0:48], field[736:864, 48:96], field[736:864, 96:144] = yh.T, yl.T, yh.T

    ed = np.zeros((3, 2, LANES, 2, LANES))
    for bi in range(3):
        for ch in range(CH):
            for k in range(MODES):
                lr, li = bi * HALF + k, bi * HALF + MODES + k
                hr, hi = ch * HALF + k, ch * HALF + MODES + k
                ed[bi, 0, hr, 0, lr] = ed[bi, 0, hi, 0, lr] = 1
                ed[bi, 1, hr, 0, li], ed[bi, 1, hi, 0, li] = 1, -1
                ed[bi, 1, hr, 1, lr], ed[bi, 1, hi, 1, lr] = -1, 1
                ed[bi, 0, hr, 1, li] = ed[bi, 0, hi, 1, li] = 1
    ed = ed.reshape(6 * LANES, 2 * LANES)

    ye = np.zeros((3, 2, GRID, 2, BETAS, KAPPAS))
    ze = np.zeros((3, 2, LANES, GRID))
    for bi in range(3):
        for beta in range(BETAS):
            ye[bi, 0, :, :, beta, :] = cos_y[3 * beta + bi][:, None, None]
            ye[bi, 1, :, :, beta, :] = sin_y[3 * beta + bi][:, None, None]
        r, i = slice(bi * HALF, bi * HALF + MODES), slice(bi * HALF + MODES, (bi + 1) * HALF)
        ze[bi, 0, r], ze[bi, 0, i] = cos_z, -sin_z
        ze[bi, 1, r], ze[bi, 1, i] = -sin_z, -cos_z
    ye = ye.reshape(6 * GRID, 2 * OWNERS)
    ze = ze.reshape(6 * LANES, GRID) * scale

    return dict(
        first=first, xb=halves(xb), xi=halves(xi), field=field, ye=halves(ye), ze=halves(ze),
        eb=eb.astype(ml_dtypes.bfloat16), ed=ed.astype(ml_dtypes.bfloat16),
    )


def split(x):
    top = x.astype(BF16)
    return top, (x - top.astype(F32)).astype(BF16)


def dot(a, b):
    return lax.dot_general(a, b, (((1,), (0,)), ((), ())), preferred_element_type=F32)


def left(table_hi, table_lo, x):
    hi, lo = split(x)
    return dot(table_hi, hi) + dot(table_hi, lo) + dot(table_lo, hi)


def right(x, table_hi, table_lo):
    hi, lo = split(x)
    return dot(hi, table_hi) + dot(lo, table_hi) + dot(hi, table_lo)


def right_exact(x, table):
    hi, lo = split(x)
    return dot(hi, table) + dot(lo, table)


def part_mask(shape):
    lane = lax.broadcasted_iota(jnp.int32, shape, 1)
    return lax.rem(lane, HALF) < MODES


def swap(x, real):
    return jnp.where(real, pltpu.roll(x, LANES - MODES, 1), pltpu.roll(x, MODES, 1))


def first_kernel(
    pen_ref, rock_ref, well_ref, s_hbm, p_hbm, d_hbm, i_hbm, tab_hbm, mix_hbm, off_hbm,
    out_ref, scal_ref, s_ref, p_ref, d_ref, i_ref, tab, mix_ref, off_ref, t_ref, sems,
):
    pairs = (
        (tab_hbm, tab), (p_hbm, p_ref), (d_hbm, d_ref), (i_hbm, i_ref),
        (mix_hbm, mix_ref), (off_hbm, off_ref), (s_hbm, s_ref),
    )
    copies = [pltpu.make_async_copy(src, dst, sems.at[k]) for k, (src, dst) in enumerate(pairs)]
    for copy in copies:
        copy.start()
    out_ref[:, :, 6:, :] = jnp.zeros((BETAS, KAPPAS, 6, LANES), F32)
    for copy in copies[:-1]:
        copy.wait()
    x = jnp.concatenate([r[k] for r in (p_ref, d_ref, i_ref) for k in range(2)], axis=0)
    z = right(x, tab[0:128], tab[128:256])
    cols = [
        jnp.concatenate([z[k * GRID : (k + 1) * GRID, :LANES], z[k * GRID : (k + 1) * GRID, LANES:]], axis=0)
        for k in range(6)
    ]
    v = left(tab[256:280], tab[288:312], jnp.concatenate(cols, axis=1))
    for k in range(6):
        col = v[:, k * LANES : (k + 1) * LANES]
        total = col[0:8]
        for bi in (1, 2):
            total = total + pltpu.roll(col[8 * bi : 8 * bi + 8], HALF * bi, 1)
        for kappa in range(KAPPAS):
            out_ref[:, kappa, k, :] = total

    rock = mix_ref[0:1] * rock_ref[0]
    well = mix_ref[0:1] * well_ref[0]
    for i in range(1, CHANNELS):
        rock = rock + mix_ref[i : i + 1] * rock_ref[i]
        well = well + mix_ref[i : i + 1] * well_ref[i]
    scal_ref[0:1], scal_ref[1:2], scal_ref[2:3] = rock, well, off_ref[...]

    copies[-1].wait()
    for part in range(2):
        rock = s_ref[part, 0] * rock_ref[0]
        well = s_ref[part, 0] * well_ref[0]
        for i in range(1, CHANNELS):
            x = s_ref[part, i]
            rock = rock + x * rock_ref[i]
            well = well + x * well_ref[i]
        t_ref[part, :, : rock.shape[1]] = rock
        t_ref[2 + part, :, : rock.shape[1]] = well
    lane = lax.broadcasted_iota(jnp.int32, (KAPPAS, LANES), 1)
    block = [[jnp.zeros((KAPPAS, LANES), F32) for _ in range(9)] for _ in range(2)]
    for ch in range(CH):
        for part in range(2):
            slot = 2 * ch + part
            inside = (lane >= slot * MODES) & (lane < (slot + 1) * MODES)
            for kind in range(2):
                x = t_ref[2 * kind + part, pl.ds(ch, KAPPAS, stride=CH), :]
                for row in range(9):
                    shift = ((slot - row) * MODES) % LANES
                    moved = pltpu.roll(x, shift, 1) if shift else x
                    block[kind][row] = jnp.where(inside, moved, block[kind][row])
    for j in range(3):
        beta = lax.rem(3 * pen_ref[0] + j, BETAS)
        for kind in range(2):
            for bi in range(3):
                out_ref[beta, :, 6 + 3 * kind + bi, :] = block[kind][3 * j + bi]


def owners_kernel(beta_ref, r_ref, xbh, xbl, xih, xil, eb, out_ref):
    fields = [
        jnp.concatenate([r_ref[:, 2 * f, :], r_ref[:, 2 * f + 1, :]], axis=0) for f in range(3)
    ]
    g = left(xbh[0], xbl[0], jnp.concatenate(fields, axis=1))
    pre = [
        right_exact(
            jnp.concatenate(
                [g[:64, f * LANES : (f + 1) * LANES], g[64:, f * LANES : (f + 1) * LANES]], axis=1
            ),
            eb[...],
        )
        for f in range(3)
    ]
    real = part_mask((OWNERS, LANES))
    stack = []
    for bi in range(3):
        t, w = r_ref[:, 6 + bi, :], r_ref[:, 9 + bi, :]
        ts, ws = swap(t, real), swap(w, real)
        lo, mid, hi = 2 * bi * LANES, (2 * bi + 1) * LANES, (2 * bi + 2) * LANES
        coeff = (
            t * pre[0][:, lo:mid] + ts * pre[0][:, mid:hi]
            + w * pre[2][:, lo:mid] + ws * pre[2][:, mid:hi]
        )
        tangent = t * pre[1][:, lo:mid] + ts * pre[1][:, mid:hi]
        for q in (coeff, 0.25 * tangent):
            s = swap(q, real)
            stack.append(jnp.concatenate([q, jnp.where(real, -s, s)], axis=0))
    o = left(xih[0], xil[0], jnp.concatenate(stack, axis=1))
    for plane in range(2):
        for k in range(6):
            out_ref[:, plane * 6 + k, :] = o[plane * 64 : plane * 64 + 64, k * LANES : (k + 1) * LANES]


ROOT = math.sqrt(2.0 / math.pi)
CUBIC = 0.044715


def twice_slope(x):
    square = x * x
    t = jnp.tanh(x * (ROOT + (ROOT * CUBIC) * square))
    return (1.0 + t) * (1.0 + (x * (ROOT + (3.0 * ROOT * CUBIC) * square)) * (1.0 - t))


def field_kernel(
    scal_hbm, r_ref, tab, p_hbm, d_hbm, i_hbm, out_ref, local_ref, scal, p_ref, d_ref, i_ref, z_ref, w0, w1, t0, t1, u0, u1, sems
):
    copies = [
        pltpu.make_async_copy(src, dst, sems.at[k])
        for k, (src, dst) in enumerate(((scal_hbm, scal), (p_hbm, p_ref), (d_hbm, d_ref), (i_hbm, i_ref)))
    ]
    for copy in copies:
        copy.start()
    w_refs, t_refs, u_refs = (w0, w1), (t0, t1), (u0, u1)
    lane = lax.broadcasted_iota(jnp.int32, (HALF, LANES), 1)
    low, high = lane < PAIR, (lane >= PAIR) & (lane < 2 * PAIR)
    zero = jnp.zeros((HALF, LANES), F32)
    local_ref[...] = jnp.zeros_like(local_ref)
    for copy in copies:
        copy.wait()

    def front(k):
        kappas = [GROUP * k + m for m in range(GROUP)]
        w_ref = w_refs[k % 2]
        rhs = []
        for field in range(2):
            for plane in range(2):
                for kappa in kappas:
                    s = jnp.concatenate(
                        [r_ref[:, kappa, plane * 6 + bi * 2 + field, :] for bi in range(3)], axis=0
                    )
                    right_pair = pltpu.roll(s, PAIR, 1)
                    left_pair = pltpu.roll(s, LANES - PAIR, 1)
                    rhs.append(
                        jnp.concatenate([jnp.where(low, s, zero), jnp.where(high, right_pair, zero)], axis=0)
                    )
                    rhs.append(
                        jnp.concatenate([jnp.where(low, left_pair, zero), jnp.where(high, s, zero)], axis=0)
                    )
        count = len(rhs)
        top, rest = split(jnp.concatenate(rhs, axis=1))
        y = dot(tab[736:864, :144], jnp.concatenate([top, top, rest], axis=0))
        top, rest = split(y)
        both = jnp.concatenate(
            [
                jnp.concatenate([h[:, c * LANES : (c + 1) * LANES] for h in (top, rest)], axis=1)
                for c in range(count)
            ],
            axis=0,
        )
        w_ref[...] = dot(both, tab[0:256]) + dot(both[:, :LANES], tab[256:384])

    def back(k):
        kappas = [GROUP * k + m for m in range(GROUP)]
        w_ref, t_ref, u_ref = w_refs[k % 2], t_refs[k % 2], u_refs[k % 2]
        half = 4 * GROUP * GRID
        at = 0
        for plane in range(2):
            perm, direc, inj = p_ref[plane], d_ref[plane], i_ref[plane]
            local = local_ref[plane]
            for kappa in kappas:
                for pair in range(2):
                    adj = []
                    for q in range(2):
                        o = kappa * CH + 2 * pair + q
                        rock = scal[0, o]
                        cells = slice(q * GRID, (q + 1) * GRID)
                        mixed = w_ref[at : at + GRID, cells] + rock * perm + scal[1, o] * inj + scal[2, o]
                        g = twice_slope(mixed)
                        a = g * g * (w_ref[half + at : half + at + GRID, cells] + (0.25 * rock) * direc)
                        local = local + rock * a
                        adj.append(a)
                    top, rest = split(jnp.concatenate(adj, axis=1))
                    t_ref[at : at + GRID], u_ref[at : at + GRID] = top, rest
                    at += GRID
            local_ref[plane] = local
        both = dot(t_ref[...], tab[384:640])
        z = both[:, :LANES] + both[:, LANES:] + dot(u_ref[...], tab[384:640, :LANES])
        top, rest = split(z)
        at = 0
        for plane in range(2):
            for kappa in kappas:
                for pair in range(2):
                    z_ref[4 * kappa + 2 * plane + pair, :GRID] = top[at : at + GRID]
                    z_ref[4 * kappa + 2 * plane + pair, GRID:] = rest[at : at + GRID]
                    at += GRID

    steps = KAPPAS // GROUP
    front(0)
    for k in range(steps):
        if k + 1 < steps:
            front(k + 1)
        back(k)

    for kappa in range(KAPPAS):
        v = dot(tab[640:736], jnp.concatenate([z_ref[4 * kappa + k] for k in range(4)], axis=1))
        v = v[:48] + v[48:]
        for plane in range(2):
            first, second = (v[:, k * LANES : (k + 1) * LANES] for k in (2 * plane, 2 * plane + 1))
            w = jnp.where(
                low,
                first[:HALF] + pltpu.roll(first[HALF:], LANES - PAIR, 1),
                jnp.where(high, pltpu.roll(second[:HALF], PAIR, 1) + second[HALF:], zero),
            )
            for bi in range(3):
                out_ref[:, kappa, plane * 3 + bi, :] = w[8 * bi : 8 * bi + 8]


GROUP = 1


def pull_kernel(beta_ref, r_ref, t_ref, xbh, xbl, xih, xil, ed, out_ref):
    fields = [
        jnp.concatenate([r_ref[:, bi, :], r_ref[:, 3 + bi, :]], axis=0) for bi in range(3)
    ]
    g = left(xbh[0], xbl[0], jnp.concatenate(fields, axis=1))
    real = part_mask((OWNERS, LANES))
    parts = []
    for bi in range(3):
        t = t_ref[:, 6 + bi, :]
        fr, fi = g[:64, bi * LANES : (bi + 1) * LANES], g[64:, bi * LANES : (bi + 1) * LANES]
        s = swap(fi, real)
        v = fr + jnp.where(real, s, -s)
        parts += [t * v, t * swap(v, real)]
    q = right_exact(jnp.concatenate(parts, axis=1), ed[...])
    h = left(xih[0], xil[0], jnp.concatenate([q[:, :LANES], q[:, LANES:]], axis=0))
    for plane in range(2):
        for source in range(2):
            out_ref[64 * source : 64 * source + 64, plane, :] = h[plane * 64 : plane * 64 + 64]


def final_kernel(
    r_ref, yh, yl, zh, zl, mine_hbm, theirs_hbm, out_ref, mine_ref, theirs_ref, sems
):
    copies = [
        pltpu.make_async_copy(src, dst, sems.at[k])
        for k, (src, dst) in enumerate(((mine_hbm, mine_ref), (theirs_hbm, theirs_ref)))
    ]
    for copy in copies:
        copy.start()
    g = left(yh[...], yl[...], jnp.concatenate([r_ref[:, 0, :], r_ref[:, 1, :]], axis=1))
    for copy in copies:
        copy.wait()
    for plane in range(2):
        rows = jnp.concatenate(
            [g[k * GRID : (k + 1) * GRID, plane * LANES : (plane + 1) * LANES] for k in range(6)], axis=1
        )
        out_ref[plane] = right(rows, zh[...], zl[...]) + (mine_ref[plane] + theirs_ref[plane])


VMEM = pl.BlockSpec(memory_space=pltpu.VMEM)
SMEM = pl.BlockSpec(memory_space=pltpu.SMEM)
HBM = pl.BlockSpec(memory_space=pltpu.HBM)
PARAMS = dict(compiler_params=pltpu.CompilerParams(vmem_limit_bytes=40 * 1024 * 1024))


def whole(shape):
    return pl.BlockSpec(shape, lambda i, beta: (0,) * len(shape))


def by_beta(shape):
    return pl.BlockSpec((1,) + shape, lambda i, beta: (beta[0], 0, 0))


def field_call(*operands):
    return pl.pallas_call(
        field_kernel,
        out_shape=[
            jax.ShapeDtypeStruct((BETAS, KAPPAS, 6, LANES), F32),
            jax.ShapeDtypeStruct((2, GRID, GRID), F32),
        ],
        in_specs=[HBM, VMEM, VMEM, HBM, HBM, HBM],
        out_specs=[VMEM] * 2,
        scratch_shapes=[pltpu.SMEM((3, CHANNELS), F32)]
        + [pltpu.VMEM((2, GRID, GRID), F32)] * 3
        + [
            pltpu.VMEM((4 * KAPPAS, 2 * GRID, LANES), BF16),
            *[pltpu.VMEM((8 * GROUP * GRID, 2 * GRID), F32)] * 2,
            *[pltpu.VMEM((4 * GROUP * GRID, 2 * GRID), BF16)] * 4,
            pltpu.SemaphoreType.DMA((4,)),
        ],
        name="field",
        **PARAMS,
    )(*operands)


def shards(permeability, direction, injection, lift_rock, lift_well, spectral, pointwise, offsets):
    tab = {
        k: tuple(jnp.asarray(x) for x in v) if isinstance(v, tuple) else jnp.asarray(v)
        for k, v in TABLES.items()
    }
    pen = lax.axis_index("pen")
    beta = (pen // KAPPAS).astype(jnp.int32).reshape(1)
    inj = injection[0]

    send, scal = pl.pallas_call(
        first_kernel,
        out_shape=[
            jax.ShapeDtypeStruct((BETAS, KAPPAS, 12, LANES), F32),
            jax.ShapeDtypeStruct((3, CHANNELS), F32),
        ],
        in_specs=[SMEM] * 3 + [HBM] * 7,
        out_specs=[VMEM] * 2,
        scratch_shapes=[
            pltpu.VMEM((2, CHANNELS, CHANNELS, spectral.shape[0]), F32),
            *[pltpu.VMEM((2, GRID, GRID), F32)] * 3,
            pltpu.VMEM((320, 2 * LANES), BF16),
            pltpu.VMEM((CHANNELS, CHANNELS), F32),
            pltpu.VMEM((1, CHANNELS), F32),
            pltpu.VMEM((4, CHANNELS, LANES), F32),
            pltpu.SemaphoreType.DMA((7,)),
        ],
        name="first",
        compiler_params=pltpu.CompilerParams(vmem_limit_bytes=60 * 1024 * 1024),
    )(
        pen.astype(jnp.int32).reshape(1), lift_rock, lift_well, spectral.transpose(1, 2, 3, 0),
        permeability, direction, inj, tab["first"], pointwise, offsets.reshape(1, CHANNELS),
    )
    send = send.reshape(OWNERS, 12, LANES)
    owned = lax.all_to_all(send, "pen", 0, 0, tiled=True)

    square = (2 * OWNERS, GRID)
    send = pl.pallas_call(
        owners_kernel,
        out_shape=jax.ShapeDtypeStruct((OWNERS, 12, LANES), F32),
        grid_spec=pltpu.PrefetchScalarGridSpec(
            num_scalar_prefetch=1,
            grid=(1,),
            in_specs=[whole((OWNERS, 12, LANES))] + [by_beta(square)] * 4 + [whole((2 * LANES, 6 * LANES))],
            out_specs=whole((OWNERS, 12, LANES)),
        ),
        name="owners",
        **PARAMS,
    )(beta, owned, *tab["xb"], *tab["xi"], tab["eb"])
    got = lax.all_to_all(send, "pen", 0, 0, tiled=True)

    send, local = field_call(scal, got.reshape(BETAS, KAPPAS, 12, LANES), tab["field"], permeability, direction, inj)
    theirs = lax.ppermute(local, "src", [(0, 1), (1, 0)])
    back = lax.all_to_all(send.reshape(OWNERS, 6, LANES), "pen", 0, 0, tiled=True)

    send = pl.pallas_call(
        pull_kernel,
        out_shape=jax.ShapeDtypeStruct((2 * OWNERS, 2, LANES), F32),
        grid_spec=pltpu.PrefetchScalarGridSpec(
            num_scalar_prefetch=1,
            grid=(1,),
            in_specs=[whole((OWNERS, 6, LANES)), whole((OWNERS, 12, LANES))]
            + [by_beta(square)] * 4
            + [whole((6 * LANES, 2 * LANES))],
            out_specs=whole((2 * OWNERS, 2, LANES)),
        ),
        name="pull",
        **PARAMS,
    )(beta, back, owned, *tab["xb"], *tab["xi"], tab["ed"])
    last = lax.all_to_all(send, ("src", "pen"), 0, 0, tiled=True)

    return pl.pallas_call(
        final_kernel,
        out_shape=jax.ShapeDtypeStruct((2, GRID, GRID), F32),
        in_specs=[VMEM] * 5 + [HBM] * 2,
        out_specs=VMEM,
        scratch_shapes=[pltpu.VMEM((2, GRID, GRID), F32)] * 2 + [pltpu.SemaphoreType.DMA((2,))],
        name="final",
        **PARAMS,
    )(last, *tab["ye"], *tab["ze"], local, theirs)


TABLES = build_tables()


def solution(mesh):
    placed = (
        P("pen", None, None),
        P("pen", None, None),
        P("src", "pen", None, None),
        P(),
        P(),
        P("pen", None, None, None),
        P(),
        P(),
    )
    return jax.shard_map(
        shards, mesh=mesh, in_specs=placed, out_specs=P("pen", None, None), check_vma=False
    )
```

time: 106 us -> 94.3 us (0.89)
  blocking collectives: 0 us -> 18.6 us
  waiting for transfers between devices: 46.9 us -> 34.1 us
  local copies, waits for them, and re-layouts: 8.17 us -> 0.74 us
  starting transfers between devices: 26.9 us -> 22.4 us
  other arithmetic: 3.3 us -> 0 us
  Pallas kernels: 19.9 us -> 17.7 us
    all_to_all x0 -> x1, blocking collectives: none -> 18.6 us  [shards(): got = lax.all_to_all(send, 'pen', 0, 0, tiled=True)]
    all_to_all x1 -> x0, waiting for transfers between devices: 12.6 us -> none  [shards(): got = lax.all_to_all(send, 'pen', 0, 0, tiled=True)]
    unnamed x58 -> x30, local copies, waits for them, and re-layouts: 5.65 us -> 0.74 us
    all_to_all x1 -> x0, starting transfers between devices: 4.78 us -> none  [shards(): got = lax.all_to_all(send, 'pen', 0, 0, tiled=True)]
    reduce_sum x2 -> x0, other arithmetic: 2.31 us -> none  [the longest x1 1.5 us: shards(): jnp.sum(spectral * lift_rock[None, None, :, None], axis=2)]
    pallas_call x3, Pallas kernels: 15.6 us -> 13.8 us  [the longest x1 7.91 us: field_call(): pl.pallas_call(field_kernel, out_shape=[jax.ShapeDtypeStruct((BETAS, KAPP...]
  transfers between devices with their start and end apart: 5 -> 4, of which waited for: 4 -> 3; matrix products, arithmetic and copies ran while one was open for 1% -> 0% of each run, Pallas kernels for 1% -> 2%
where the time goes in v2:
time: 94.3 us; the launch traced here: 93.9 us
  waiting for transfers between devices  34.1 us (36%)
  starting transfers between devices  22.4 us (24%)
  blocking collectives  18.6 us (20%)
  Pallas kernels  17.7 us (19%)
    all_to_all x1, blocking collectives, shards(): got = lax.all_to_all(send, 'pen', 0, 0, tiled=True)  18.6 us
    all_to_all x1, waiting for transfers between devices, shards(): owned = lax.all_to_all(send, 'pen', 0, 0, tiled=True)  14 us
    all_to_all x1, starting transfers between devices, shards(): owned = lax.all_to_all(send, 'pen', 0, 0, tiled=True)  12.4 us
    all_to_all x1, waiting for transfers between devices, shards(): lax.all_to_all(send.reshape(OWNERS, 6, LANES), 'pen', 0, 0, tiled=True)  10.3 us
    all_to_all x1, waiting for transfers between devices, shards(): last = lax.all_to_all(send, ('src', 'pen'), 0, 0, tiled=True)  9.78 us
    pallas_call x1, Pallas kernels, field_call(): pl.pallas_call(field_kernel, out_shape=[jax.ShapeDtypeStruct((BETAS, KAPP...  7.91 us
    all_to_all x1, starting transfers between devices, shards(): lax.all_to_all(send.reshape(OWNERS, 6, LANES), 'pen', 0, 0, tiled=True)  4.78 us
    pallas_call x1, Pallas kernels, shards(): pl.pallas_call(first_kernel, out_shape=[jax.ShapeDtypeStruct((BETAS, KAPP...  4.2 us
  transfers between devices with their start and end apart: 4, of which 3 were waited for; matrix products, arithmetic and copies ran while one was open for 0% of the time, Pallas kernels for 2%

profile of v2, /device:TPU:1, one launch (start us, length us, event | category | flops | bytes accessed | tf_op | source)
XLA Modules:
  0.0 93.9 jit_solution(15271284042641152097)
XLA Ops:
  0.0 4.2 %first.1 = (f32[8,8,12,128]{3,2,1,0:T(8,128)}, f32[3,32]{1,0:T(4,128)}) custom-call(s32[1]{0:T(128)} %bitcast.1.pen_ref, f32[32]{0:T(128)} %rock_ref.1, f32[32]{0:T(128)} %well_ref.1, f32[2,32,32,108]{3,2,1,0:T(8,128)} %bitcast.11, f32[2,128,128]{2,1,0:T(8,128)} %p_hbm.3, f32[2,128,128]{2,1,0:T(8,128)} %d_hbm.3, f32[2,128,128]{2,1,0:T(8,128)} %bitcast.9, ...), custom_call_target="tpu_custom_call" | custom-call | tf_op jit(solution)/shard_map/first/pallas_call | solution.py:466
  4.2 0.0 copy-start
  4.2 0.0 copy-start.1
  4.2 0.0 copy-start.2
  4.2 0.0 copy-start.3
  4.3 12.4 %all-to-all-start = ((f32[64,12,128]{2,1,0:T(8,128)}), f32[64,12,128]{2,1,0:T(8,128)S(1)}, u32[]{:S(2)}, u32[]{:S(2)}) async-start(f32[64,12,128]{2,1,0:T(8,128)} %bitcast.12), calls=%async_computation | async-start | bytes 1048576 | tf_op jit(solution)/shard_map/all_to_all | solution.py:490
  16.7 14.0 %all-to-all-done.r_ref.t_ref = f32[64,12,128]{2,1,0:T(8,128)S(1)} async-done(((f32[64,12,128]{2,1,0:T(8,128)}), f32[64,12,128]{2,1,0:T(8,128)S(1)}, u32[]{:S(2)}, u32[]{:S(2)}) %all-to-all-start) | async-done | bytes 393248 | tf_op jit(solution)/shard_map/all_to_all | solution.py:490
  30.8 1.3 %owners.1 = f32[64,12,128]{2,1,0:T(8,128)S(1)} custom-call(s32[1]{0:T(128)} %bitcast.beta_ref, f32[64,12,128]{2,1,0:T(8,128)S(1)} %all-to-all-done.r_ref.t_ref, bf16[8,128,128]{2,1,0:T(8,128)(2,1)S(1)} %copy-done.3, bf16[8,128,128]{2,1,0:T(8,128)(2,1)S(1)} %copy-done.2, bf16[8,128,128]{2,1,0:T(8,128)(2,1)S(1)} %copy-done.1, ...), custom_call_target="tpu_custom_call" | custom-call | tf_op jit(solution)/shard_map/owners/pallas_call | solution.py:493
  32.1 0.0 copy-start.4
  32.1 0.0 copy-start.5
  32.1 0.0 copy-start.6
  32.2 0.0 copy-start.7
  32.2 18.6 %all_to_all.20 = f32[64,12,128]{2,1,0:T(8,128)S(1)} all-to-all(f32[64,12,128]{2,1,0:T(8,128)S(1)} %owners.1), channel_id=1, replica_groups=mesh['src'=2,'pen'=64] {'pen'}, dimensions={0} | all-to-all | bytes 786432 | tf_op jit(solution)/shard_map/all_to_all | solution.py:505
  50.8 0.7 copy-done.14
  51.5 7.9 %field.1 = (f32[8,8,6,128]{3,2,1,0:T(8,128)}, f32[2,128,128]{2,1,0:T(8,128)S(1)}) custom-call(f32[3,32]{1,0:T(4,128)S(1)} %copy-done.14, f32[8,8,12,128]{3,2,1,0:T(8,128)S(1)} %bitcast.8, bf16[864,256]{1,0:T(8,128)(2,1)S(1)} %copy-done.7, f32[2,128,128]{2,1,0:T(8,128)S(1)} %copy-done.4, f32[2,128,128]{2,1,0:T(8,128)S(1)} %copy-done.5, ...), custom_call_target="tpu_custom_call" | custom-call | tf_op jit(solution)/shard_map/field/pallas_call | solution.py:436
  59.4 0.0 copy-start.8
  59.4 4.8 %all-to-all-start.2 = ((f32[64,6,128]{2,1,0:T(8,128)}), f32[64,6,128]{2,1,0:T(8,128)S(1)}, u32[]{:S(2)}, u32[]{:S(2)}) async-start(f32[64,6,128]{2,1,0:T(8,128)} %bitcast.7), calls=%async_computation.2 | async-start | bytes 524288 | tf_op jit(solution)/shard_map/all_to_all | solution.py:509
  64.2 1.0 %collective-permute-start = (f32[2,128,128]{2,1,0:T(8,128)S(1)}, f32[2,128,128]{2,1,0:T(8,128)S(1)}, u32[]{:S(2)}, u32[]{:S(2)}) collective-permute-start(f32[2,128,128]{2,1,0:T(8,128)S(1)} %get-tuple-element.12.mine_hbm), channel_id=1, source_target_pairs={{0,64},{64,0},{1,65},{65,1},{2,66},{66,2},{3,67},{67,3},{4,68},{68... | collective-permute-start | bytes 393224 | tf_op jit(solution)/shard_map/ppermute | solution.py:508
  65.2 10.3 %all-to-all-done.2.r_ref = f32[64,6,128]{2,1,0:T(8,128)S(1)} async-done(((f32[64,6,128]{2,1,0:T(8,128)}), f32[64,6,128]{2,1,0:T(8,128)S(1)}, u32[]{:S(2)}, u32[]{:S(2)}) %all-to-all-start.2) | async-done | bytes 196640 | tf_op jit(solution)/shard_map/all_to_all | solution.py:509
  75.5 1.7 %pull.1 = f32[128,2,128]{2,1,0:T(2,128)} custom-call(s32[1]{0:T(128)} %bitcast.beta_ref, f32[64,6,128]{2,1,0:T(8,128)S(1)} %all-to-all-done.2.r_ref, f32[64,12,128]{2,1,0:T(8,128)S(1)} %all-to-all-done.r_ref.t_ref, bf16[8,128,128]{2,1,0:T(8,128)(2,1)S(1)} %copy-done.3, bf16[8,128,128]{2,1,0:T(8,128)(2,1)S(1)} %copy-done.2, ...), custom_call_target="tpu_custom_call" | custom-call | tf_op jit(solution)/shard_map/pull/pallas_call | solution.py:511
  77.2 4.1 %all-to-all-start.3 = ((f32[128,2,128]{2,1,0:T(2,128)}), f32[128,2,128]{2,1,0:T(2,128)S(1)}, u32[]{:S(2)}, u32[]{:S(2)}) async-start(f32[128,2,128]{2,1,0:T(2,128)} %pull.1), calls=%async_computation.3 | async-start | bytes 262144 | tf_op jit(solution)/shard_map/all_to_all | solution.py:525
  81.4 0.0 collective-permute-done.theirs_hbm
  81.4 9.8 %all-to-all-done.3.r_ref = f32[128,2,128]{2,1,0:T(2,128)S(1)} async-done(((f32[128,2,128]{2,1,0:T(2,128)}), f32[128,2,128]{2,1,0:T(2,128)S(1)}, u32[]{:S(2)}, u32[]{:S(2)}) %all-to-all-start.3) | async-done | bytes 131104 | tf_op jit(solution)/shard_map/all_to_all | solution.py:525
  91.2 2.6 %final.1 = f32[2,128,128]{2,1,0:T(8,128)} custom-call(f32[128,2,128]{2,1,0:T(2,128)S(1)} %all-to-all-done.3.r_ref, bf16[768,128]{1,0:T(8,128)(2,1)S(1)} %copy-done.13, bf16[768,128]{1,0:T(8,128)(2,1)S(1)} %copy-done.12, bf16[768,128]{1,0:T(8,128)(2,1)S(1)} %copy-done.11, bf16[768,128]{1,0:T(8,128)(2,1)S(1)} %copy-done.10, ...), custom_call_target="tpu_custom_call" | custom-call | tf_op jit(solution)/shard_map/final/pallas_call | solution.py:527
  (20 shorter events, 0.0 us)
Async XLA Ops:
  0.0 30.8 %copy-start.9 = (bf16[256,768]{1,0:T(8,128)(2,1)S(1)}, bf16[256,768]{1,0:T(8,128)(2,1)}, u32[]{:S(2)}) copy-start(bf16[256,768]{1,0:T(8,128)(2,1)} %constant.54.clone.eb) | copy-start | bytes 1179652
  4.2 26.6 %copy-start = (bf16[8,128,128]{2,1,0:T(8,128)(2,1)S(1)}, bf16[8,128,128]{2,1,0:T(8,128)(2,1)}, u32[]{:S(2)}) copy-start(bf16[8,128,128]{2,1,0:T(8,128)(2,1)} %constant.48.clone.xil) | copy-start | bytes 786436
  4.2 26.5 %copy-start.1 = (bf16[8,128,128]{2,1,0:T(8,128)(2,1)S(1)}, bf16[8,128,128]{2,1,0:T(8,128)(2,1)}, u32[]{:S(2)}) copy-start(bf16[8,128,128]{2,1,0:T(8,128)(2,1)} %constant.47.clone.xih) | copy-start | bytes 786436
  4.2 26.5 %copy-start.2 = (bf16[8,128,128]{2,1,0:T(8,128)(2,1)S(1)}, bf16[8,128,128]{2,1,0:T(8,128)(2,1)}, u32[]{:S(2)}) copy-start(bf16[8,128,128]{2,1,0:T(8,128)(2,1)} %constant.46.clone.xbl) | copy-start | bytes 786436
  4.2 26.5 %copy-start.3 = (bf16[8,128,128]{2,1,0:T(8,128)(2,1)S(1)}, bf16[8,128,128]{2,1,0:T(8,128)(2,1)}, u32[]{:S(2)}) copy-start(bf16[8,128,128]{2,1,0:T(8,128)(2,1)} %constant.45.clone.xbh) | copy-start | bytes 786436
  4.3 26.5 %all-to-all-start = ((f32[64,12,128]{2,1,0:T(8,128)}), f32[64,12,128]{2,1,0:T(8,128)S(1)}, u32[]{:S(2)}, u32[]{:S(2)}) async-start(f32[64,12,128]{2,1,0:T(8,128)} %bitcast.12), calls=%async_computation | async-start | bytes 1048576 | tf_op jit(solution)/shard_map/all_to_all | solution.py:490
  32.1 18.7 %copy-start.4 = (f32[2,128,128]{2,1,0:T(8,128)S(1)}, f32[2,128,128]{2,1,0:T(8,128)}, u32[]{:S(2)}) copy-start(f32[2,128,128]{2,1,0:T(8,128)} %p_hbm.3) | copy-start | bytes 393220
  32.1 18.7 %copy-start.5 = (f32[2,128,128]{2,1,0:T(8,128)S(1)}, f32[2,128,128]{2,1,0:T(8,128)}, u32[]{:S(2)}) copy-start(f32[2,128,128]{2,1,0:T(8,128)} %d_hbm.3) | copy-start | bytes 393220
  32.1 18.6 %copy-start.6 = (f32[1,2,128,128]{3,2,1,0:T(8,128)S(1)}, f32[1,2,128,128]{3,2,1,0:T(8,128)}, u32[]{:S(2)}) copy-start(f32[1,2,128,128]{3,2,1,0:T(8,128)} %param.22) | copy-start | bytes 393220
  32.2 18.6 %copy-start.7 = (bf16[864,256]{1,0:T(8,128)(2,1)S(1)}, bf16[864,256]{1,0:T(8,128)(2,1)}, u32[]{:S(2)}) copy-start(bf16[864,256]{1,0:T(8,128)(2,1)} %constant.49.clone.tab) | copy-start | bytes 1327108
  50.8 0.7 copy-start.14
  59.4 16.1 %copy-start.8 = (bf16[768,256]{1,0:T(8,128)(2,1)S(1)}, bf16[768,256]{1,0:T(8,128)(2,1)}, u32[]{:S(2)}) copy-start(bf16[768,256]{1,0:T(8,128)(2,1)} %constant.55.clone.ed) | copy-start | bytes 1179652
  59.4 16.1 %all-to-all-start.2 = ((f32[64,6,128]{2,1,0:T(8,128)}), f32[64,6,128]{2,1,0:T(8,128)S(1)}, u32[]{:S(2)}, u32[]{:S(2)}) async-start(f32[64,6,128]{2,1,0:T(8,128)} %bitcast.7), calls=%async_computation.2 | async-start | bytes 524288 | tf_op jit(solution)/shard_map/all_to_all | solution.py:509
  64.2 17.2 %collective-permute-start = (f32[2,128,128]{2,1,0:T(8,128)S(1)}, f32[2,128,128]{2,1,0:T(8,128)S(1)}, u32[]{:S(2)}, u32[]{:S(2)}) collective-permute-start(f32[2,128,128]{2,1,0:T(8,128)S(1)} %get-tuple-element.12.mine_hbm), channel_id=1, source_target_pairs={{0,64},{64,0},{1,65},{65,1},{2,66},{66,2},{3,67},{67,3},{4,68},{68... | collective-permute-start | bytes 393224 | tf_op jit(solution)/shard_map/ppermute | solution.py:508
  75.5 15.6 %copy-start.11 = (bf16[768,128]{1,0:T(8,128)(2,1)S(1)}, bf16[768,128]{1,0:T(8,128)(2,1)}, u32[]{:S(2)}) copy-start(bf16[768,128]{1,0:T(8,128)(2,1)} %constant.52.clone.zh) | copy-start | bytes 589828
  75.5 15.6 %copy-start.12 = (bf16[768,128]{1,0:T(8,128)(2,1)S(1)}, bf16[768,128]{1,0:T(8,128)(2,1)}, u32[]{:S(2)}) copy-start(bf16[768,128]{1,0:T(8,128)(2,1)} %constant.51.clone.yl) | copy-start | bytes 589828
  75.5 15.6 %copy-start.13 = (bf16[768,128]{1,0:T(8,128)(2,1)S(1)}, bf16[768,128]{1,0:T(8,128)(2,1)}, u32[]{:S(2)}) copy-start(bf16[768,128]{1,0:T(8,128)(2,1)} %constant.50.clone.yh) | copy-start | bytes 589828
  77.2 14.0 %copy-start.10 = (bf16[768,128]{1,0:T(8,128)(2,1)S(1)}, bf16[768,128]{1,0:T(8,128)(2,1)}, u32[]{:S(2)}) copy-start(bf16[768,128]{1,0:T(8,128)(2,1)} %constant.53.clone.zl) | copy-start | bytes 589828
  77.2 13.9 %all-to-all-start.3 = ((f32[128,2,128]{2,1,0:T(2,128)}), f32[128,2,128]{2,1,0:T(2,128)S(1)}, u32[]{:S(2)}, u32[]{:S(2)}) async-start(f32[128,2,128]{2,1,0:T(2,128)} %pull.1), calls=%async_computation.3 | async-start | bytes 262144 | tf_op jit(solution)/shard_map/all_to_all | solution.py:525

commit v3 on v2

--- a/solution.py
+++ b/solution.py
@@ -69,6 +69,7 @@
                 ang = angle * ((signed(np.array(a)) * x_of) % GRID)
                 xb[beta, slot], xb[beta, 64 + slot] = np.cos(ang), np.sin(ang)
     xi = xb.transpose(0, 2, 1).copy()
+    xp = xi.reshape(BETAS, 2, 64, 2 * OWNERS).transpose(0, 2, 1, 3).reshape(BETAS, GRID, 2 * OWNERS).copy()
 
     eb = np.zeros((2 * LANES, 3, 2, LANES))
     for bi in range(3):
@@ -112,20 +113,18 @@
                 ed[bi, 0, hr, 1, li] = ed[bi, 0, hi, 1, li] = 1
     ed = ed.reshape(6 * LANES, 2 * LANES)
 
-    ye = np.zeros((3, 2, GRID, 2, BETAS, KAPPAS))
-    ze = np.zeros((3, 2, LANES, GRID))
-    for bi in range(3):
-        for beta in range(BETAS):
-            ye[bi, 0, :, :, beta, :] = cos_y[3 * beta + bi][:, None, None]
-            ye[bi, 1, :, :, beta, :] = sin_y[3 * beta + bi][:, None, None]
-        r, i = slice(bi * HALF, bi * HALF + MODES), slice(bi * HALF + MODES, (bi + 1) * HALF)
-        ze[bi, 0, r], ze[bi, 0, i] = cos_z, -sin_z
-        ze[bi, 1, r], ze[bi, 1, i] = -sin_z, -cos_z
-    ye = ye.reshape(6 * GRID, 2 * OWNERS)
-    ze = ze.reshape(6 * LANES, GRID) * scale
+    ze = np.zeros((LANES, 2, GRID))
+    for q in range(2):
+        at = q * PAIR
+        ze[at : at + 12, q], ze[at + 12 : at + 24, q] = cos_z, -sin_z
+        ze[at + 24 : at + 36, q], ze[at + 36 : at + 48, q] = -sin_z, -cos_z
+    zh, zl = halves(ze.reshape(LANES, 2 * GRID) * scale)
+    final = np.zeros((512, 2 * GRID), ml_dtypes.bfloat16)
+    final[0:128], final[128:256], final[256:384] = zh, zh, zl
+    final[384:512] = field[736:864]
 
     return dict(
-        first=first, xb=halves(xb), xi=halves(xi), field=field, ye=halves(ye), ze=halves(ze),
+        first=first, xb=halves(xb), xi=halves(xi), field=field, final=final, xp=halves(xp),
         eb=eb.astype(ml_dtypes.bfloat16), ed=ed.astype(ml_dtypes.bfloat16),
     )
 
@@ -164,17 +163,16 @@
 
 
 def first_kernel(
-    pen_ref, rock_ref, well_ref, s_hbm, p_hbm, d_hbm, i_hbm, tab_hbm, mix_hbm, off_hbm,
-    out_ref, scal_ref, s_ref, p_ref, d_ref, i_ref, tab, mix_ref, off_ref, t_ref, sems,
+    pen_ref, rock_ref, well_ref, s_hbm, p_hbm, d_hbm, i_hbm, tab_hbm,
+    out_ref, s_ref, p_ref, d_ref, i_ref, tab, t_ref, sems,
 ):
     pairs = (
         (tab_hbm, tab), (p_hbm, p_ref), (d_hbm, d_ref), (i_hbm, i_ref),
-        (mix_hbm, mix_ref), (off_hbm, off_ref), (s_hbm, s_ref),
+        (s_hbm, s_ref),
     )
     copies = [pltpu.make_async_copy(src, dst, sems.at[k]) for k, (src, dst) in enumerate(pairs)]
     for copy in copies:
         copy.start()
-    out_ref[:, :, 6:, :] = jnp.zeros((BETAS, KAPPAS, 6, LANES), F32)
     for copy in copies[:-1]:
         copy.wait()
     x = jnp.concatenate([r[k] for r in (p_ref, d_ref, i_ref) for k in range(2)], axis=0)
@@ -184,20 +182,22 @@
         for k in range(6)
     ]
     v = left(tab[256:280], tab[288:312], jnp.concatenate(cols, axis=1))
-    for k in range(6):
-        col = v[:, k * LANES : (k + 1) * LANES]
-        total = col[0:8]
-        for bi in (1, 2):
-            total = total + pltpu.roll(col[8 * bi : 8 * bi + 8], HALF * bi, 1)
+    lane = lax.broadcasted_iota(jnp.int32, (BETAS, LANES), 1)
+    piece = [
+        [v[8 * bi : 8 * bi + 8, k * LANES : (k + 1) * LANES] for bi in range(3)] for k in range(6)
+    ]
+    rows = [pltpu.roll(piece[k][2], 96, 1) for k in range(6)]
+    for bi in range(2):
+        for third in range(3):
+            moved = pltpu.roll(piece[5][bi], 120 - 8 * third, 1)
+            rows[3 * bi + third] = jnp.where(lane >= 120, moved, rows[3 * bi + third])
+        total = piece[0][bi]
+        for k in range(1, 5):
+            total = total + pltpu.roll(piece[k][bi], HALF * k, 1)
+        rows.append(total)
+    for r in range(8):
         for kappa in range(KAPPAS):
-            out_ref[:, kappa, k, :] = total
-
-    rock = mix_ref[0:1] * rock_ref[0]
-    well = mix_ref[0:1] * well_ref[0]
-    for i in range(1, CHANNELS):
-        rock = rock + mix_ref[i : i + 1] * rock_ref[i]
-        well = well + mix_ref[i : i + 1] * well_ref[i]
-    scal_ref[0:1], scal_ref[1:2], scal_ref[2:3] = rock, well, off_ref[...]
+            out_ref[kappa, :, r, :] = rows[r]
 
     copies[-1].wait()
     for part in range(2):
@@ -225,13 +225,30 @@
         beta = lax.rem(3 * pen_ref[0] + j, BETAS)
         for kind in range(2):
             for bi in range(3):
-                out_ref[beta, :, 6 + 3 * kind + bi, :] = block[kind][3 * j + bi]
+                r = 3 * kind + bi
+                out_ref[:, beta, r, :] = out_ref[:, beta, r, :] + block[kind][3 * j + bi]
 
 
 def owners_kernel(beta_ref, r_ref, xbh, xbl, xih, xil, eb, out_ref):
-    fields = [
-        jnp.concatenate([r_ref[:, 2 * f, :], r_ref[:, 2 * f + 1, :]], axis=0) for f in range(3)
-    ]
+    raw = [r_ref[:, r, :] for r in range(8)]
+    lane = lax.broadcasted_iota(jnp.int32, (OWNERS, LANES), 1)
+
+    def take(x, source, target, width, base):
+        shift = (target - source) % LANES
+        moved = pltpu.roll(x, shift, 1) if shift else x
+        return jnp.where((lane >= target) & (lane < target + width), moved, base)
+
+    planes = []
+    for k in range(6):
+        x = take(raw[k], 96, 48, HALF, jnp.zeros((OWNERS, LANES), F32))
+        for bi in range(2):
+            if k < 5:
+                x = take(raw[6 + bi], HALF * k, HALF * bi, HALF, x)
+            else:
+                for third in range(3):
+                    x = take(raw[3 * bi + third], 120, HALF * bi + 8 * third, 8, x)
+        planes.append(x)
+    fields = [jnp.concatenate(planes[2 * f : 2 * f + 2], axis=0) for f in range(3)]
     g = left(xbh[0], xbl[0], jnp.concatenate(fields, axis=1))
     pre = [
         right_exact(
@@ -245,7 +262,7 @@
     real = part_mask((OWNERS, LANES))
     stack = []
     for bi in range(3):
-        t, w = r_ref[:, 6 + bi, :], r_ref[:, 9 + bi, :]
+        t, w = raw[bi], raw[3 + bi]
         ts, ws = swap(t, real), swap(w, real)
         lo, mid, hi = 2 * bi * LANES, (2 * bi + 1) * LANES, (2 * bi + 2) * LANES
         coeff = (
@@ -297,7 +314,7 @@
             for plane in range(2):
                 for kappa in kappas:
                     s = jnp.concatenate(
-                        [r_ref[:, kappa, plane * 6 + bi * 2 + field, :] for bi in range(3)], axis=0
+                        [r_ref[kappa, :, plane * 6 + bi * 2 + field, :] for bi in range(3)], axis=0
                     )
                     right_pair = pltpu.roll(s, PAIR, 1)
                     left_pair = pltpu.roll(s, LANES - PAIR, 1)
@@ -373,7 +390,7 @@
                 jnp.where(high, pltpu.roll(second[:HALF], PAIR, 1) + second[HALF:], zero),
             )
             for bi in range(3):
-                out_ref[:, kappa, plane * 3 + bi, :] = w[8 * bi : 8 * bi + 8]
+                out_ref[kappa, :, plane * 3 + bi, :] = w[8 * bi : 8 * bi + 8]
 
 
 GROUP = 1
@@ -387,35 +404,49 @@
     real = part_mask((OWNERS, LANES))
     parts = []
     for bi in range(3):
-        t = t_ref[:, 6 + bi, :]
+        t = t_ref[:, bi, :]
         fr, fi = g[:64, bi * LANES : (bi + 1) * LANES], g[64:, bi * LANES : (bi + 1) * LANES]
         s = swap(fi, real)
         v = fr + jnp.where(real, s, -s)
         parts += [t * v, t * swap(v, real)]
     q = right_exact(jnp.concatenate(parts, axis=1), ed[...])
     h = left(xih[0], xil[0], jnp.concatenate([q[:, :LANES], q[:, LANES:]], axis=0))
-    for plane in range(2):
-        for source in range(2):
-            out_ref[64 * source : 64 * source + 64, plane, :] = h[plane * 64 : plane * 64 + 64]
-
-
-def final_kernel(
-    r_ref, yh, yl, zh, zl, mine_hbm, theirs_hbm, out_ref, mine_ref, theirs_ref, sems
-):
+    for source in range(2):
+        out_ref[GRID * source : GRID * source + GRID] = h
+
+
+def final_kernel(r_ref, tab, mine_hbm, theirs_hbm, out_ref, mine_ref, theirs_ref, sems):
     copies = [
         pltpu.make_async_copy(src, dst, sems.at[k])
         for k, (src, dst) in enumerate(((mine_hbm, mine_ref), (theirs_hbm, theirs_ref)))
     ]
     for copy in copies:
         copy.start()
-    g = left(yh[...], yl[...], jnp.concatenate([r_ref[:, 0, :], r_ref[:, 1, :]], axis=1))
+    lane = lax.broadcasted_iota(jnp.int32, (BETAS, LANES), 1)
+    rows = [[], []]
+    total = []
+    for plane in range(2):
+        x = r_ref[pl.ds(plane, BETAS, stride=2), :]
+        for k in range(1, 2 * KAPPAS):
+            x = x + r_ref[pl.ds(2 * BETAS * k + plane, BETAS, stride=2), :]
+        total.append(x)
+    for part in range(2):
+        for bi in range(3):
+            x = jnp.zeros((BETAS, LANES), F32)
+            for plane in range(2):
+                at = plane * PAIR + part * HALF
+                shift = (at - HALF * bi) % LANES
+                moved = pltpu.roll(total[plane], shift, 1) if shift else total[plane]
+                x = jnp.where((lane >= at) & (lane < at + HALF), moved, x)
+            rows[part].append(x)
+    top, rest = split(jnp.concatenate(rows[0] + rows[1], axis=0))
+    y = dot(tab[384:512, :144], jnp.concatenate([top, top, rest], axis=0))
+    top, rest = split(y)
+    z = dot(jnp.concatenate([top, rest], axis=1), tab[0:256]) + dot(top, tab[256:384])
     for copy in copies:
         copy.wait()
     for plane in range(2):
-        rows = jnp.concatenate(
-            [g[k * GRID : (k + 1) * GRID, plane * LANES : (plane + 1) * LANES] for k in range(6)], axis=1
-        )
-        out_ref[plane] = right(rows, zh[...], zl[...]) + (mine_ref[plane] + theirs_ref[plane])
+        out_ref[plane] = z[:, plane * GRID : (plane + 1) * GRID] + (mine_ref[plane] + theirs_ref[plane])
 
 
 VMEM = pl.BlockSpec(memory_space=pltpu.VMEM)
@@ -436,7 +467,7 @@
     return pl.pallas_call(
         field_kernel,
         out_shape=[
-            jax.ShapeDtypeStruct((BETAS, KAPPAS, 6, LANES), F32),
+            jax.ShapeDtypeStruct((KAPPAS, BETAS, 6, LANES), F32),
             jax.ShapeDtypeStruct((2, GRID, GRID), F32),
         ],
         in_specs=[HBM, VMEM, VMEM, HBM, HBM, HBM],
@@ -460,33 +491,28 @@
         for k, v in TABLES.items()
     }
     pen = lax.axis_index("pen")
-    beta = (pen // KAPPAS).astype(jnp.int32).reshape(1)
+    beta = lax.rem(pen, BETAS).astype(jnp.int32).reshape(1)
     inj = injection[0]
 
-    send, scal = pl.pallas_call(
+    send = pl.pallas_call(
         first_kernel,
-        out_shape=[
-            jax.ShapeDtypeStruct((BETAS, KAPPAS, 12, LANES), F32),
-            jax.ShapeDtypeStruct((3, CHANNELS), F32),
-        ],
-        in_specs=[SMEM] * 3 + [HBM] * 7,
-        out_specs=[VMEM] * 2,
+        out_shape=jax.ShapeDtypeStruct((KAPPAS, BETAS, 8, LANES), F32),
+        in_specs=[SMEM] * 3 + [HBM] * 5,
+        out_specs=VMEM,
         scratch_shapes=[
             pltpu.VMEM((2, CHANNELS, CHANNELS, spectral.shape[0]), F32),
             *[pltpu.VMEM((2, GRID, GRID), F32)] * 3,
             pltpu.VMEM((320, 2 * LANES), BF16),
-            pltpu.VMEM((CHANNELS, CHANNELS), F32),
-            pltpu.VMEM((1, CHANNELS), F32),
             pltpu.VMEM((4, CHANNELS, LANES), F32),
-            pltpu.SemaphoreType.DMA((7,)),
+            pltpu.SemaphoreType.DMA((5,)),
         ],
         name="first",
         compiler_params=pltpu.CompilerParams(vmem_limit_bytes=60 * 1024 * 1024),
     )(
         pen.astype(jnp.int32).reshape(1), lift_rock, lift_well, spectral.transpose(1, 2, 3, 0),
-        permeability, direction, inj, tab["first"], pointwise, offsets.reshape(1, CHANNELS),
+        permeability, direction, inj, tab["first"],
     )
-    send = send.reshape(OWNERS, 12, LANES)
+    send = send.reshape(OWNERS, 8, LANES)
     owned = lax.all_to_all(send, "pen", 0, 0, tiled=True)
 
     square = (2 * OWNERS, GRID)
@@ -496,7 +522,7 @@
         grid_spec=pltpu.PrefetchScalarGridSpec(
             num_scalar_prefetch=1,
             grid=(1,),
-            in_specs=[whole((OWNERS, 12, LANES))] + [by_beta(square)] * 4 + [whole((2 * LANES, 6 * LANES))],
+            in_specs=[whole((OWNERS, 8, LANES))] + [by_beta(square)] * 4 + [whole((2 * LANES, 6 * LANES))],
             out_specs=whole((OWNERS, 12, LANES)),
         ),
         name="owners",
@@ -504,35 +530,38 @@
     )(beta, owned, *tab["xb"], *tab["xi"], tab["eb"])
     got = lax.all_to_all(send, "pen", 0, 0, tiled=True)
 
-    send, local = field_call(scal, got.reshape(BETAS, KAPPAS, 12, LANES), tab["field"], permeability, direction, inj)
+    rock = jnp.sum(pointwise * lift_rock[:, None], axis=0)
+    well = jnp.sum(pointwise * lift_well[:, None], axis=0)
+    scal = jnp.stack([rock, well, offsets])
+    send, local = field_call(scal, got.reshape(KAPPAS, BETAS, 12, LANES), tab["field"], permeability, direction, inj)
     theirs = lax.ppermute(local, "src", [(0, 1), (1, 0)])
     back = lax.all_to_all(send.reshape(OWNERS, 6, LANES), "pen", 0, 0, tiled=True)
 
     send = pl.pallas_call(
         pull_kernel,
-        out_shape=jax.ShapeDtypeStruct((2 * OWNERS, 2, LANES), F32),
+        out_shape=jax.ShapeDtypeStruct((4 * OWNERS, LANES), F32),
         grid_spec=pltpu.PrefetchScalarGridSpec(
             num_scalar_prefetch=1,
             grid=(1,),
-            in_specs=[whole((OWNERS, 6, LANES)), whole((OWNERS, 12, LANES))]
+            in_specs=[whole((OWNERS, 6, LANES)), whole((OWNERS, 8, LANES))]
             + [by_beta(square)] * 4
             + [whole((6 * LANES, 2 * LANES))],
-            out_specs=whole((2 * OWNERS, 2, LANES)),
+            out_specs=whole((4 * OWNERS, LANES)),
         ),
         name="pull",
         **PARAMS,
-    )(beta, back, owned, *tab["xb"], *tab["xi"], tab["ed"])
+    )(beta, back, owned, *tab["xb"], *tab["xp"], tab["ed"])
     last = lax.all_to_all(send, ("src", "pen"), 0, 0, tiled=True)
 
     return pl.pallas_call(
         final_kernel,
         out_shape=jax.ShapeDtypeStruct((2, GRID, GRID), F32),
-        in_specs=[VMEM] * 5 + [HBM] * 2,
+        in_specs=[VMEM] * 2 + [HBM] * 2,
         out_specs=VMEM,
         scratch_shapes=[pltpu.VMEM((2, GRID, GRID), F32)] * 2 + [pltpu.SemaphoreType.DMA((2,))],
         name="final",
         **PARAMS,
-    )(last, *tab["ye"], *tab["ze"], local, theirs)
+    )(last, tab["final"], local, theirs)
 
 
 TABLES = build_tables()

time: 94.3 us -> 90.6 us (0.961)
  blocking collectives: 18.6 us -> 0 us
  waiting for transfers between devices: 34.1 us -> 44.9 us
  starting transfers between devices: 22.4 us -> 26.8 us
    all_to_all x1 -> x0, blocking collectives: 18.6 us -> none  [shards(): got = lax.all_to_all(send, 'pen', 0, 0, tiled=True)]
    all_to_all x0 -> x1, waiting for transfers between devices: none -> 13.3 us  [shards(): got = lax.all_to_all(send, 'pen', 0, 0, tiled=True)]
    all_to_all x0 -> x1, starting transfers between devices: none -> 4.68 us  [shards(): got = lax.all_to_all(send, 'pen', 0, 0, tiled=True)]
    all_to_all x1, waiting for transfers between devices: 14 us -> 11.3 us  [shards(): owned = lax.all_to_all(send, 'pen', 0, 0, tiled=True)]
    pallas_call x1, Pallas kernels: 2.57 us -> 1.41 us  [shards(): pl.pallas_call(final_kernel, out_shape=jax.ShapeDtypeStruct((2, GRID, GRI...]
  transfers between devices with their start and end apart: 4 -> 5, of which waited for: 3 -> 4; matrix products, arithmetic and copies ran while one was open for 0% -> 0% of each run, Pallas kernels for 2% -> 2%
where the time goes in v3:
time: 90.6 us; the launch traced here: 90.1 us
  waiting for transfers between devices  44.9 us (50%)
  starting transfers between devices  26.8 us (30%)
  Pallas kernels  17.4 us (19%)
    all_to_all x1, waiting for transfers between devices, shards(): got = lax.all_to_all(send, 'pen', 0, 0, tiled=True)  13.3 us
    all_to_all x1, starting transfers between devices, shards(): owned = lax.all_to_all(send, 'pen', 0, 0, tiled=True)  12.4 us
    all_to_all x1, waiting for transfers between devices, shards(): owned = lax.all_to_all(send, 'pen', 0, 0, tiled=True)  11.3 us
    all_to_all x1, waiting for transfers between devices, shards(): lax.all_to_all(send.reshape(OWNERS, 6, LANES), 'pen', 0, 0, tiled=True)  10.5 us
    all_to_all x1, waiting for transfers between devices, shards(): last = lax.all_to_all(send, ('src', 'pen'), 0, 0, tiled=True)  9.78 us
    pallas_call x1, Pallas kernels, field_call(): pl.pallas_call(field_kernel, out_shape=[jax.ShapeDtypeStruct((KAPPAS, BET...  7.91 us
    all_to_all x1, starting transfers between devices, shards(): lax.all_to_all(send.reshape(OWNERS, 6, LANES), 'pen', 0, 0, tiled=True)  4.78 us
    all_to_all x1, starting transfers between devices, shards(): got = lax.all_to_all(send, 'pen', 0, 0, tiled=True)  4.68 us
  transfers between devices with their start and end apart: 5, of which 4 were waited for; matrix products, arithmetic and copies ran while one was open for 0% of the time, Pallas kernels for 2%

profile of v3, /device:TPU:1, one launch (start us, length us, event | category | flops | bytes accessed | tf_op | source)
XLA Modules:
  0.0 90.1 jit_solution(12731455627597997019)
XLA Ops:
  0.0 4.2 %first.1 = f32[8,8,8,128]{3,2,1,0:T(8,128)} custom-call(s32[1]{0:T(128)} %bitcast.4.pen_ref, f32[32]{0:T(128)} %rock_ref.1, f32[32]{0:T(128)} %well_ref.1, f32[2,32,32,108]{3,2,1,0:T(8,128)} %bitcast.16, f32[2,128,128]{2,1,0:T(8,128)} %p_hbm.3, f32[2,128,128]{2,1,0:T(8,128)} %d_hbm.3, f32[2,128,128]{2,1,0:T(8,128)} %bitcast.14, ...), custom_call_target="tpu_custom_call" | custom-call | tf_op jit(solution)/shard_map/first/pallas_call | solution.py:497
  4.2 0.0 copy-start
  4.2 0.0 copy-start.1
  4.2 12.4 %all-to-all-start = ((f32[64,8,128]{2,1,0:T(8,128)}), f32[64,8,128]{2,1,0:T(8,128)S(1)}, u32[]{:S(2)}, u32[]{:S(2)}) async-start(f32[64,8,128]{2,1,0:T(8,128)} %bitcast.17), calls=%async_computation | async-start | bytes 524288 | tf_op jit(solution)/shard_map/all_to_all | solution.py:516
  16.7 11.3 %all-to-all-done.r_ref.t_ref = f32[64,8,128]{2,1,0:T(8,128)S(1)} async-done(((f32[64,8,128]{2,1,0:T(8,128)}), f32[64,8,128]{2,1,0:T(8,128)S(1)}, u32[]{:S(2)}, u32[]{:S(2)}) %all-to-all-start) | async-done | bytes 262176 | tf_op jit(solution)/shard_map/all_to_all | solution.py:516
  28.0 2.2 %owners.1 = f32[64,12,128]{2,1,0:T(8,128)} custom-call(s32[1]{0:T(128)} %bitcast.beta_ref, f32[64,8,128]{2,1,0:T(8,128)S(1)} %all-to-all-done.r_ref.t_ref, bf16[8,128,128]{2,1,0:T(8,128)(2,1)S(1)} %copy-done, bf16[8,128,128]{2,1,0:T(8,128)(2,1)S(1)} %copy-done.1, bf16[8,128,128]{2,1,0:T(8,128)(2,1)S(1)} %copy-done.11, bf16[8,128,128]{2,1,0:T(8,128)(2,1)S(1)} %copy-done.12, ...), custom_call_target="tpu_custom_call" | custom-call | tf_op jit(solution)/shard_map/owners/pallas_call | solution.py:519
  30.3 0.0 copy-start.3
  30.3 0.0 copy-start.4
  30.3 0.0 copy-start.5
  30.3 4.7 %all-to-all-start.1 = ((f32[64,12,128]{2,1,0:T(8,128)}), f32[64,12,128]{2,1,0:T(8,128)S(1)}, u32[]{:S(2)}, u32[]{:S(2)}) async-start(f32[64,12,128]{2,1,0:T(8,128)} %owners.1), calls=%async_computation.1 | async-start | bytes 1048576 | tf_op jit(solution)/shard_map/all_to_all | solution.py:531
  35.0 0.1 multiply_reduce_fusion.1
  35.1 0.7 copy-done.16
  35.8 13.3 %all-to-all-done.1 = f32[64,12,128]{2,1,0:T(8,128)S(1)} async-done(((f32[64,12,128]{2,1,0:T(8,128)}), f32[64,12,128]{2,1,0:T(8,128)S(1)}, u32[]{:S(2)}, u32[]{:S(2)}) %all-to-all-start.1) | async-done | bytes 393248 | tf_op jit(solution)/shard_map/all_to_all | solution.py:531
  49.1 0.0 copy-start.9
  49.1 0.0 copy-start.10
  49.1 7.9 %field.1 = (f32[8,8,6,128]{3,2,1,0:T(8,128)}, f32[2,128,128]{2,1,0:T(8,128)S(1)}) custom-call(f32[3,32]{1,0:T(4,128)S(1)} %pad_maximum_fusion.scal_hbm, f32[8,8,12,128]{3,2,1,0:T(8,128)S(1)} %bitcast.12, bf16[864,256]{1,0:T(8,128)(2,1)S(1)} %copy-done.5, f32[2,128,128]{2,1,0:T(8,128)S(1)} %copy-done.2, f32[2,128,128]{2,1,0:T(8,128)S(1)} %copy-done.3, ...), custom_call_target="tpu_custom_call" | custom-call | tf_op jit(solution)/shard_map/field/pallas_call | solution.py:467
  57.0 0.0 copy-start.6
  57.0 4.8 %all-to-all-start.2 = ((f32[64,6,128]{2,1,0:T(8,128)}), f32[64,6,128]{2,1,0:T(8,128)S(1)}, u32[]{:S(2)}, u32[]{:S(2)}) async-start(f32[64,6,128]{2,1,0:T(8,128)} %bitcast.9), calls=%async_computation.2 | async-start | bytes 524288 | tf_op jit(solution)/shard_map/all_to_all | solution.py:538
  61.8 0.8 collective-permute-start
  62.6 10.5 %all-to-all-done.2.r_ref = f32[64,6,128]{2,1,0:T(8,128)S(1)} async-done(((f32[64,6,128]{2,1,0:T(8,128)}), f32[64,6,128]{2,1,0:T(8,128)S(1)}, u32[]{:S(2)}, u32[]{:S(2)}) %all-to-all-start.2) | async-done | bytes 196640 | tf_op jit(solution)/shard_map/all_to_all | solution.py:538
  73.2 1.6 %pull.1 = f32[256,128]{1,0:T(8,128)} custom-call(s32[1]{0:T(128)} %bitcast.beta_ref, f32[64,6,128]{2,1,0:T(8,128)S(1)} %all-to-all-done.2.r_ref, f32[64,8,128]{2,1,0:T(8,128)S(1)} %all-to-all-done.r_ref.t_ref, bf16[8,128,128]{2,1,0:T(8,128)(2,1)S(1)} %copy-done, bf16[8,128,128]{2,1,0:T(8,128)(2,1)S(1)} %copy-done.1, bf16[8,128,128]{2,1,0:T(8,128)(2,1)S(1)} %copy-done.9, ...), custom_call_target="tpu_custom_call" | custom-call | tf_op jit(solution)/shard_map/pull/pallas_call | solution.py:540
  74.8 4.1 %all-to-all-start.3 = ((f32[128,2,128]{2,1,0:T(2,128)}), f32[128,2,128]{2,1,0:T(2,128)S(1)}, u32[]{:S(2)}, u32[]{:S(2)}) async-start(f32[128,2,128]{2,1,0:T(2,128)} %bitcast.10), calls=%async_computation.3 | async-start | bytes 262144 | tf_op jit(solution)/shard_map/all_to_all | solution.py:554
  78.9 9.8 %all-to-all-done.3 = f32[128,2,128]{2,1,0:T(2,128)S(1)} async-done(((f32[128,2,128]{2,1,0:T(2,128)}), f32[128,2,128]{2,1,0:T(2,128)S(1)}, u32[]{:S(2)}, u32[]{:S(2)}) %all-to-all-start.3) | async-done | bytes 131104 | tf_op jit(solution)/shard_map/all_to_all | solution.py:554
  88.7 1.4 %final.1 = f32[2,128,128]{2,1,0:T(8,128)} custom-call(f32[256,128]{1,0:T(8,128)S(1)} %bitcast.13, bf16[512,256]{1,0:T(8,128)(2,1)S(1)} %copy-done.8, f32[2,128,128]{2,1,0:T(8,128)S(1)} %get-tuple-element.8.mine_hbm, f32[2,128,128]{2,1,0:T(8,128)S(1)} %collective-permute-done.theirs_hbm), custom_call_target="tpu_custom_call" | custom-call | tf_op jit(solution)/shard_map/final/pallas_call | solution.py:556
  (27 shorter events, 0.1 us)
Async XLA Ops:
  0.0 28.0 %copy-start.7 = (bf16[256,768]{1,0:T(8,128)(2,1)S(1)}, bf16[256,768]{1,0:T(8,128)(2,1)}, u32[]{:S(2)}) copy-start(bf16[256,768]{1,0:T(8,128)(2,1)} %constant.42.clone.eb) | copy-start | bytes 1179652
  0.0 28.0 %copy-start.11 = (bf16[8,128,128]{2,1,0:T(8,128)(2,1)S(1)}, bf16[8,128,128]{2,1,0:T(8,128)(2,1)}, u32[]{:S(2)}) copy-start(bf16[8,128,128]{2,1,0:T(8,128)(2,1)} %constant.36.clone.xih) | copy-start | bytes 786436
  0.0 28.0 %copy-start.12 = (bf16[8,128,128]{2,1,0:T(8,128)(2,1)S(1)}, bf16[8,128,128]{2,1,0:T(8,128)(2,1)}, u32[]{:S(2)}) copy-start(bf16[8,128,128]{2,1,0:T(8,128)(2,1)} %constant.37.clone.xil) | copy-start | bytes 786436
  4.2 23.8 %copy-start = (bf16[8,128,128]{2,1,0:T(8,128)(2,1)S(1)}, bf16[8,128,128]{2,1,0:T(8,128)(2,1)}, u32[]{:S(2)}) copy-start(bf16[8,128,128]{2,1,0:T(8,128)(2,1)} %constant.34.clone.xbh) | copy-start | bytes 786436
  4.2 23.8 %copy-start.1 = (bf16[8,128,128]{2,1,0:T(8,128)(2,1)S(1)}, bf16[8,128,128]{2,1,0:T(8,128)(2,1)}, u32[]{:S(2)}) copy-start(bf16[8,128,128]{2,1,0:T(8,128)(2,1)} %constant.35.clone.xbl) | copy-start | bytes 786436
  4.2 23.8 %all-to-all-start = ((f32[64,8,128]{2,1,0:T(8,128)}), f32[64,8,128]{2,1,0:T(8,128)S(1)}, u32[]{:S(2)}, u32[]{:S(2)}) async-start(f32[64,8,128]{2,1,0:T(8,128)} %bitcast.17), calls=%async_computation | async-start | bytes 524288 | tf_op jit(solution)/shard_map/all_to_all | solution.py:516
  30.3 4.7 %copy-start.13 = (f32[32,32]{1,0:T(8,128)S(1)}, f32[32,32]{1,0:T(8,128)}, u32[]{:S(2)}) copy-start(f32[32,32]{1,0:T(8,128)} %param.25) | copy-start | bytes 12292
  30.3 4.7 %copy-start.14 = (f32[32]{0:T(128)S(1)}, f32[32]{0:T(128)}, u32[]{:S(2)}) copy-start(f32[32]{0:T(128)} %rock_ref.1) | copy-start | bytes 388
  30.3 4.8 %copy-start.15 = (f32[32]{0:T(128)S(1)}, f32[32]{0:T(128)}, u32[]{:S(2)}) copy-start(f32[32]{0:T(128)} %well_ref.1) | copy-start | bytes 388
  30.3 18.8 %copy-start.2 = (f32[2,128,128]{2,1,0:T(8,128)S(1)}, f32[2,128,128]{2,1,0:T(8,128)}, u32[]{:S(2)}) copy-start(f32[2,128,128]{2,1,0:T(8,128)} %p_hbm.3) | copy-start | bytes 393220
  30.3 18.8 %copy-start.3 = (f32[2,128,128]{2,1,0:T(8,128)S(1)}, f32[2,128,128]{2,1,0:T(8,128)}, u32[]{:S(2)}) copy-start(f32[2,128,128]{2,1,0:T(8,128)} %d_hbm.3) | copy-start | bytes 393220
  30.3 18.8 %copy-start.4 = (f32[1,2,128,128]{3,2,1,0:T(8,128)S(1)}, f32[1,2,128,128]{3,2,1,0:T(8,128)}, u32[]{:S(2)}) copy-start(f32[1,2,128,128]{3,2,1,0:T(8,128)} %param.21) | copy-start | bytes 393220
  30.3 18.8 %copy-start.5 = (bf16[864,256]{1,0:T(8,128)(2,1)S(1)}, bf16[864,256]{1,0:T(8,128)(2,1)}, u32[]{:S(2)}) copy-start(bf16[864,256]{1,0:T(8,128)(2,1)} %constant.38.clone.tab) | copy-start | bytes 1327108
  30.3 18.8 %all-to-all-start.1 = ((f32[64,12,128]{2,1,0:T(8,128)}), f32[64,12,128]{2,1,0:T(8,128)S(1)}, u32[]{:S(2)}, u32[]{:S(2)}) async-start(f32[64,12,128]{2,1,0:T(8,128)} %owners.1), calls=%async_computation.1 | async-start | bytes 1048576 | tf_op jit(solution)/shard_map/all_to_all | solution.py:531
  35.1 0.7 copy-start.16
  49.1 24.1 %copy-start.9 = (bf16[8,128,128]{2,1,0:T(8,128)(2,1)S(1)}, bf16[8,128,128]{2,1,0:T(8,128)(2,1)}, u32[]{:S(2)}) copy-start(bf16[8,128,128]{2,1,0:T(8,128)(2,1)} %constant.40.clone.xih) | copy-start | bytes 786436
  49.1 24.1 %copy-start.10 = (bf16[8,128,128]{2,1,0:T(8,128)(2,1)S(1)}, bf16[8,128,128]{2,1,0:T(8,128)(2,1)}, u32[]{:S(2)}) copy-start(bf16[8,128,128]{2,1,0:T(8,128)(2,1)} %constant.41.clone.xil) | copy-start | bytes 786436
  57.0 16.1 %copy-start.6 = (bf16[768,256]{1,0:T(8,128)(2,1)S(1)}, bf16[768,256]{1,0:T(8,128)(2,1)}, u32[]{:S(2)}) copy-start(bf16[768,256]{1,0:T(8,128)(2,1)} %constant.43.clone.ed) | copy-start | bytes 1179652
  57.0 16.1 %all-to-all-start.2 = ((f32[64,6,128]{2,1,0:T(8,128)}), f32[64,6,128]{2,1,0:T(8,128)S(1)}, u32[]{:S(2)}, u32[]{:S(2)}) async-start(f32[64,6,128]{2,1,0:T(8,128)} %bitcast.9), calls=%async_computation.2 | async-start | bytes 524288 | tf_op jit(solution)/shard_map/all_to_all | solution.py:538
  61.8 17.1 %collective-permute-start = (f32[2,128,128]{2,1,0:T(8,128)S(1)}, f32[2,128,128]{2,1,0:T(8,128)S(1)}, u32[]{:S(2)}, u32[]{:S(2)}) collective-permute-start(f32[2,128,128]{2,1,0:T(8,128)S(1)} %get-tuple-element.8.mine_hbm), channel_id=1, source_target_pairs={{0,64},{64,0},{1,65},{65,1},{2,66},{66,2},{3,67},{67,3},{4,68},{68... | collective-permute-start | bytes 393224 | tf_op jit(solution)/shard_map/ppermute | solution.py:537
  74.8 13.9 %copy-start.8 = (bf16[512,256]{1,0:T(8,128)(2,1)S(1)}, bf16[512,256]{1,0:T(8,128)(2,1)}, u32[]{:S(2)}) copy-start(bf16[512,256]{1,0:T(8,128)(2,1)} %constant.39.clone.tab) | copy-start | bytes 786436
  74.8 13.9 %all-to-all-start.3 = ((f32[128,2,128]{2,1,0:T(2,128)}), f32[128,2,128]{2,1,0:T(2,128)S(1)}, u32[]{:S(2)}, u32[]{:S(2)}) async-start(f32[128,2,128]{2,1,0:T(2,128)} %bitcast.10), calls=%async_computation.3 | async-start | bytes 262144 | tf_op jit(solution)/shard_map/all_to_all | solution.py:554

commit v4 on v3

--- a/solution.py
+++ b/solution.py
@@ -124,7 +124,7 @@
     final[384:512] = field[736:864]
 
     return dict(
-        first=first, xb=halves(xb), xi=halves(xi), field=field, final=final, xp=halves(xp),
+        first=first, across=np.concatenate([h for t in (xi, xb, xp) for h in halves(t)], axis=1), field=field, final=final,
         eb=eb.astype(ml_dtypes.bfloat16), ed=ed.astype(ml_dtypes.bfloat16),
     )
 
@@ -229,7 +229,16 @@
                 out_ref[:, beta, r, :] = out_ref[:, beta, r, :] + block[kind][3 * j + bi]
 
 
-def owners_kernel(beta_ref, r_ref, xbh, xbl, xih, xil, eb, out_ref):
+def owners_kernel(
+    pen_ref, r_ref, across, eb, rock_ref, well_ref, mix_ref, off_ref, out_ref, scal_ref
+):
+    beta = lax.rem(pen_ref[0], BETAS)
+    rock = mix_ref[0:1] * rock_ref[0]
+    well = mix_ref[0:1] * well_ref[0]
+    for i in range(1, CHANNELS):
+        rock = rock + mix_ref[i : i + 1] * rock_ref[i]
+        well = well + mix_ref[i : i + 1] * well_ref[i]
+    scal_ref[0:1], scal_ref[1:2], scal_ref[2:3] = rock, well, off_ref[...]
     raw = [r_ref[:, r, :] for r in range(8)]
     lane = lax.broadcasted_iota(jnp.int32, (OWNERS, LANES), 1)
 
@@ -249,7 +258,7 @@
                     x = take(raw[3 * bi + third], 120, HALF * bi + 8 * third, 8, x)
         planes.append(x)
     fields = [jnp.concatenate(planes[2 * f : 2 * f + 2], axis=0) for f in range(3)]
-    g = left(xbh[0], xbl[0], jnp.concatenate(fields, axis=1))
+    g = left(across[beta, 256:384], across[beta, 384:512], jnp.concatenate(fields, axis=1))
     pre = [
         right_exact(
             jnp.concatenate(
@@ -273,10 +282,12 @@
         for q in (coeff, 0.25 * tangent):
             s = swap(q, real)
             stack.append(jnp.concatenate([q, jnp.where(real, -s, s)], axis=0))
-    o = left(xih[0], xil[0], jnp.concatenate(stack, axis=1))
+    o = left(across[beta, 0:128], across[beta, 128:256], jnp.concatenate(stack, axis=1))
     for plane in range(2):
-        for k in range(6):
-            out_ref[:, plane * 6 + k, :] = o[plane * 64 : plane * 64 + 64, k * LANES : (k + 1) * LANES]
+        piece = [o[plane * 64 : plane * 64 + 64, k * LANES : (k + 1) * LANES] for k in range(6)]
+        for k in range(5):
+            spare = take(piece[5], HALF * k, 96, HALF, piece[k]) if k < CH else piece[k]
+            out_ref[:, plane, k * LANES : (k + 1) * LANES] = spare
 
 
 ROOT = math.sqrt(2.0 / math.pi)
@@ -290,21 +301,26 @@
 
 
 def field_kernel(
-    scal_hbm, r_ref, tab, p_hbm, d_hbm, i_hbm, out_ref, local_ref, scal, p_ref, d_ref, i_ref, z_ref, w0, w1, t0, t1, u0, u1, sems
+    scal_hbm, r_ref, tab, p_ref, d_ref, i_ref,
+    out_ref, local_ref, scal, z_ref, w0, w1, t0, t1, u0, u1, sem,
 ):
-    copies = [
-        pltpu.make_async_copy(src, dst, sems.at[k])
-        for k, (src, dst) in enumerate(((scal_hbm, scal), (p_hbm, p_ref), (d_hbm, d_ref), (i_hbm, i_ref)))
-    ]
-    for copy in copies:
-        copy.start()
+    copy = pltpu.make_async_copy(scal_hbm, scal, sem)
+    copy.start()
     w_refs, t_refs, u_refs = (w0, w1), (t0, t1), (u0, u1)
     lane = lax.broadcasted_iota(jnp.int32, (HALF, LANES), 1)
     low, high = lane < PAIR, (lane >= PAIR) & (lane < 2 * PAIR)
     zero = jnp.zeros((HALF, LANES), F32)
+    row = lax.broadcasted_iota(jnp.int32, (BETAS, LANES), 1)
     local_ref[...] = jnp.zeros_like(local_ref)
-    for copy in copies:
-        copy.wait()
+
+    def piece(kappa, plane, k):
+        if k < 5:
+            return r_ref[kappa, :, plane, k * LANES : (k + 1) * LANES]
+        x = jnp.zeros((BETAS, LANES), F32)
+        for q in range(CH):
+            moved = pltpu.roll(r_ref[kappa, :, plane, q * LANES : (q + 1) * LANES], 32 + HALF * q, 1)
+            x = jnp.where((row >= HALF * q) & (row < HALF * (q + 1)), moved, x)
+        return x
 
     def front(k):
         kappas = [GROUP * k + m for m in range(GROUP)]
@@ -313,9 +329,7 @@
         for field in range(2):
             for plane in range(2):
                 for kappa in kappas:
-                    s = jnp.concatenate(
-                        [r_ref[kappa, :, plane * 6 + bi * 2 + field, :] for bi in range(3)], axis=0
-                    )
+                    s = jnp.concatenate([piece(kappa, plane, bi * 2 + field) for bi in range(3)], axis=0)
                     right_pair = pltpu.roll(s, PAIR, 1)
                     left_pair = pltpu.roll(s, LANES - PAIR, 1)
                     rhs.append(
@@ -374,6 +388,7 @@
 
     steps = KAPPAS // GROUP
     front(0)
+    copy.wait()
     for k in range(steps):
         if k + 1 < steps:
             front(k + 1)
@@ -390,17 +405,19 @@
                 jnp.where(high, pltpu.roll(second[:HALF], PAIR, 1) + second[HALF:], zero),
             )
             for bi in range(3):
-                out_ref[kappa, :, plane * 3 + bi, :] = w[8 * bi : 8 * bi + 8]
+                out_ref[kappa, :, plane, bi * LANES : (bi + 1) * LANES] = w[8 * bi : 8 * bi + 8]
 
 
 GROUP = 1
 
 
-def pull_kernel(beta_ref, r_ref, t_ref, xbh, xbl, xih, xil, ed, out_ref):
+def pull_kernel(pen_ref, r_ref, t_ref, across, ed, out_ref):
+    beta = lax.rem(pen_ref[0], BETAS)
     fields = [
-        jnp.concatenate([r_ref[:, bi, :], r_ref[:, 3 + bi, :]], axis=0) for bi in range(3)
+        jnp.concatenate([r_ref[:, k, bi * LANES : (bi + 1) * LANES] for k in range(2)], axis=0)
+        for bi in range(3)
     ]
-    g = left(xbh[0], xbl[0], jnp.concatenate(fields, axis=1))
+    g = left(across[beta, 256:384], across[beta, 384:512], jnp.concatenate(fields, axis=1))
     real = part_mask((OWNERS, LANES))
     parts = []
     for bi in range(3):
@@ -410,18 +427,12 @@
         v = fr + jnp.where(real, s, -s)
         parts += [t * v, t * swap(v, real)]
     q = right_exact(jnp.concatenate(parts, axis=1), ed[...])
-    h = left(xih[0], xil[0], jnp.concatenate([q[:, :LANES], q[:, LANES:]], axis=0))
+    h = left(across[beta, 512:640], across[beta, 640:768], jnp.concatenate([q[:, :LANES], q[:, LANES:]], axis=0))
     for source in range(2):
         out_ref[GRID * source : GRID * source + GRID] = h
 
 
-def final_kernel(r_ref, tab, mine_hbm, theirs_hbm, out_ref, mine_ref, theirs_ref, sems):
-    copies = [
-        pltpu.make_async_copy(src, dst, sems.at[k])
-        for k, (src, dst) in enumerate(((mine_hbm, mine_ref), (theirs_hbm, theirs_ref)))
-    ]
-    for copy in copies:
-        copy.start()
+def final_kernel(r_ref, tab, mine_ref, theirs_ref, out_ref):
     lane = lax.broadcasted_iota(jnp.int32, (BETAS, LANES), 1)
     rows = [[], []]
     total = []
@@ -443,8 +454,6 @@
     y = dot(tab[384:512, :144], jnp.concatenate([top, top, rest], axis=0))
     top, rest = split(y)
     z = dot(jnp.concatenate([top, rest], axis=1), tab[0:256]) + dot(top, tab[256:384])
-    for copy in copies:
-        copy.wait()
     for plane in range(2):
         out_ref[plane] = z[:, plane * GRID : (plane + 1) * GRID] + (mine_ref[plane] + theirs_ref[plane])
 
@@ -455,30 +464,21 @@
 PARAMS = dict(compiler_params=pltpu.CompilerParams(vmem_limit_bytes=40 * 1024 * 1024))
 
 
-def whole(shape):
-    return pl.BlockSpec(shape, lambda i, beta: (0,) * len(shape))
-
-
-def by_beta(shape):
-    return pl.BlockSpec((1,) + shape, lambda i, beta: (beta[0], 0, 0))
-
-
 def field_call(*operands):
     return pl.pallas_call(
         field_kernel,
         out_shape=[
-            jax.ShapeDtypeStruct((KAPPAS, BETAS, 6, LANES), F32),
+            jax.ShapeDtypeStruct((KAPPAS, BETAS, 2, 3 * LANES), F32),
             jax.ShapeDtypeStruct((2, GRID, GRID), F32),
         ],
-        in_specs=[HBM, VMEM, VMEM, HBM, HBM, HBM],
+        in_specs=[HBM] + [VMEM] * 5,
         out_specs=[VMEM] * 2,
         scratch_shapes=[pltpu.SMEM((3, CHANNELS), F32)]
-        + [pltpu.VMEM((2, GRID, GRID), F32)] * 3
         + [
             pltpu.VMEM((4 * KAPPAS, 2 * GRID, LANES), BF16),
             *[pltpu.VMEM((8 * GROUP * GRID, 2 * GRID), F32)] * 2,
             *[pltpu.VMEM((4 * GROUP * GRID, 2 * GRID), BF16)] * 4,
-            pltpu.SemaphoreType.DMA((4,)),
+            pltpu.SemaphoreType.DMA,
         ],
         name="field",
         **PARAMS,
@@ -490,8 +490,7 @@
         k: tuple(jnp.asarray(x) for x in v) if isinstance(v, tuple) else jnp.asarray(v)
         for k, v in TABLES.items()
     }
-    pen = lax.axis_index("pen")
-    beta = lax.rem(pen, BETAS).astype(jnp.int32).reshape(1)
+    pen = lax.axis_index("pen").astype(jnp.int32).reshape(1)
     inj = injection[0]
 
     send = pl.pallas_call(
@@ -509,56 +508,48 @@
         name="first",
         compiler_params=pltpu.CompilerParams(vmem_limit_bytes=60 * 1024 * 1024),
     )(
-        pen.astype(jnp.int32).reshape(1), lift_rock, lift_well, spectral.transpose(1, 2, 3, 0),
+        pen, lift_rock, lift_well, spectral.transpose(1, 2, 3, 0),
         permeability, direction, inj, tab["first"],
     )
     send = send.reshape(OWNERS, 8, LANES)
     owned = lax.all_to_all(send, "pen", 0, 0, tiled=True)
 
-    square = (2 * OWNERS, GRID)
-    send = pl.pallas_call(
+    send, scal = pl.pallas_call(
         owners_kernel,
-        out_shape=jax.ShapeDtypeStruct((OWNERS, 12, LANES), F32),
-        grid_spec=pltpu.PrefetchScalarGridSpec(
-            num_scalar_prefetch=1,
-            grid=(1,),
-            in_specs=[whole((OWNERS, 8, LANES))] + [by_beta(square)] * 4 + [whole((2 * LANES, 6 * LANES))],
-            out_specs=whole((OWNERS, 12, LANES)),
-        ),
+        out_shape=[
+            jax.ShapeDtypeStruct((OWNERS, 2, 5 * LANES), F32),
+            jax.ShapeDtypeStruct((3, CHANNELS), F32),
+        ],
+        in_specs=[SMEM, VMEM, VMEM, VMEM, SMEM, SMEM, VMEM, VMEM],
+        out_specs=[VMEM] * 2,
         name="owners",
         **PARAMS,
-    )(beta, owned, *tab["xb"], *tab["xi"], tab["eb"])
+    )(
+        pen, owned, tab["across"], tab["eb"],
+        lift_rock, lift_well, pointwise, offsets.reshape(1, CHANNELS),
+    )
     got = lax.all_to_all(send, "pen", 0, 0, tiled=True)
 
-    rock = jnp.sum(pointwise * lift_rock[:, None], axis=0)
-    well = jnp.sum(pointwise * lift_well[:, None], axis=0)
-    scal = jnp.stack([rock, well, offsets])
-    send, local = field_call(scal, got.reshape(KAPPAS, BETAS, 12, LANES), tab["field"], permeability, direction, inj)
+    send, local = field_call(scal, got.reshape(KAPPAS, BETAS, 2, 5 * LANES), tab["field"], permeability, direction, inj)
     theirs = lax.ppermute(local, "src", [(0, 1), (1, 0)])
-    back = lax.all_to_all(send.reshape(OWNERS, 6, LANES), "pen", 0, 0, tiled=True)
+    back = lax.all_to_all(send.reshape(OWNERS, 2, 3 * LANES), "pen", 0, 0, tiled=True)
+    back, theirs = lax.optimization_barrier((back, theirs))
 
     send = pl.pallas_call(
         pull_kernel,
         out_shape=jax.ShapeDtypeStruct((4 * OWNERS, LANES), F32),
-        grid_spec=pltpu.PrefetchScalarGridSpec(
-            num_scalar_prefetch=1,
-            grid=(1,),
-            in_specs=[whole((OWNERS, 6, LANES)), whole((OWNERS, 8, LANES))]
-            + [by_beta(square)] * 4
-            + [whole((6 * LANES, 2 * LANES))],
-            out_specs=whole((4 * OWNERS, LANES)),
-        ),
+        in_specs=[SMEM] + [VMEM] * 4,
+        out_specs=VMEM,
         name="pull",
         **PARAMS,
-    )(beta, back, owned, *tab["xb"], *tab["xp"], tab["ed"])
+    )(pen, back, owned, tab["across"], tab["ed"])
     last = lax.all_to_all(send, ("src", "pen"), 0, 0, tiled=True)
 
     return pl.pallas_call(
         final_kernel,
         out_shape=jax.ShapeDtypeStruct((2, GRID, GRID), F32),
-        in_specs=[VMEM] * 2 + [HBM] * 2,
+        in_specs=[VMEM] * 4,
         out_specs=VMEM,
-        scratch_shapes=[pltpu.VMEM((2, GRID, GRID), F32)] * 2 + [pltpu.SemaphoreType.DMA((2,))],
         name="final",
         **PARAMS,
     )(last, tab["final"], local, theirs)

time: 90.6 us -> 88.4 us (0.976)
  blocking collectives: 0 us -> 55.9 us
  waiting for transfers between devices: 44.9 us -> 9.88 us
  starting transfers between devices: 26.8 us -> 5.57 us
    all_to_all x0 -> x3, blocking collectives: none -> 55.9 us  [the longest x1 23.6 us: shards(): owned = lax.all_to_all(send, 'pen', 0, 0, tiled=True)]
    all_to_all x4 -> x1, waiting for transfers between devices: 44.9 us -> 4.9 us  [shards(): lax.all_to_all(send.reshape(OWNERS, 2, 3 * LANES), 'pen', 0, 0, tiled=True)]
    all_to_all x4 -> x1, starting transfers between devices: 26 us -> 4.76 us  [shards(): lax.all_to_all(send.reshape(OWNERS, 2, 3 * LANES), 'pen', 0, 0, tiled=True)]
    ppermute x1, waiting for transfers between devices: 0.01 us -> 4.97 us  [shards(): theirs = lax.ppermute(local, 'src', [(0, 1), (1, 0)])]
  transfers between devices with their start and end apart: 5 -> 2, of which waited for: 4 -> 2; matrix products, arithmetic and copies ran while one was open for 0% -> 0% of each run, Pallas kernels for 2% -> 0%
where the time goes in v4:
time: 88.4 us; the launch traced here: 88.1 us
  blocking collectives  55.9 us (63%)
  Pallas kernels  16.6 us (19%)
  waiting for transfers between devices  9.88 us (11%)
  starting transfers between devices  5.57 us (6%)
    all_to_all x1, blocking collectives, shards(): owned = lax.all_to_all(send, 'pen', 0, 0, tiled=True)  23.6 us
    all_to_all x1, blocking collectives, shards(): got = lax.all_to_all(send, 'pen', 0, 0, tiled=True)  16.4 us
    all_to_all x1, blocking collectives, shards(): last = lax.all_to_all(send, ('src', 'pen'), 0, 0, tiled=True)  15.8 us
    pallas_call x1, Pallas kernels, field_call(): pl.pallas_call(field_kernel, out_shape=[jax.ShapeDtypeStruct((KAPPAS, BET...  8.3 us
    ppermute x1, waiting for transfers between devices, shards(): theirs = lax.ppermute(local, 'src', [(0, 1), (1, 0)])  4.97 us
    all_to_all x1, waiting for transfers between devices, shards(): lax.all_to_all(send.reshape(OWNERS, 2, 3 * LANES), 'pen', 0, 0, tiled=True)  4.9 us
    all_to_all x1, starting transfers between devices, shards(): lax.all_to_all(send.reshape(OWNERS, 2, 3 * LANES), 'pen', 0, 0, tiled=True)  4.76 us
    pallas_call x1, Pallas kernels, shards(): pl.pallas_call(first_kernel, out_shape=jax.ShapeDtypeStruct((KAPPAS, BETA...  4.16 us
  transfers between devices with their start and end apart: 2, of which 2 were waited for; matrix products, arithmetic and copies ran while one was open for 0% of the time, Pallas kernels for 0%

profile of v4, /device:TPU:1, one launch (start us, length us, event | category | flops | bytes accessed | tf_op | source)
XLA Modules:
  0.0 88.1 jit_solution(204905775130135907)
XLA Ops:
  0.0 0.0 copy-start.9
  0.0 0.0 copy-start.11
  0.0 0.0 copy-start.8
  0.0 4.2 %first.1 = f32[8,8,8,128]{3,2,1,0:T(8,128)} custom-call(s32[1]{0:T(128)} %bitcast.pen_ref, f32[32]{0:T(128)} %rock_ref.3, f32[32]{0:T(128)} %well_ref.3, f32[2,32,32,108]{3,2,1,0:T(8,128)} %bitcast.15, f32[2,128,128]{2,1,0:T(8,128)} %p_ref.1, f32[2,128,128]{2,1,0:T(8,128)} %d_ref.1, f32[2,128,128]{2,1,0:T(8,128)} %bitcast.10, ...), custom_call_target="tpu_custom_call" | custom-call | tf_op jit(solution)/shard_map/first/pallas_call | solution.py:496
  4.2 23.6 %all_to_all.26.r_ref.t_ref = f32[64,8,128]{2,1,0:T(8,128)S(1)} all-to-all(f32[64,8,128]{2,1,0:T(8,128)} %bitcast.16), channel_id=1, replica_groups=mesh['src'=2,'pen'=64] {'pen'}, dimensions={0} | all-to-all | bytes 524288 | tf_op jit(solution)/shard_map/all_to_all | solution.py:515
  27.9 0.0 copy-done
  27.9 0.0 copy-done.5
  27.9 0.0 copy-done.10
  27.9 0.0 copy-done.9
  27.9 2.0 %owners.1 = (f32[64,2,640]{2,1,0:T(2,128)S(1)}, f32[3,32]{1,0:T(4,128)S(1)}) custom-call(s32[1]{0:T(128)} %bitcast.pen_ref, f32[64,8,128]{2,1,0:T(8,128)S(1)} %all_to_all.26.r_ref.t_ref, bf16[8,768,128]{2,1,0:T(8,128)(2,1)S(1)} %copy-done, bf16[256,768]{1,0:T(8,128)(2,1)S(1)} %copy-done.5, f32[32]{0:T(128)S(1)} %copy-done.9, f32[32]{0:T(128)S(1)} %copy-done.10, ...), custom_call_target="tpu_custom_call" | custom-call | tf_op jit(solution)/shard_map/owners/pallas_call | solution.py:517
  29.9 0.0 copy-start.6
  29.9 16.4 %all_to_all.27 = f32[64,2,640]{2,1,0:T(2,128)S(1)} all-to-all(f32[64,2,640]{2,1,0:T(2,128)S(1)} %get-tuple-element.12), channel_id=1, replica_groups=mesh['src'=2,'pen'=64] {'pen'}, dimensions={0} | all-to-all | bytes 655360 | tf_op jit(solution)/shard_map/all_to_all | solution.py:531
  46.4 0.0 copy-done.2
  46.4 8.3 %field.1 = (f32[8,8,2,384]{3,2,1,0:T(2,128)}, f32[2,128,128]{2,1,0:T(8,128)S(1)}) custom-call(f32[3,32]{1,0:T(4,128)S(1)} %get-tuple-element.11.scal_hbm, f32[8,8,2,640]{3,2,1,0:T(2,128)S(1)} %bitcast.9, bf16[864,256]{1,0:T(8,128)(2,1)S(1)} %copy-done.4, f32[2,128,128]{2,1,0:T(8,128)S(1)} %copy-done.1, f32[2,128,128]{2,1,0:T(8,128)S(1)} %copy-done.2, ...), custom_call_target="tpu_custom_call" | custom-call | tf_op jit(solution)/shard_map/field/pallas_call | solution.py:468
  54.7 0.0 copy-start.7
  54.7 4.8 %all-to-all-start.2 = ((f32[64,2,384]{2,1,0:T(2,128)}), f32[64,2,384]{2,1,0:T(2,128)S(1)}, u32[]{:S(2)}, u32[]{:S(2)}) async-start(f32[64,2,384]{2,1,0:T(2,128)} %bitcast.6), calls=%async_computation.2 | async-start | bytes 393216 | tf_op jit(solution)/shard_map/all_to_all | solution.py:535
  59.5 0.8 collective-permute-start
  60.3 5.0 %collective-permute-done.theirs_ref = f32[2,128,128]{2,1,0:T(8,128)S(1)} collective-permute-done((f32[2,128,128]{2,1,0:T(8,128)S(1)}, f32[2,128,128]{2,1,0:T(8,128)S(1)}, u32[]{:S(2)}, u32[]{:S(2)}) %collective-permute-start) | collective-permute-done | bytes 131104 | tf_op jit(solution)/shard_map/ppermute | solution.py:534
  65.3 4.9 %all-to-all-done.2.r_ref = f32[64,2,384]{2,1,0:T(2,128)S(1)} async-done(((f32[64,2,384]{2,1,0:T(2,128)}), f32[64,2,384]{2,1,0:T(2,128)S(1)}, u32[]{:S(2)}, u32[]{:S(2)}) %all-to-all-start.2) | async-done | bytes 196640 | tf_op jit(solution)/shard_map/all_to_all | solution.py:535
  70.2 0.0 copy-done.6
  70.2 1.0 %pull.1 = f32[256,128]{1,0:T(8,128)S(1)} custom-call(s32[1]{0:T(128)} %bitcast.pen_ref, f32[64,2,384]{2,1,0:T(2,128)S(1)} %all-to-all-done.2.r_ref, f32[64,8,128]{2,1,0:T(8,128)S(1)} %all_to_all.26.r_ref.t_ref, bf16[8,768,128]{2,1,0:T(8,128)(2,1)S(1)} %copy-done, bf16[768,256]{1,0:T(8,128)(2,1)S(1)} %copy-done.6), custom_call_target="tpu_custom_call" | custom-call | tf_op jit(solution)/shard_map/pull/pallas_call | solution.py:538
  71.2 15.8 %all_to_all.28 = f32[128,2,128]{2,1,0:T(2,128)S(1)} all-to-all(f32[128,2,128]{2,1,0:T(2,128)S(1)} %bitcast.12), channel_id=1, replica_groups=mesh['src'=2,'pen'=64] {'src','pen'}, dimensions={0} | all-to-all | bytes 262144 | tf_op jit(solution)/shard_map/all_to_all | solution.py:546
  87.0 0.0 copy-done.7
  87.0 1.1 %final.1 = f32[2,128,128]{2,1,0:T(8,128)} custom-call(f32[256,128]{1,0:T(8,128)S(1)} %bitcast.13, bf16[512,256]{1,0:T(8,128)(2,1)S(1)} %copy-done.7, f32[2,128,128]{2,1,0:T(8,128)S(1)} %get-tuple-element.14.mine_ref, f32[2,128,128]{2,1,0:T(8,128)S(1)} %collective-permute-done.theirs_ref), custom_call_target="tpu_custom_call" | custom-call | tf_op jit(solution)/shard_map/final/pallas_call | solution.py:548
  (12 shorter events, 0.0 us)
Async XLA Ops:
  0.0 27.9 %copy-start = (bf16[8,768,128]{2,1,0:T(8,128)(2,1)S(1)}, bf16[8,768,128]{2,1,0:T(8,128)(2,1)}, u32[]{:S(2)}) copy-start(bf16[8,768,128]{2,1,0:T(8,128)(2,1)} %constant.17.clone.across) | copy-start | bytes 4718596
  0.0 27.9 %copy-start.5 = (bf16[256,768]{1,0:T(8,128)(2,1)S(1)}, bf16[256,768]{1,0:T(8,128)(2,1)}, u32[]{:S(2)}) copy-start(bf16[256,768]{1,0:T(8,128)(2,1)} %constant.20.clone.eb) | copy-start | bytes 1179652
  0.0 27.9 %copy-start.10 = (f32[32]{0:T(128)S(1)}, f32[32]{0:T(128)}, u32[]{:S(2)}) copy-start(f32[32]{0:T(128)} %well_ref.3) | copy-start | bytes 388
  0.0 27.9 %copy-start.9 = (f32[32]{0:T(128)S(1)}, f32[32]{0:T(128)}, u32[]{:S(2)}) copy-start(f32[32]{0:T(128)} %rock_ref.3) | copy-start | bytes 388
  0.0 27.9 %copy-start.11 = (f32[32]{0:T(128)S(1)}, f32[32]{0:T(128)}, u32[]{:S(2)}) copy-start(f32[32]{0:T(128)} %param.21) | copy-start | bytes 388
  0.0 27.9 %copy-start.8 = (f32[32,32]{1,0:T(8,128)S(1)}, f32[32,32]{1,0:T(8,128)}, u32[]{:S(2)}) copy-start(f32[32,32]{1,0:T(8,128)} %mix_ref.1) | copy-start | bytes 12292
  27.9 18.5 %copy-start.1 = (f32[2,128,128]{2,1,0:T(8,128)S(1)}, f32[2,128,128]{2,1,0:T(8,128)}, u32[]{:S(2)}) copy-start(f32[2,128,128]{2,1,0:T(8,128)} %p_ref.1) | copy-start | bytes 393220
  27.9 18.5 %copy-start.2 = (f32[2,128,128]{2,1,0:T(8,128)S(1)}, f32[2,128,128]{2,1,0:T(8,128)}, u32[]{:S(2)}) copy-start(f32[2,128,128]{2,1,0:T(8,128)} %d_ref.1) | copy-start | bytes 393220
  27.9 18.5 %copy-start.3 = (f32[1,2,128,128]{3,2,1,0:T(8,128)S(1)}, f32[1,2,128,128]{3,2,1,0:T(8,128)}, u32[]{:S(2)}) copy-start(f32[1,2,128,128]{3,2,1,0:T(8,128)} %param.16) | copy-start | bytes 393220
  27.9 18.5 %copy-start.4 = (bf16[864,256]{1,0:T(8,128)(2,1)S(1)}, bf16[864,256]{1,0:T(8,128)(2,1)}, u32[]{:S(2)}) copy-start(bf16[864,256]{1,0:T(8,128)(2,1)} %constant.18.clone.tab) | copy-start | bytes 1327108
  29.9 40.2 %copy-start.6 = (bf16[768,256]{1,0:T(8,128)(2,1)S(1)}, bf16[768,256]{1,0:T(8,128)(2,1)}, u32[]{:S(2)}) copy-start(bf16[768,256]{1,0:T(8,128)(2,1)} %constant.21.clone.ed) | copy-start | bytes 1179652
  54.7 32.3 %copy-start.7 = (bf16[512,256]{1,0:T(8,128)(2,1)S(1)}, bf16[512,256]{1,0:T(8,128)(2,1)}, u32[]{:S(2)}) copy-start(bf16[512,256]{1,0:T(8,128)(2,1)} %constant.19.clone.tab) | copy-start | bytes 786436
  54.7 15.5 %all-to-all-start.2 = ((f32[64,2,384]{2,1,0:T(2,128)}), f32[64,2,384]{2,1,0:T(2,128)S(1)}, u32[]{:S(2)}, u32[]{:S(2)}) async-start(f32[64,2,384]{2,1,0:T(2,128)} %bitcast.6), calls=%async_computation.2 | async-start | bytes 393216 | tf_op jit(solution)/shard_map/all_to_all | solution.py:535
  59.5 5.8 %collective-permute-start = (f32[2,128,128]{2,1,0:T(8,128)S(1)}, f32[2,128,128]{2,1,0:T(8,128)S(1)}, u32[]{:S(2)}, u32[]{:S(2)}) collective-permute-start(f32[2,128,128]{2,1,0:T(8,128)S(1)} %get-tuple-element.14.mine_ref), channel_id=1, source_target_pairs={{0,64},{64,0},{1,65},{65,1},{2,66},{66,2},{3,67},{67,3},{4,68},{68... | collective-permute-start | bytes 393224 | tf_op jit(solution)/shard_map/ppermute | solution.py:534

commit v5 on v4

--- a/solution.py
+++ b/solution.py
@@ -163,12 +163,12 @@
 
 
 def first_kernel(
-    pen_ref, rock_ref, well_ref, s_hbm, p_hbm, d_hbm, i_hbm, tab_hbm,
-    out_ref, s_ref, p_ref, d_ref, i_ref, tab, t_ref, sems,
+    rock_hbm, well_hbm, s_hbm, p_hbm, d_hbm, i_hbm, tab_hbm,
+    out_ref, rock_ref, well_ref, s_ref, p_ref, d_ref, i_ref, tab, t_ref, sems,
 ):
     pairs = (
         (tab_hbm, tab), (p_hbm, p_ref), (d_hbm, d_ref), (i_hbm, i_ref),
-        (s_hbm, s_ref),
+        (rock_hbm, rock_ref), (well_hbm, well_ref), (s_hbm, s_ref),
     )
     copies = [pltpu.make_async_copy(src, dst, sems.at[k]) for k, (src, dst) in enumerate(pairs)]
     for copy in copies:
@@ -222,7 +222,7 @@
                     moved = pltpu.roll(x, shift, 1) if shift else x
                     block[kind][row] = jnp.where(inside, moved, block[kind][row])
     for j in range(3):
-        beta = lax.rem(3 * pen_ref[0] + j, BETAS)
+        beta = lax.rem(3 * lax.axis_index("pen") + j, BETAS)
         for kind in range(2):
             for bi in range(3):
                 r = 3 * kind + bi
@@ -230,15 +230,15 @@
 
 
 def owners_kernel(
-    pen_ref, r_ref, across, eb, rock_ref, well_ref, mix_ref, off_ref, out_ref, scal_ref
+    r_ref, across, eb, rock_hbm, well_hbm, mix_ref, off_ref, out_ref, scal_ref, rock_ref, well_ref, sems
 ):
-    beta = lax.rem(pen_ref[0], BETAS)
-    rock = mix_ref[0:1] * rock_ref[0]
-    well = mix_ref[0:1] * well_ref[0]
-    for i in range(1, CHANNELS):
-        rock = rock + mix_ref[i : i + 1] * rock_ref[i]
-        well = well + mix_ref[i : i + 1] * well_ref[i]
-    scal_ref[0:1], scal_ref[1:2], scal_ref[2:3] = rock, well, off_ref[...]
+    beta = lax.rem(lax.axis_index("pen"), BETAS)
+    copies = [
+        pltpu.make_async_copy(src, dst, sems.at[k])
+        for k, (src, dst) in enumerate(((rock_hbm, rock_ref), (well_hbm, well_ref)))
+    ]
+    for copy in copies:
+        copy.start()
     raw = [r_ref[:, r, :] for r in range(8)]
     lane = lax.broadcasted_iota(jnp.int32, (OWNERS, LANES), 1)
 
@@ -288,6 +288,14 @@
         for k in range(5):
             spare = take(piece[5], HALF * k, 96, HALF, piece[k]) if k < CH else piece[k]
             out_ref[:, plane, k * LANES : (k + 1) * LANES] = spare
+    for copy in copies:
+        copy.wait()
+    rock = mix_ref[0:1] * rock_ref[0]
+    well = mix_ref[0:1] * well_ref[0]
+    for i in range(1, CHANNELS):
+        rock = rock + mix_ref[i : i + 1] * rock_ref[i]
+        well = well + mix_ref[i : i + 1] * well_ref[i]
+    scal_ref[0:1], scal_ref[1:2], scal_ref[2:3] = rock, well, off_ref[...]
 
 
 ROOT = math.sqrt(2.0 / math.pi)
@@ -411,8 +419,8 @@
 GROUP = 1
 
 
-def pull_kernel(pen_ref, r_ref, t_ref, across, ed, out_ref):
-    beta = lax.rem(pen_ref[0], BETAS)
+def pull_kernel(r_ref, t_ref, across, ed, out_ref):
+    beta = lax.rem(lax.axis_index("pen"), BETAS)
     fields = [
         jnp.concatenate([r_ref[:, k, bi * LANES : (bi + 1) * LANES] for k in range(2)], axis=0)
         for bi in range(3)
@@ -490,25 +498,25 @@
         k: tuple(jnp.asarray(x) for x in v) if isinstance(v, tuple) else jnp.asarray(v)
         for k, v in TABLES.items()
     }
-    pen = lax.axis_index("pen").astype(jnp.int32).reshape(1)
     inj = injection[0]
 
     send = pl.pallas_call(
         first_kernel,
         out_shape=jax.ShapeDtypeStruct((KAPPAS, BETAS, 8, LANES), F32),
-        in_specs=[SMEM] * 3 + [HBM] * 5,
+        in_specs=[HBM] * 7,
         out_specs=VMEM,
         scratch_shapes=[
+            *[pltpu.SMEM((CHANNELS,), F32)] * 2,
             pltpu.VMEM((2, CHANNELS, CHANNELS, spectral.shape[0]), F32),
             *[pltpu.VMEM((2, GRID, GRID), F32)] * 3,
             pltpu.VMEM((320, 2 * LANES), BF16),
             pltpu.VMEM((4, CHANNELS, LANES), F32),
-            pltpu.SemaphoreType.DMA((5,)),
+            pltpu.SemaphoreType.DMA((7,)),
         ],
         name="first",
         compiler_params=pltpu.CompilerParams(vmem_limit_bytes=60 * 1024 * 1024),
     )(
-        pen, lift_rock, lift_well, spectral.transpose(1, 2, 3, 0),
+        lift_rock, lift_well, spectral.transpose(1, 2, 3, 0),
         permeability, direction, inj, tab["first"],
     )
     send = send.reshape(OWNERS, 8, LANES)
@@ -520,12 +528,13 @@
             jax.ShapeDtypeStruct((OWNERS, 2, 5 * LANES), F32),
             jax.ShapeDtypeStruct((3, CHANNELS), F32),
         ],
-        in_specs=[SMEM, VMEM, VMEM, VMEM, SMEM, SMEM, VMEM, VMEM],
+        in_specs=[VMEM, VMEM, VMEM, HBM, HBM, VMEM, VMEM],
         out_specs=[VMEM] * 2,
+        scratch_shapes=[pltpu.SMEM((CHANNELS,), F32)] * 2 + [pltpu.SemaphoreType.DMA((2,))],
         name="owners",
         **PARAMS,
     )(
-        pen, owned, tab["across"], tab["eb"],
+        owned, tab["across"], tab["eb"],
         lift_rock, lift_well, pointwise, offsets.reshape(1, CHANNELS),
     )
     got = lax.all_to_all(send, "pen", 0, 0, tiled=True)
@@ -533,16 +542,15 @@
     send, local = field_call(scal, got.reshape(KAPPAS, BETAS, 2, 5 * LANES), tab["field"], permeability, direction, inj)
     theirs = lax.ppermute(local, "src", [(0, 1), (1, 0)])
     back = lax.all_to_all(send.reshape(OWNERS, 2, 3 * LANES), "pen", 0, 0, tiled=True)
-    back, theirs = lax.optimization_barrier((back, theirs))
 
     send = pl.pallas_call(
         pull_kernel,
         out_shape=jax.ShapeDtypeStruct((4 * OWNERS, LANES), F32),
-        in_specs=[SMEM] + [VMEM] * 4,
+        in_specs=[VMEM] * 4,
         out_specs=VMEM,
         name="pull",
         **PARAMS,
-    )(pen, back, owned, tab["across"], tab["ed"])
+    )(back, owned, tab["across"], tab["ed"])
     last = lax.all_to_all(send, ("src", "pen"), 0, 0, tiled=True)
 
     return pl.pallas_call(

time: 88.4 us -> 86.4 us (0.977)
  blocking collectives: 55.9 us -> 40.1 us
  waiting for transfers between devices: 9.88 us -> 19.6 us
  starting transfers between devices: 5.57 us -> 9.63 us
    all_to_all x1 -> x0, blocking collectives: 15.8 us -> none  [shards(): last = lax.all_to_all(send, ('src', 'pen'), 0, 0, tiled=True)]
    all_to_all x0 -> x1, waiting for transfers between devices: none -> 9.78 us  [shards(): last = lax.all_to_all(send, ('src', 'pen'), 0, 0, tiled=True)]
    ppermute x1, waiting for transfers between devices: 4.97 us -> 0.01 us  [shards(): theirs = lax.ppermute(local, 'src', [(0, 1), (1, 0)])]
    all_to_all x1, waiting for transfers between devices: 4.9 us -> 9.87 us  [shards(): lax.all_to_all(send.reshape(OWNERS, 2, 3 * LANES), 'pen', 0, 0, tiled=True)]
    all_to_all x0 -> x1, starting transfers between devices: none -> 4.06 us  [shards(): last = lax.all_to_all(send, ('src', 'pen'), 0, 0, tiled=True)]
  transfers between devices with their start and end apart: 2 -> 3, of which waited for: 2 -> 2; matrix products, arithmetic and copies ran while one was open for 0% -> 0% of each run, Pallas kernels for 0% -> 2%
where the time goes in v5:
time: 86.4 us; the launch traced here: 86.1 us
  blocking collectives  40.1 us (46%)
  waiting for transfers between devices  19.6 us (23%)
  Pallas kernels  16.5 us (19%)
  starting transfers between devices  9.63 us (11%)
    all_to_all x1, blocking collectives, shards(): owned = lax.all_to_all(send, 'pen', 0, 0, tiled=True)  23.6 us
    all_to_all x1, blocking collectives, shards(): got = lax.all_to_all(send, 'pen', 0, 0, tiled=True)  16.4 us
    all_to_all x1, waiting for transfers between devices, shards(): lax.all_to_all(send.reshape(OWNERS, 2, 3 * LANES), 'pen', 0, 0, tiled=True)  9.87 us
    all_to_all x1, waiting for transfers between devices, shards(): last = lax.all_to_all(send, ('src', 'pen'), 0, 0, tiled=True)  9.78 us
    pallas_call x1, Pallas kernels, field_call(): pl.pallas_call(field_kernel, out_shape=[jax.ShapeDtypeStruct((KAPPAS, BET...  8.33 us
    all_to_all x1, starting transfers between devices, shards(): lax.all_to_all(send.reshape(OWNERS, 2, 3 * LANES), 'pen', 0, 0, tiled=True)  4.74 us
    all_to_all x1, starting transfers between devices, shards(): last = lax.all_to_all(send, ('src', 'pen'), 0, 0, tiled=True)  4.06 us
    pallas_call x1, Pallas kernels, shards(): pl.pallas_call(first_kernel, out_shape=jax.ShapeDtypeStruct((KAPPAS, BETA...  3.53 us
  transfers between devices with their start and end apart: 3, of which 2 were waited for; matrix products, arithmetic and copies ran while one was open for 0% of the time, Pallas kernels for 2%

profile of v5, /device:TPU:1, one launch (start us, length us, event | category | flops | bytes accessed | tf_op | source)
XLA Modules:
  0.0 86.1 jit_solution(6804820456600762401)
XLA Ops:
  0.0 0.0 copy-start.9
  0.0 0.0 copy-start.11
  0.0 0.0 copy-start.8
  0.0 3.5 %first.1 = f32[8,8,8,128]{3,2,1,0:T(8,128)} custom-call(f32[32]{0:T(128)} %rock_hbm.3, f32[32]{0:T(128)} %well_hbm.3, f32[2,32,32,108]{3,2,1,0:T(8,128)} %bitcast.14, f32[2,128,128]{2,1,0:T(8,128)} %p_ref.1, f32[2,128,128]{2,1,0:T(8,128)} %d_ref.1, f32[2,128,128]{2,1,0:T(8,128)} %bitcast.9, bf16[320,256]{1,0:T(8,128)(2,1)} %constant.12.clone.tab_hbm), custom_call_target="tpu_custom_call" | custom-call | tf_op jit(solution)/shard_map/first/pallas_call | solution.py:503
  3.6 23.6 %all_to_all.26.r_ref.t_ref = f32[64,8,128]{2,1,0:T(8,128)S(1)} all-to-all(f32[64,8,128]{2,1,0:T(8,128)} %bitcast.13), channel_id=1, replica_groups=mesh['src'=2,'pen'=64] {'pen'}, dimensions={0} | all-to-all | bytes 524288 | tf_op jit(solution)/shard_map/all_to_all | solution.py:523
  27.2 0.0 copy-done
  27.2 0.0 copy-done.6
  27.3 0.0 copy-done.10
  27.3 1.9 %owners.1 = (f32[64,2,640]{2,1,0:T(2,128)S(1)}, f32[3,32]{1,0:T(4,128)S(1)}) custom-call(f32[64,8,128]{2,1,0:T(8,128)S(1)} %all_to_all.26.r_ref.t_ref, bf16[8,768,128]{2,1,0:T(8,128)(2,1)S(1)} %copy-done, bf16[256,768]{1,0:T(8,128)(2,1)S(1)} %copy-done.6, f32[32]{0:T(128)S(1)} %copy-done.9, f32[32]{0:T(128)S(1)} %copy-done.10, f32[32,32]{1,0:T(8,128)S(1)} %copy-done.8, ...), custom_call_target="tpu_custom_call" | custom-call | tf_op jit(solution)/shard_map/owners/pallas_call | solution.py:525
  29.2 0.0 copy-start.5
  29.2 16.4 %all_to_all.27 = f32[64,2,640]{2,1,0:T(2,128)S(1)} all-to-all(f32[64,2,640]{2,1,0:T(2,128)S(1)} %get-tuple-element.10), channel_id=1, replica_groups=mesh['src'=2,'pen'=64] {'pen'}, dimensions={0} | all-to-all | bytes 655360 | tf_op jit(solution)/shard_map/all_to_all | solution.py:540
  45.7 0.0 copy-done.2
  45.7 8.3 %field.1 = (f32[8,8,2,384]{3,2,1,0:T(2,128)}, f32[2,128,128]{2,1,0:T(8,128)S(1)}) custom-call(f32[3,32]{1,0:T(4,128)S(1)} %get-tuple-element.9.scal_hbm, f32[8,8,2,640]{3,2,1,0:T(2,128)S(1)} %bitcast.8, bf16[864,256]{1,0:T(8,128)(2,1)S(1)} %copy-done.4, f32[2,128,128]{2,1,0:T(8,128)S(1)} %copy-done.1, f32[2,128,128]{2,1,0:T(8,128)S(1)} %copy-done.2, ...), custom_call_target="tpu_custom_call" | custom-call | tf_op jit(solution)/shard_map/field/pallas_call | solution.py:476
  54.0 0.0 copy-start.7
  54.0 4.7 %all-to-all-start.2 = ((f32[64,2,384]{2,1,0:T(2,128)}), f32[64,2,384]{2,1,0:T(2,128)S(1)}, u32[]{:S(2)}, u32[]{:S(2)}) async-start(f32[64,2,384]{2,1,0:T(2,128)} %bitcast.5), calls=%async_computation.2 | async-start | bytes 393216 | tf_op jit(solution)/shard_map/all_to_all | solution.py:544
  58.8 0.8 collective-permute-start
  59.6 9.9 %all-to-all-done.2.r_ref = f32[64,2,384]{2,1,0:T(2,128)S(1)} async-done(((f32[64,2,384]{2,1,0:T(2,128)}), f32[64,2,384]{2,1,0:T(2,128)S(1)}, u32[]{:S(2)}, u32[]{:S(2)}) %all-to-all-start.2) | async-done | bytes 196640 | tf_op jit(solution)/shard_map/all_to_all | solution.py:544
  69.5 0.0 copy-done.5
  69.5 1.7 %pull.1 = f32[256,128]{1,0:T(8,128)} custom-call(f32[64,2,384]{2,1,0:T(2,128)S(1)} %all-to-all-done.2.r_ref, f32[64,8,128]{2,1,0:T(8,128)S(1)} %all_to_all.26.r_ref.t_ref, bf16[8,768,128]{2,1,0:T(8,128)(2,1)S(1)} %copy-done, bf16[768,256]{1,0:T(8,128)(2,1)S(1)} %copy-done.5), custom_call_target="tpu_custom_call" | custom-call | tf_op jit(solution)/shard_map/pull/pallas_call | solution.py:546
  71.2 4.1 %all-to-all-start.3 = ((f32[128,2,128]{2,1,0:T(2,128)}), f32[128,2,128]{2,1,0:T(2,128)S(1)}, u32[]{:S(2)}, u32[]{:S(2)}) async-start(f32[128,2,128]{2,1,0:T(2,128)} %bitcast.6), calls=%async_computation.3 | async-start | bytes 262144 | tf_op jit(solution)/shard_map/all_to_all | solution.py:554
  75.3 0.0 collective-permute-done.theirs_ref
  75.3 9.8 %all-to-all-done.3 = f32[128,2,128]{2,1,0:T(2,128)S(1)} async-done(((f32[128,2,128]{2,1,0:T(2,128)}), f32[128,2,128]{2,1,0:T(2,128)S(1)}, u32[]{:S(2)}, u32[]{:S(2)}) %all-to-all-start.3) | async-done | bytes 131104 | tf_op jit(solution)/shard_map/all_to_all | solution.py:554
  85.0 0.0 copy-done.7
  85.0 1.1 %final.1 = f32[2,128,128]{2,1,0:T(8,128)} custom-call(f32[256,128]{1,0:T(8,128)S(1)} %bitcast.11, bf16[512,256]{1,0:T(8,128)(2,1)S(1)} %copy-done.7, f32[2,128,128]{2,1,0:T(8,128)S(1)} %get-tuple-element.12.mine_ref, f32[2,128,128]{2,1,0:T(8,128)S(1)} %collective-permute-done.theirs_ref), custom_call_target="tpu_custom_call" | custom-call | tf_op jit(solution)/shard_map/final/pallas_call | solution.py:556
  (13 shorter events, 0.0 us)
Async XLA Ops:
  0.0 27.2 %copy-start = (bf16[8,768,128]{2,1,0:T(8,128)(2,1)S(1)}, bf16[8,768,128]{2,1,0:T(8,128)(2,1)}, u32[]{:S(2)}) copy-start(bf16[8,768,128]{2,1,0:T(8,128)(2,1)} %constant.13.clone.across) | copy-start | bytes 4718596
  0.0 27.2 %copy-start.6 = (bf16[256,768]{1,0:T(8,128)(2,1)S(1)}, bf16[256,768]{1,0:T(8,128)(2,1)}, u32[]{:S(2)}) copy-start(bf16[256,768]{1,0:T(8,128)(2,1)} %constant.16.clone.eb) | copy-start | bytes 1179652
  0.0 27.3 %copy-start.10 = (f32[32]{0:T(128)S(1)}, f32[32]{0:T(128)}, u32[]{:S(2)}) copy-start(f32[32]{0:T(128)} %well_hbm.3) | copy-start | bytes 388
  0.0 27.3 %copy-start.9 = (f32[32]{0:T(128)S(1)}, f32[32]{0:T(128)}, u32[]{:S(2)}) copy-start(f32[32]{0:T(128)} %rock_hbm.3) | copy-start | bytes 388
  0.0 27.3 %copy-start.11 = (f32[32]{0:T(128)S(1)}, f32[32]{0:T(128)}, u32[]{:S(2)}) copy-start(f32[32]{0:T(128)} %param.21) | copy-start | bytes 388
  0.0 27.3 %copy-start.8 = (f32[32,32]{1,0:T(8,128)S(1)}, f32[32,32]{1,0:T(8,128)}, u32[]{:S(2)}) copy-start(f32[32,32]{1,0:T(8,128)} %mix_ref.1) | copy-start | bytes 12292
  27.2 18.4 %copy-start.1 = (f32[2,128,128]{2,1,0:T(8,128)S(1)}, f32[2,128,128]{2,1,0:T(8,128)}, u32[]{:S(2)}) copy-start(f32[2,128,128]{2,1,0:T(8,128)} %p_ref.1) | copy-start | bytes 393220
  27.2 18.4 %copy-start.2 = (f32[2,128,128]{2,1,0:T(8,128)S(1)}, f32[2,128,128]{2,1,0:T(8,128)}, u32[]{:S(2)}) copy-start(f32[2,128,128]{2,1,0:T(8,128)} %d_ref.1) | copy-start | bytes 393220
  27.2 18.4 %copy-start.3 = (f32[1,2,128,128]{3,2,1,0:T(8,128)S(1)}, f32[1,2,128,128]{3,2,1,0:T(8,128)}, u32[]{:S(2)}) copy-start(f32[1,2,128,128]{3,2,1,0:T(8,128)} %param.16) | copy-start | bytes 393220
  27.2 18.4 %copy-start.4 = (bf16[864,256]{1,0:T(8,128)(2,1)S(1)}, bf16[864,256]{1,0:T(8,128)(2,1)}, u32[]{:S(2)}) copy-start(bf16[864,256]{1,0:T(8,128)(2,1)} %constant.14.clone.tab) | copy-start | bytes 1327108
  29.2 40.3 %copy-start.5 = (bf16[768,256]{1,0:T(8,128)(2,1)S(1)}, bf16[768,256]{1,0:T(8,128)(2,1)}, u32[]{:S(2)}) copy-start(bf16[768,256]{1,0:T(8,128)(2,1)} %constant.17.clone.ed) | copy-start | bytes 1179652
  54.0 31.0 %copy-start.7 = (bf16[512,256]{1,0:T(8,128)(2,1)S(1)}, bf16[512,256]{1,0:T(8,128)(2,1)}, u32[]{:S(2)}) copy-start(bf16[512,256]{1,0:T(8,128)(2,1)} %constant.15.clone.tab) | copy-start | bytes 786436
  54.0 15.4 %all-to-all-start.2 = ((f32[64,2,384]{2,1,0:T(2,128)}), f32[64,2,384]{2,1,0:T(2,128)S(1)}, u32[]{:S(2)}, u32[]{:S(2)}) async-start(f32[64,2,384]{2,1,0:T(2,128)} %bitcast.5), calls=%async_computation.2 | async-start | bytes 393216 | tf_op jit(solution)/shard_map/all_to_all | solution.py:544
  58.8 16.5 %collective-permute-start = (f32[2,128,128]{2,1,0:T(8,128)S(1)}, f32[2,128,128]{2,1,0:T(8,128)S(1)}, u32[]{:S(2)}, u32[]{:S(2)}) collective-permute-start(f32[2,128,128]{2,1,0:T(8,128)S(1)} %get-tuple-element.12.mine_ref), channel_id=1, source_target_pairs={{0,64},{64,0},{1,65},{65,1},{2,66},{66,2},{3,67},{67,3},{4,68},{68... | collective-permute-start | bytes 393224 | tf_op jit(solution)/shard_map/ppermute | solution.py:543
  71.2 13.9 %all-to-all-start.3 = ((f32[128,2,128]{2,1,0:T(2,128)}), f32[128,2,128]{2,1,0:T(2,128)S(1)}, u32[]{:S(2)}, u32[]{:S(2)}) async-start(f32[128,2,128]{2,1,0:T(2,128)} %bitcast.6), calls=%async_computation.3 | async-start | bytes 262144 | tf_op jit(solution)/shard_map/all_to_all | solution.py:554

commit v6 on v5

--- a/solution.py
+++ b/solution.py
@@ -259,15 +259,15 @@
         planes.append(x)
     fields = [jnp.concatenate(planes[2 * f : 2 * f + 2], axis=0) for f in range(3)]
     g = left(across[beta, 256:384], across[beta, 384:512], jnp.concatenate(fields, axis=1))
-    pre = [
-        right_exact(
-            jnp.concatenate(
-                [g[:64, f * LANES : (f + 1) * LANES], g[64:, f * LANES : (f + 1) * LANES]], axis=1
-            ),
-            eb[...],
-        )
-        for f in range(3)
-    ]
+    wide = jnp.concatenate(
+        [
+            jnp.concatenate([g[k : k + 64, f * LANES : (f + 1) * LANES] for k in (0, 64)], axis=1)
+            for f in range(3)
+        ],
+        axis=0,
+    )
+    wide = right_exact(wide, eb[...])
+    pre = [wide[OWNERS * f : OWNERS * (f + 1)] for f in range(3)]
     real = part_mask((OWNERS, LANES))
     stack = []
     for bi in range(3):
@@ -540,7 +540,6 @@
     got = lax.all_to_all(send, "pen", 0, 0, tiled=True)
 
     send, local = field_call(scal, got.reshape(KAPPAS, BETAS, 2, 5 * LANES), tab["field"], permeability, direction, inj)
-    theirs = lax.ppermute(local, "src", [(0, 1), (1, 0)])
     back = lax.all_to_all(send.reshape(OWNERS, 2, 3 * LANES), "pen", 0, 0, tiled=True)
 
     send = pl.pallas_call(
@@ -551,7 +550,9 @@
         name="pull",
         **PARAMS,
     )(back, owned, tab["across"], tab["ed"])
+    send, held = lax.optimization_barrier((send, local))
     last = lax.all_to_all(send, ("src", "pen"), 0, 0, tiled=True)
+    theirs = lax.ppermute(held, "src", [(0, 1), (1, 0)])
 
     return pl.pallas_call(
         final_kernel,

time: 86.4 us -> 85.7 us (level)
  blocking collectives: 40.1 us -> 69.3 us
  waiting for transfers between devices: 19.6 us -> 0.01 us
  starting transfers between devices: 9.63 us -> 0.81 us
  Pallas kernels: 16.5 us -> 15.1 us
    all_to_all x0 -> x2, blocking collectives: none -> 29.2 us  [the longest x1 15.2 us: shards(): lax.all_to_all(send.reshape(OWNERS, 2, 3 * LANES), 'pen', 0, 0, tiled=True)]
    all_to_all x2 -> x0, waiting for transfers between devices: 19.6 us -> none  [the longest x1 9.87 us: shards(): lax.all_to_all(send.reshape(OWNERS, 2, 3 * LANES), 'pen', 0, 0, tiled=True)]
    all_to_all x2 -> x0, starting transfers between devices: 8.8 us -> none  [the longest x1 4.74 us: shards(): lax.all_to_all(send.reshape(OWNERS, 2, 3 * LANES), 'pen', 0, 0, tiled=True)]
  transfers between devices with their start and end apart: 3 -> 1, of which waited for: 2 -> 0; matrix products, arithmetic and copies ran while one was open for 0% -> 0% of each run, Pallas kernels for 2% -> 0%
where the time goes in v6:
time: 85.7 us; the launch traced here: 85.4 us
  blocking collectives  69.3 us (81%)
  Pallas kernels  15.1 us (18%)
    all_to_all x1, blocking collectives, shards(): owned = lax.all_to_all(send, 'pen', 0, 0, tiled=True)  23.6 us
    all_to_all x1, blocking collectives, shards(): got = lax.all_to_all(send, 'pen', 0, 0, tiled=True)  16.4 us
    all_to_all x1, blocking collectives, shards(): lax.all_to_all(send.reshape(OWNERS, 2, 3 * LANES), 'pen', 0, 0, tiled=True)  15.2 us
    all_to_all x1, blocking collectives, shards(): last = lax.all_to_all(send, ('src', 'pen'), 0, 0, tiled=True)  14 us
    pallas_call x1, Pallas kernels, field_call(): pl.pallas_call(field_kernel, out_shape=[jax.ShapeDtypeStruct((KAPPAS, BET...  7.55 us
    pallas_call x1, Pallas kernels, shards(): pl.pallas_call(first_kernel, out_shape=jax.ShapeDtypeStruct((KAPPAS, BETA...  3.53 us
    pallas_call x1, Pallas kernels, shards(): pl.pallas_call(owners_kernel, out_shape=[jax.ShapeDtypeStruct((OWNERS, 2,...  1.92 us
  transfers between devices with their start and end apart: 1, of which 0 were waited for; matrix products, arithmetic and copies ran while one was open for 0% of the time, Pallas kernels for 0%

profile of v6, /device:TPU:1, one launch (start us, length us, event | category | flops | bytes accessed | tf_op | source)
XLA Modules:
  0.0 85.4 jit_solution(5764952068322920284)
XLA Ops:
  0.0 0.0 copy-start.9
  0.0 0.0 copy-start.11
  0.0 0.0 copy-start.8
  0.0 3.5 %first.1 = f32[8,8,8,128]{3,2,1,0:T(8,128)} custom-call(f32[32]{0:T(128)} %rock_hbm.3, f32[32]{0:T(128)} %well_hbm.3, f32[2,32,32,108]{3,2,1,0:T(8,128)} %bitcast.16, f32[2,128,128]{2,1,0:T(8,128)} %p_ref.1, f32[2,128,128]{2,1,0:T(8,128)} %d_ref.1, f32[2,128,128]{2,1,0:T(8,128)} %bitcast.9, bf16[320,256]{1,0:T(8,128)(2,1)} %constant.12.clone.tab_hbm), custom_call_target="tpu_custom_call" | custom-call | tf_op jit(solution)/shard_map/first/pallas_call | solution.py:503
  3.6 23.6 %all_to_all.26.r_ref.t_ref = f32[64,8,128]{2,1,0:T(8,128)S(1)} all-to-all(f32[64,8,128]{2,1,0:T(8,128)} %bitcast.15), channel_id=1, replica_groups=mesh['src'=2,'pen'=64] {'pen'}, dimensions={0} | all-to-all | bytes 524288 | tf_op jit(solution)/shard_map/all_to_all | solution.py:523
  27.2 0.0 copy-done
  27.2 0.0 copy-done.6
  27.3 0.0 copy-done.10
  27.3 0.0 copy-done.9
  27.3 1.9 %owners.1 = (f32[64,2,640]{2,1,0:T(2,128)S(1)}, f32[3,32]{1,0:T(4,128)S(1)}) custom-call(f32[64,8,128]{2,1,0:T(8,128)S(1)} %all_to_all.26.r_ref.t_ref, bf16[8,768,128]{2,1,0:T(8,128)(2,1)S(1)} %copy-done, bf16[256,768]{1,0:T(8,128)(2,1)S(1)} %copy-done.6, f32[32]{0:T(128)S(1)} %copy-done.9, f32[32]{0:T(128)S(1)} %copy-done.10, f32[32,32]{1,0:T(8,128)S(1)} %copy-done.8, ...), custom_call_target="tpu_custom_call" | custom-call | tf_op jit(solution)/shard_map/owners/pallas_call | solution.py:525
  29.2 0.0 copy-start.5
  29.2 16.4 %all_to_all.27 = f32[64,2,640]{2,1,0:T(2,128)S(1)} all-to-all(f32[64,2,640]{2,1,0:T(2,128)S(1)} %get-tuple-element.12), channel_id=1, replica_groups=mesh['src'=2,'pen'=64] {'pen'}, dimensions={0} | all-to-all | bytes 655360 | tf_op jit(solution)/shard_map/all_to_all | solution.py:540
  45.7 0.0 copy-done.3
  45.7 0.0 copy-done.4
  45.7 7.6 %field.1 = (f32[8,8,2,384]{3,2,1,0:T(2,128)S(1)}, f32[2,128,128]{2,1,0:T(8,128)S(1)}) custom-call(f32[3,32]{1,0:T(4,128)S(1)} %get-tuple-element.11.scal_hbm, f32[8,8,2,640]{3,2,1,0:T(2,128)S(1)} %bitcast.8, bf16[864,256]{1,0:T(8,128)(2,1)S(1)} %copy-done.4, f32[2,128,128]{2,1,0:T(8,128)S(1)} %copy-done.1, f32[2,128,128]{2,1,0:T(8,128)S(1)} %copy-done.2, ...), custom_call_target="tpu_custom_call" | custom-call | tf_op jit(solution)/shard_map/field/pallas_call | solution.py:476
  53.2 0.0 copy-start.7
  53.3 15.2 %all_to_all.28.r_ref = f32[64,2,384]{2,1,0:T(2,128)S(1)} all-to-all(f32[64,2,384]{2,1,0:T(2,128)S(1)} %bitcast.13), channel_id=1, replica_groups=mesh['src'=2,'pen'=64] {'pen'}, dimensions={0} | all-to-all | bytes 393216 | tf_op jit(solution)/shard_map/all_to_all | solution.py:543
  68.5 0.0 copy-done.5
  68.5 1.0 %pull.1 = f32[256,128]{1,0:T(8,128)S(1)} custom-call(f32[64,2,384]{2,1,0:T(2,128)S(1)} %all_to_all.28.r_ref, f32[64,8,128]{2,1,0:T(8,128)S(1)} %all_to_all.26.r_ref.t_ref, bf16[8,768,128]{2,1,0:T(8,128)(2,1)S(1)} %copy-done, bf16[768,256]{1,0:T(8,128)(2,1)S(1)} %copy-done.5), custom_call_target="tpu_custom_call" | custom-call | tf_op jit(solution)/shard_map/pull/pallas_call | solution.py:545
  69.5 0.8 collective-permute-start
  70.4 14.0 %all_to_all.29 = f32[128,2,128]{2,1,0:T(2,128)S(1)} all-to-all(f32[128,2,128]{2,1,0:T(2,128)S(1)} %bitcast.11), channel_id=1, replica_groups=mesh['src'=2,'pen'=64] {'src','pen'}, dimensions={0} | all-to-all | bytes 262144 | tf_op jit(solution)/shard_map/all_to_all | solution.py:554
  84.4 0.0 collective-permute-done.theirs_ref
  84.4 0.0 copy-done.7
  84.4 1.1 %final.1 = f32[2,128,128]{2,1,0:T(8,128)} custom-call(f32[256,128]{1,0:T(8,128)S(1)} %bitcast.12, bf16[512,256]{1,0:T(8,128)(2,1)S(1)} %copy-done.7, f32[2,128,128]{2,1,0:T(8,128)S(1)} %get-tuple-element.16.mine_ref, f32[2,128,128]{2,1,0:T(8,128)S(1)} %collective-permute-done.theirs_ref), custom_call_target="tpu_custom_call" | custom-call | tf_op jit(solution)/shard_map/final/pallas_call | solution.py:557
  (11 shorter events, 0.0 us)
Async XLA Ops:
  0.0 27.2 %copy-start = (bf16[8,768,128]{2,1,0:T(8,128)(2,1)S(1)}, bf16[8,768,128]{2,1,0:T(8,128)(2,1)}, u32[]{:S(2)}) copy-start(bf16[8,768,128]{2,1,0:T(8,128)(2,1)} %constant.13.clone.across) | copy-start | bytes 4718596
  0.0 27.2 %copy-start.6 = (bf16[256,768]{1,0:T(8,128)(2,1)S(1)}, bf16[256,768]{1,0:T(8,128)(2,1)}, u32[]{:S(2)}) copy-start(bf16[256,768]{1,0:T(8,128)(2,1)} %constant.16.clone.eb) | copy-start | bytes 1179652
  0.0 27.2 %copy-start.10 = (f32[32]{0:T(128)S(1)}, f32[32]{0:T(128)}, u32[]{:S(2)}) copy-start(f32[32]{0:T(128)} %well_hbm.3) | copy-start | bytes 388
  0.0 27.3 %copy-start.9 = (f32[32]{0:T(128)S(1)}, f32[32]{0:T(128)}, u32[]{:S(2)}) copy-start(f32[32]{0:T(128)} %rock_hbm.3) | copy-start | bytes 388
  0.0 27.3 %copy-start.11 = (f32[32]{0:T(128)S(1)}, f32[32]{0:T(128)}, u32[]{:S(2)}) copy-start(f32[32]{0:T(128)} %param.21) | copy-start | bytes 388
  0.0 27.3 %copy-start.8 = (f32[32,32]{1,0:T(8,128)S(1)}, f32[32,32]{1,0:T(8,128)}, u32[]{:S(2)}) copy-start(f32[32,32]{1,0:T(8,128)} %mix_ref.1) | copy-start | bytes 12292
  27.2 18.4 %copy-start.1 = (f32[2,128,128]{2,1,0:T(8,128)S(1)}, f32[2,128,128]{2,1,0:T(8,128)}, u32[]{:S(2)}) copy-start(f32[2,128,128]{2,1,0:T(8,128)} %p_ref.1) | copy-start | bytes 393220
  27.2 18.4 %copy-start.2 = (f32[2,128,128]{2,1,0:T(8,128)S(1)}, f32[2,128,128]{2,1,0:T(8,128)}, u32[]{:S(2)}) copy-start(f32[2,128,128]{2,1,0:T(8,128)} %d_ref.1) | copy-start | bytes 393220
  27.2 18.4 %copy-start.3 = (f32[1,2,128,128]{3,2,1,0:T(8,128)S(1)}, f32[1,2,128,128]{3,2,1,0:T(8,128)}, u32[]{:S(2)}) copy-start(f32[1,2,128,128]{3,2,1,0:T(8,128)} %param.16) | copy-start | bytes 393220
  27.2 18.4 %copy-start.4 = (bf16[864,256]{1,0:T(8,128)(2,1)S(1)}, bf16[864,256]{1,0:T(8,128)(2,1)}, u32[]{:S(2)}) copy-start(bf16[864,256]{1,0:T(8,128)(2,1)} %constant.14.clone.tab) | copy-start | bytes 1327108
  29.2 39.3 %copy-start.5 = (bf16[768,256]{1,0:T(8,128)(2,1)S(1)}, bf16[768,256]{1,0:T(8,128)(2,1)}, u32[]{:S(2)}) copy-start(bf16[768,256]{1,0:T(8,128)(2,1)} %constant.17.clone.ed) | copy-start | bytes 1179652
  53.2 31.1 %copy-start.7 = (bf16[512,256]{1,0:T(8,128)(2,1)S(1)}, bf16[512,256]{1,0:T(8,128)(2,1)}, u32[]{:S(2)}) copy-start(bf16[512,256]{1,0:T(8,128)(2,1)} %constant.15.clone.tab) | copy-start | bytes 786436
  69.5 14.8 %collective-permute-start = (f32[2,128,128]{2,1,0:T(8,128)S(1)}, f32[2,128,128]{2,1,0:T(8,128)S(1)}, u32[]{:S(2)}, u32[]{:S(2)}) collective-permute-start(f32[2,128,128]{2,1,0:T(8,128)S(1)} %get-tuple-element.16.mine_ref), channel_id=1, source_target_pairs={{0,64},{64,0},{1,65},{65,1},{2,66},{66,2},{3,67},{67,3},{4,68},{68... | collective-permute-start | bytes 393224 | tf_op jit(solution)/shard_map/ppermute | solution.py:555

commit v7 on v6

--- a/solution.py
+++ b/solution.py
@@ -394,15 +394,7 @@
                     z_ref[4 * kappa + 2 * plane + pair, GRID:] = rest[at : at + GRID]
                     at += GRID
 
-    steps = KAPPAS // GROUP
-    front(0)
-    copy.wait()
-    for k in range(steps):
-        if k + 1 < steps:
-            front(k + 1)
-        back(k)
-
-    for kappa in range(KAPPAS):
+    def finish(kappa):
         v = dot(tab[640:736], jnp.concatenate([z_ref[4 * kappa + k] for k in range(4)], axis=1))
         v = v[:48] + v[48:]
         for plane in range(2):
@@ -414,6 +406,17 @@
             )
             for bi in range(3):
                 out_ref[kappa, :, plane, bi * LANES : (bi + 1) * LANES] = w[8 * bi : 8 * bi + 8]
+
+    steps = KAPPAS // GROUP
+    front(0)
+    copy.wait()
+    for k in range(steps):
+        if k + 1 < steps:
+            front(k + 1)
+        back(k)
+        if k > 0:
+            finish(k - 1)
+    finish(steps - 1)
 
 
 GROUP = 1

time: 85.7 us -> 85.7 us (level)
  no operation moved by 1% of the time
where the time goes in v7:
time: 85.7 us; the launch traced here: 85.4 us
  blocking collectives  69.3 us (81%)
  Pallas kernels  15.1 us (18%)
    all_to_all x1, blocking collectives, shards(): owned = lax.all_to_all(send, 'pen', 0, 0, tiled=True)  23.6 us
    all_to_all x1, blocking collectives, shards(): got = lax.all_to_all(send, 'pen', 0, 0, tiled=True)  16.4 us
    all_to_all x1, blocking collectives, shards(): lax.all_to_all(send.reshape(OWNERS, 2, 3 * LANES), 'pen', 0, 0, tiled=True)  15.2 us
    all_to_all x1, blocking collectives, shards(): last = lax.all_to_all(send, ('src', 'pen'), 0, 0, tiled=True)  14 us
    pallas_call x1, Pallas kernels, field_call(): pl.pallas_call(field_kernel, out_shape=[jax.ShapeDtypeStruct((KAPPAS, BET...  7.56 us
    pallas_call x1, Pallas kernels, shards(): pl.pallas_call(first_kernel, out_shape=jax.ShapeDtypeStruct((KAPPAS, BETA...  3.53 us
    pallas_call x1, Pallas kernels, shards(): pl.pallas_call(owners_kernel, out_shape=[jax.ShapeDtypeStruct((OWNERS, 2,...  1.92 us
  transfers between devices with their start and end apart: 1, of which 0 were waited for; matrix products, arithmetic and copies ran while one was open for 0% of the time, Pallas kernels for 0%

profile of v7, /device:TPU:1, one launch (start us, length us, event | category | flops | bytes accessed | tf_op | source)
XLA Modules:
  0.0 85.4 jit_solution(15264925538752271168)
XLA Ops:
  0.0 0.0 copy-start.9
  0.0 0.0 copy-start.11
  0.0 0.0 copy-start.8
  0.0 3.5 %first.1 = f32[8,8,8,128]{3,2,1,0:T(8,128)} custom-call(f32[32]{0:T(128)} %rock_hbm.3, f32[32]{0:T(128)} %well_hbm.3, f32[2,32,32,108]{3,2,1,0:T(8,128)} %bitcast.16, f32[2,128,128]{2,1,0:T(8,128)} %p_ref.1, f32[2,128,128]{2,1,0:T(8,128)} %d_ref.1, f32[2,128,128]{2,1,0:T(8,128)} %bitcast.9, bf16[320,256]{1,0:T(8,128)(2,1)} %constant.12.clone.tab_hbm), custom_call_target="tpu_custom_call" | custom-call | tf_op jit(solution)/shard_map/first/pallas_call | solution.py:506
  3.6 23.6 %all_to_all.26.r_ref.t_ref = f32[64,8,128]{2,1,0:T(8,128)S(1)} all-to-all(f32[64,8,128]{2,1,0:T(8,128)} %bitcast.15), channel_id=1, replica_groups=mesh['src'=2,'pen'=64] {'pen'}, dimensions={0} | all-to-all | bytes 524288 | tf_op jit(solution)/shard_map/all_to_all | solution.py:526
  27.2 0.0 copy-done
  27.2 0.0 copy-done.6
  27.3 0.0 copy-done.10
  27.3 0.0 copy-done.9
  27.3 0.0 copy-done.11
  27.3 1.9 %owners.1 = (f32[64,2,640]{2,1,0:T(2,128)S(1)}, f32[3,32]{1,0:T(4,128)S(1)}) custom-call(f32[64,8,128]{2,1,0:T(8,128)S(1)} %all_to_all.26.r_ref.t_ref, bf16[8,768,128]{2,1,0:T(8,128)(2,1)S(1)} %copy-done, bf16[256,768]{1,0:T(8,128)(2,1)S(1)} %copy-done.6, f32[32]{0:T(128)S(1)} %copy-done.9, f32[32]{0:T(128)S(1)} %copy-done.10, f32[32,32]{1,0:T(8,128)S(1)} %copy-done.8, ...), custom_call_target="tpu_custom_call" | custom-call | tf_op jit(solution)/shard_map/owners/pallas_call | solution.py:528
  29.2 0.0 copy-start.5
  29.2 16.4 %all_to_all.27 = f32[64,2,640]{2,1,0:T(2,128)S(1)} all-to-all(f32[64,2,640]{2,1,0:T(2,128)S(1)} %get-tuple-element.12), channel_id=1, replica_groups=mesh['src'=2,'pen'=64] {'pen'}, dimensions={0} | all-to-all | bytes 655360 | tf_op jit(solution)/shard_map/all_to_all | solution.py:543
  45.7 0.0 copy-done.3
  45.7 0.0 copy-done.4
  45.7 7.6 %field.1 = (f32[8,8,2,384]{3,2,1,0:T(2,128)S(1)}, f32[2,128,128]{2,1,0:T(8,128)S(1)}) custom-call(f32[3,32]{1,0:T(4,128)S(1)} %get-tuple-element.11.scal_hbm, f32[8,8,2,640]{3,2,1,0:T(2,128)S(1)} %bitcast.8, bf16[864,256]{1,0:T(8,128)(2,1)S(1)} %copy-done.4, f32[2,128,128]{2,1,0:T(8,128)S(1)} %copy-done.1, f32[2,128,128]{2,1,0:T(8,128)S(1)} %copy-done.2, ...), custom_call_target="tpu_custom_call" | custom-call | tf_op jit(solution)/shard_map/field/pallas_call | solution.py:479
  53.3 0.0 copy-start.7
  53.3 15.2 %all_to_all.28.r_ref = f32[64,2,384]{2,1,0:T(2,128)S(1)} all-to-all(f32[64,2,384]{2,1,0:T(2,128)S(1)} %bitcast.13), channel_id=1, replica_groups=mesh['src'=2,'pen'=64] {'pen'}, dimensions={0} | all-to-all | bytes 393216 | tf_op jit(solution)/shard_map/all_to_all | solution.py:546
  68.5 1.0 %pull.1 = f32[256,128]{1,0:T(8,128)S(1)} custom-call(f32[64,2,384]{2,1,0:T(2,128)S(1)} %all_to_all.28.r_ref, f32[64,8,128]{2,1,0:T(8,128)S(1)} %all_to_all.26.r_ref.t_ref, bf16[8,768,128]{2,1,0:T(8,128)(2,1)S(1)} %copy-done, bf16[768,256]{1,0:T(8,128)(2,1)S(1)} %copy-done.5), custom_call_target="tpu_custom_call" | custom-call | tf_op jit(solution)/shard_map/pull/pallas_call | solution.py:548
  69.6 0.8 collective-permute-start
  70.4 14.0 %all_to_all.29 = f32[128,2,128]{2,1,0:T(2,128)S(1)} all-to-all(f32[128,2,128]{2,1,0:T(2,128)S(1)} %bitcast.11), channel_id=1, replica_groups=mesh['src'=2,'pen'=64] {'src','pen'}, dimensions={0} | all-to-all | bytes 262144 | tf_op jit(solution)/shard_map/all_to_all | solution.py:557
  84.4 0.0 collective-permute-done.theirs_ref
  84.4 0.0 copy-done.7
  84.4 1.1 %final.1 = f32[2,128,128]{2,1,0:T(8,128)} custom-call(f32[256,128]{1,0:T(8,128)S(1)} %bitcast.12, bf16[512,256]{1,0:T(8,128)(2,1)S(1)} %copy-done.7, f32[2,128,128]{2,1,0:T(8,128)S(1)} %get-tuple-element.16.mine_ref, f32[2,128,128]{2,1,0:T(8,128)S(1)} %collective-permute-done.theirs_ref), custom_call_target="tpu_custom_call" | custom-call | tf_op jit(solution)/shard_map/final/pallas_call | solution.py:560
  (11 shorter events, 0.0 us)
Async XLA Ops:
  0.0 27.2 %copy-start = (bf16[8,768,128]{2,1,0:T(8,128)(2,1)S(1)}, bf16[8,768,128]{2,1,0:T(8,128)(2,1)}, u32[]{:S(2)}) copy-start(bf16[8,768,128]{2,1,0:T(8,128)(2,1)} %constant.13.clone.across) | copy-start | bytes 4718596
  0.0 27.2 %copy-start.6 = (bf16[256,768]{1,0:T(8,128)(2,1)S(1)}, bf16[256,768]{1,0:T(8,128)(2,1)}, u32[]{:S(2)}) copy-start(bf16[256,768]{1,0:T(8,128)(2,1)} %constant.16.clone.eb) | copy-start | bytes 1179652
  0.0 27.2 %copy-start.10 = (f32[32]{0:T(128)S(1)}, f32[32]{0:T(128)}, u32[]{:S(2)}) copy-start(f32[32]{0:T(128)} %well_hbm.3) | copy-start | bytes 388
  0.0 27.3 %copy-start.9 = (f32[32]{0:T(128)S(1)}, f32[32]{0:T(128)}, u32[]{:S(2)}) copy-start(f32[32]{0:T(128)} %rock_hbm.3) | copy-start | bytes 388
  0.0 27.3 %copy-start.11 = (f32[32]{0:T(128)S(1)}, f32[32]{0:T(128)}, u32[]{:S(2)}) copy-start(f32[32]{0:T(128)} %param.21) | copy-start | bytes 388
  0.0 27.3 %copy-start.8 = (f32[32,32]{1,0:T(8,128)S(1)}, f32[32,32]{1,0:T(8,128)}, u32[]{:S(2)}) copy-start(f32[32,32]{1,0:T(8,128)} %mix_ref.1) | copy-start | bytes 12292
  27.2 18.4 %copy-start.1 = (f32[2,128,128]{2,1,0:T(8,128)S(1)}, f32[2,128,128]{2,1,0:T(8,128)}, u32[]{:S(2)}) copy-start(f32[2,128,128]{2,1,0:T(8,128)} %p_ref.1) | copy-start | bytes 393220
  27.2 18.4 %copy-start.2 = (f32[2,128,128]{2,1,0:T(8,128)S(1)}, f32[2,128,128]{2,1,0:T(8,128)}, u32[]{:S(2)}) copy-start(f32[2,128,128]{2,1,0:T(8,128)} %d_ref.1) | copy-start | bytes 393220
  27.2 18.4 %copy-start.3 = (f32[1,2,128,128]{3,2,1,0:T(8,128)S(1)}, f32[1,2,128,128]{3,2,1,0:T(8,128)}, u32[]{:S(2)}) copy-start(f32[1,2,128,128]{3,2,1,0:T(8,128)} %param.16) | copy-start | bytes 393220
  27.2 18.4 %copy-start.4 = (bf16[864,256]{1,0:T(8,128)(2,1)S(1)}, bf16[864,256]{1,0:T(8,128)(2,1)}, u32[]{:S(2)}) copy-start(bf16[864,256]{1,0:T(8,128)(2,1)} %constant.14.clone.tab) | copy-start | bytes 1327108
  29.2 39.3 %copy-start.5 = (bf16[768,256]{1,0:T(8,128)(2,1)S(1)}, bf16[768,256]{1,0:T(8,128)(2,1)}, u32[]{:S(2)}) copy-start(bf16[768,256]{1,0:T(8,128)(2,1)} %constant.17.clone.ed) | copy-start | bytes 1179652
  53.3 31.1 %copy-start.7 = (bf16[512,256]{1,0:T(8,128)(2,1)S(1)}, bf16[512,256]{1,0:T(8,128)(2,1)}, u32[]{:S(2)}) copy-start(bf16[512,256]{1,0:T(8,128)(2,1)} %constant.15.clone.tab) | copy-start | bytes 786436
  69.6 14.8 %collective-permute-start = (f32[2,128,128]{2,1,0:T(8,128)S(1)}, f32[2,128,128]{2,1,0:T(8,128)S(1)}, u32[]{:S(2)}, u32[]{:S(2)}) collective-permute-start(f32[2,128,128]{2,1,0:T(8,128)S(1)} %get-tuple-element.16.mine_ref), channel_id=1, source_target_pairs={{0,64},{64,0},{1,65},{65,1},{2,66},{66,2},{3,67},{67,3},{4,68},{68... | collective-permute-start | bytes 393224 | tf_op jit(solution)/shard_map/ppermute | solution.py:558
